TPU v7x, 32 devices: a whole 2x2x4 slice. The times are simulated.
32 devices in a mesh: groups: 2 (over x), dp: 8 (over z, y), tensor: 2 (over core).
Axes of the slice: x: 2, y: 2, z: 4, core: 2. Of those that a mesh axis runs over, the one named last changes fastest.
Arguments:
- queries: bfloat16 [128, 8, 8192], P(('groups', 'dp'), None, 'tensor'), parts along dimension 0, may hold values from -200 to 200
- cache_keys: bfloat16 [128, 96, 1024], P(('groups', 'dp'), None, 'tensor'), parts along dimension 0, may hold values from -6 to 6
- cache_values: bfloat16 [128, 96, 1024], P(('groups', 'dp'), None, 'tensor'), parts along dimension 0, may hold values from -6 to 6
- new_keys: bfloat16 [128, 8, 1024], P(('groups', 'dp'), None, 'tensor'), parts along dimension 0, may hold values from -6 to 6
- new_values: bfloat16 [128, 8, 1024], P(('groups', 'dp'), None, 'tensor'), parts along dimension 0, may hold values from -6 to 6
- features: bfloat16 [128, 104, 5120], P(('groups', 'dp')), parts along dimension 0, may hold values from -6 to 6
- cotangent: bfloat16 [128, 8, 8192], P(('groups', 'dp'), None, 'tensor'), parts along dimension 0, may hold values from -6 to 6
- rewards: float32 [128], P(('groups', 'dp')), parts along dimension 0, may hold values from 0 to 4
- lengths: int32 [128], P(('groups', 'dp')), parts along dimension 0, may hold values from 1 to 96, 3072 in all
Outputs:
- attended: bfloat16 [128, 8, 8192], P(('groups', 'dp'), None, 'tensor'), parts along dimension 0
- value_grad: float32 [10240, 1024], P(('groups', 'dp'), 'tensor'), parts along dimension 0
- bucket_peaks: float32 [16], P(('groups', 'tensor')), parts along dimension 0
There are 2 independent parts, one for each index of `groups`. A program takes and returns all parts, laid end to end along the dimension named above; each array names one. Nothing has to cross between parts.
Inputs may be any that keep to these rules, and one draw needn't show every extreme that they name: lengths of one part sum to half of 64 times 96, and some rollout has length 96.
All inputs are finite; a program needn't handle non-finite values. No bound on the sum of `lengths` on one device may be relied on, other than what follows from the above.
Results may differ from a plain program's by a relative error of at most 0.0057.
Values sent between devices are 32-bit elements; how exact they have to be, the bound alone decides.
No kernel may reach another device: no remote copies, remote signals or barrier semaphores. Data moves between devices by JAX's collectives and lax.ppermute only.
A program may use at most 64 MiB of HBM per device.

v0:
```python
import math

import jax
import jax.numpy as jnp
from jax import lax
from jax.sharding import PartitionSpec as P

HD = 128
GROUP = 8
BUCKET = 128


def attend_rollout(
    queries_one,
    past_keys,
    past_values,
    fresh_keys,
    fresh_values,
    cot_one,
    live_count,
    advantage_one,
):
    step_count = queries_one.shape[0]
    group_count = past_keys.shape[-1] // HD
    head_count = queries_one.shape[-1] // HD
    grouped = queries_one.reshape(step_count, group_count, head_count // group_count, HD)
    keys_past = past_keys.reshape(-1, group_count, HD)
    values_past = past_values.reshape(-1, group_count, HD)
    keys_new = fresh_keys.reshape(step_count, group_count, HD)
    values_new = fresh_values.reshape(step_count, group_count, HD)
    scaling = 1.0 / math.sqrt(HD)
    scores_past = (
        jnp.einsum("sgjd,cgd->sgjc", grouped, keys_past, preferred_element_type=jnp.float32)
        * scaling
    )
    scores_new = (
        jnp.einsum("sgjd,tgd->sgjt", grouped, keys_new, preferred_element_type=jnp.float32)
        * scaling
    )
    filled = jnp.arange(keys_past.shape[0])[None, None, None, :] < live_count
    scores_past = jnp.where(filled, scores_past, -1e30)
    causal = (
        jnp.arange(step_count)[:, None, None, None] >= jnp.arange(step_count)[None, None, None, :]
    )
    scores_new = jnp.where(causal, scores_new, -1e30)
    highest = jnp.maximum(jnp.max(scores_past, axis=-1), jnp.max(scores_new, axis=-1))[..., None]
    lift_past = jnp.exp(scores_past - highest)
    lift_new = jnp.exp(scores_new - highest)
    totals = jnp.sum(lift_past, axis=-1, keepdims=True) + jnp.sum(lift_new, axis=-1, keepdims=True)
    weight_past = (lift_past / totals).astype(jnp.bfloat16)
    weight_new = (lift_new / totals).astype(jnp.bfloat16)
    result = jnp.einsum(
        "sgjc,cgd->sgjd", weight_past, values_past, preferred_element_type=jnp.float32
    )
    result = result + jnp.einsum(
        "sgjt,tgd->sgjd", weight_new, values_new, preferred_element_type=jnp.float32
    )
    scaled = (cot_one.astype(jnp.float32) * advantage_one).astype(jnp.bfloat16)
    scaled = scaled.reshape(step_count, group_count, head_count // group_count, HD)
    cot_past = jnp.einsum(
        "sgjc,sgjd->cgd", weight_past, scaled, preferred_element_type=jnp.float32
    ).reshape(-1, group_count * HD)
    cot_new = jnp.einsum(
        "sgjt,sgjd->tgd", weight_new, scaled, preferred_element_type=jnp.float32
    ).reshape(step_count, group_count * HD)
    value_cot = jnp.concatenate([cot_past, cot_new], axis=0).astype(jnp.bfloat16)
    return (result.reshape(step_count, head_count * HD).astype(jnp.bfloat16), value_cot)


def per_device(
    queries, cache_keys, cache_values, new_keys, new_values, features, cotangent, rewards, lengths
):
    grouped_rewards = rewards.reshape(-1, GROUP)
    centre = jnp.mean(grouped_rewards, axis=1, keepdims=True)
    spread = jnp.sqrt(jnp.mean((grouped_rewards - centre) ** 2, axis=1, keepdims=True))
    advantage = ((grouped_rewards - centre) / jnp.maximum(spread, 1.0)).reshape(-1)
    attended, value_cot = jax.vmap(attend_rollout)(
        queries, cache_keys, cache_values, new_keys, new_values, cotangent, lengths, advantage
    )
    model_width = features.shape[2]
    column_count = value_cot.shape[-1]
    flat_features = features.reshape(-1, model_width)
    flat_cot = value_cot.reshape(-1, column_count)
    partial_value = lax.dot_general(
        flat_features, flat_cot, (((0,), (0,)), ((), ())), preferred_element_type=jnp.float32
    )
    bucket_count = column_count // BUCKET
    shards = []
    for bucket in range(bucket_count):
        shards.append(
            lax.psum_scatter(
                partial_value[:, bucket * BUCKET : (bucket + 1) * BUCKET],
                "dp",
                scatter_dimension=0,
                tiled=True,
            )
        )
    value_grad = jnp.concatenate(shards, axis=1)
    local_peaks = jnp.max(jnp.abs(value_grad).reshape(-1, bucket_count, BUCKET), axis=(0, 2))
    peak_list = []
    for bucket in range(bucket_count):
        peak_list.append(lax.pmax(local_peaks[bucket : bucket + 1], "dp"))
    bucket_peaks = jnp.concatenate(peak_list)
    return (attended, value_grad, bucket_peaks)


def solution(mesh):
    in_specs = (
        P(("groups", "dp"), None, "tensor"),
        P(("groups", "dp"), None, "tensor"),
        P(("groups", "dp"), None, "tensor"),
        P(("groups", "dp"), None, "tensor"),
        P(("groups", "dp"), None, "tensor"),
        P(("groups", "dp"), None, None),
        P(("groups", "dp"), None, "tensor"),
        P(("groups", "dp")),
        P(("groups", "dp")),
    )
    out_specs = (
        P(("groups", "dp"), None, "tensor"),
        P(("groups", "dp"), "tensor"),
        P(("groups", "tensor")),
    )
    return jax.shard_map(
        per_device, mesh=mesh, in_specs=in_specs, out_specs=out_specs, check_vma=False
    )
```

profile of v0, /device:TPU:0, one launch (start us, length us, event | category | flops | bytes accessed | tf_op | source)
XLA Modules:
  0.0 357.4 jit_solution(14770040190178998563)
XLA Ops:
  7.2 0.8 iota_compare_fusion.1
  8.0 1.8 reshape.108
  9.8 0.7 fusion.26
  10.5 2.4 fusion.27
  13.0 0.4 fusion.11
  13.4 0.6 fusion.10
  14.1 0.4 divide_convert_fusion
  14.5 0.7 divide_convert_fusion.1
  15.2 0.6 reduce_sum.38
  16.5 0.6 multiply_reduce_fusion
  17.8 0.5 copy.28
  18.4 0.3 fusion.9
  18.7 0.4 fusion.5
  19.3 8.1 %convolution_bitcast_fusion = f32[5120,512]{0,1:T(8,128)S(1)} fusion(bf16[8,104,5120]{2,1,0:T(8,128)(2,1)} %param.14, bf16[8,8,512]{2,1,0:T(8,128)(2,1)S(1)} %fusion.9, bf16[8,96,512]{2,1,0:T(8,128)(2,1)S(1)} %bitcast.76), kind=kOutput, calls=%fused_computation | convolution fusion | flops 4363780096 | bytes 19857408 | tf_op jit(solution)/shard_map/dot_general | solution.py:84
  27.4 4.1 %fusion.24 = (f32[5120,128]{0,1:T(8,128)}, f32[5120,128]{0,1:T(8,128)}, f32[5120,128]{0,1:T(8,128)}, f32[5120,128]{0,1:T(8,128)}) fusion(f32[5120,512]{0,1:T(8,128)S(1)} %convolution_bitcast_fusion), kind=kLoop, calls=%fused_computation.43 | loop fusion | bytes 20971520 | tf_op jit(solution)/shard_map/slice | solution.py:92
  31.6 0.7 reduce-scatter.11.cloned.1.call-update
  32.3 0.7 reduce-scatter.9.cloned.1.call-update
  33.1 0.5 reduce-scatter.7.cloned.1.call-update
  33.6 0.5 copy-done.1
  34.4 0.3 fusion.15
  35.0 0.4 fusion.7
  35.5 1.0 convert_element_type.26
  36.5 68.3 %reduce-scatter.5.cloned.1.call-done = f32[640,128]{0,1:T(8,128)} async-done(((f32[5120,128]{0,1:T(8,128)}), f32[640,128]{0,1:T(8,128)}) %reduce-scatter.5.cloned.1.call-update) | async-done | bytes 327696 | tf_op jit(solution)/shard_map/reduce_scatter | solution.py:91
  104.8 72.9 %reduce-scatter.11.cloned.1.call-done = f32[640,128]{0,1:T(8,128)} async-done(((f32[5120,128]{0,1:T(8,128)}), f32[640,128]{0,1:T(8,128)}) %reduce-scatter.11.cloned.1.call-update) | async-done | bytes 327696 | tf_op jit(solution)/shard_map/reduce_scatter | solution.py:91
  177.7 72.7 %reduce-scatter.9.cloned.1.call-done = f32[640,128]{0,1:T(8,128)} async-done(((f32[5120,128]{0,1:T(8,128)}), f32[640,128]{0,1:T(8,128)}) %reduce-scatter.9.cloned.1.call-update) | async-done | bytes 327696 | tf_op jit(solution)/shard_map/reduce_scatter | solution.py:91
  250.3 72.6 %reduce-scatter.7.cloned.1.call-done = f32[640,128]{0,1:T(8,128)} async-done(((f32[5120,128]{0,1:T(8,128)}), f32[640,128]{0,1:T(8,128)}) %reduce-scatter.7.cloned.1.call-update) | async-done | bytes 327696 | tf_op jit(solution)/shard_map/reduce_scatter | solution.py:91
  322.9 1.4 fusion.4
  324.3 0.7 fusion.25
  325.0 1.4 pad_maximum_fusion
  326.4 1.5 copy.29
  327.8 20.0 %all-reduce = (f32[1]{0:T(128)}, f32[1]{0:T(128)}, f32[1]{0:T(128)}, f32[1]{0:T(128)}) all-reduce(f32[1]{0:T(128)} %get-tuple-element.18, f32[1]{0:T(128)} %get-tuple-element.19, f32[1]{0:T(128)} %get-tuple-element.20, f32[1]{0:T(128)} %get-tuple-element.17), channel_id=1, replica_groups=mesh['groups'=2,'dp'=8,'tensor'=2] {'dp'}, use_global_device_ids=true, to_apply=%region_14.15 | all-reduce | flops 4 | bytes 32 | tf_op jit(solution)/shard_map/pmax | solution.py:102
  347.8 3.0 pad_maximum_fusion.1
  (24 shorter events, 1.1 us)
Async XLA Ops:
  7.2 2.6 copy-start
  7.2 97.6 %reduce-scatter.5.cloned.1.call-start = ((), (), s32[]{:S(2)}) async-start(), calls=%async_computation.4 | async-start | bytes 2949120 | tf_op jit(solution)/shard_map/reduce_scatter | solution.py:91
  8.0 2.5 copy-start.3
  14.1 1.1 copy-start.5
  14.4 3.8 %copy-start.2 = (bf16[8,8,4096]{2,1,0:T(8,128)(2,1)S(1)}, bf16[8,8,4096]{2,1,0:T(8,128)(2,1)}, u32[]{:S(2)}) copy-start(bf16[8,8,4096]{2,1,0:T(8,128)(2,1)} %param.15) | copy-start | bytes 1572868
  31.5 146.1 %reduce-scatter.11.cloned.1.call-start = ((), (), s32[]{:S(2)}) async-start(), calls=%async_computation.7 | async-start | bytes 2949120 | tf_op jit(solution)/shard_map/reduce_scatter | solution.py:91
  32.3 218.0 %reduce-scatter.9.cloned.1.call-start = ((), (), s32[]{:S(2)}) async-start(), calls=%async_computation.6 | async-start | bytes 2949120 | tf_op jit(solution)/shard_map/reduce_scatter | solution.py:91
  33.0 1.1 copy-start.1
  33.0 289.9 %reduce-scatter.7.cloned.1.call-start = ((), (), s32[]{:S(2)}) async-start(), calls=%async_computation.5 | async-start | bytes 2949120 | tf_op jit(solution)/shard_map/reduce_scatter | solution.py:91
  34.2 0.8 copy-start.4
Sparse Core Ops, SparseCore 0:
  31.7 73.0 reduce-scatter.4
  108.3 69.3 reduce-scatter.10
  181.2 69.1 reduce-scatter.8
  253.7 69.1 reduce-scatter.6
where the time goes:
time: 358 us; the launch traced here: 357 us
  waiting for transfers between devices  288 us (80%)
  blocking collectives  20 us (6%)
  between operations  15.3 us (4%)
  matrix products  12.6 us (4%)
  local copies, waits for them, and re-layouts  10.8 us (3%)
  other arithmetic  10.1 us (3%)
    reduce_scatter x4, waiting for transfers between devices, per_device(): lax.psum_scatter(partial_value[:, bucket * BUCKET:(bucket + 1) * BUCKET],...  286 us
    pmax x1, blocking collectives, per_device(): peak_list.append(lax.pmax(local_peaks[bucket:bucket + 1], 'dp'))  20 us
    dot_general x1, matrix products, per_device(): lax.dot_general(flat_features, flat_cot, (((0,), (0,)), ((), ())), prefer...  8.11 us
  transfers between devices with their start and end apart: 4, of which 4 were waited for; matrix products, arithmetic and copies ran while one was open for 1% of the time, Pallas kernels for 0%

commit v1 on v0

v1 whole, which is shorter than its diff:
```python
import functools
import math

import jax
import jax.numpy as jnp
from jax import lax
from jax.experimental import pallas as pl
from jax.experimental.pallas import tpu as pltpu
from jax.sharding import PartitionSpec as P

HD = 128
GROUP = 8
BUCKET = 128
VMEM_BYTES = 40 * 1024 * 1024


def attend_kernel(lengths, rewards, q, ck, cv, nk, nv, cot, *rest):
    out, cot_t, rows = rest[-3:]
    rollouts, steps, width = q.shape
    heads = width // HD
    ctx = ck.shape[1]
    slots = ctx + steps
    padded = -(-slots // HD) * HD
    pad = padded - slots
    scaling = 1.0 / math.sqrt(HD)

    def by_head(block):
        return jnp.concatenate(
            [block[:, j * HD : (j + 1) * HD].astype(jnp.float32) for j in range(heads)], axis=0
        )

    def joined(past, fresh):
        fresh = jnp.concatenate(
            [fresh.astype(jnp.float32), jnp.zeros((pad, HD), jnp.float32)], axis=0
        ).astype(jnp.bfloat16)
        return jnp.concatenate([past, fresh], axis=0)

    shape = (heads * steps, padded)
    column = lax.broadcasted_iota(jnp.int32, shape, 1)
    step = lax.broadcasted_iota(jnp.int32, shape, 0) % steps
    fresh_live = (column >= ctx) & (column - ctx <= step)
    for base in range(0, rollouts, GROUP):
        centre = rewards[base]
        for i in range(1, GROUP):
            centre = centre + rewards[base + i]
        centre = centre * (1.0 / GROUP)
        spread = (rewards[base] - centre) * (rewards[base] - centre)
        for i in range(1, GROUP):
            spread = spread + (rewards[base + i] - centre) * (rewards[base + i] - centre)
        spread = jnp.sqrt(jnp.full((1, HD), spread * (1.0 / GROUP), jnp.float32))
        spread = jnp.maximum(spread, 1.0)
        for r in range(base, base + GROUP):
            advantage = jnp.full((1, HD), rewards[r] - centre, jnp.float32) / spread
            keys = joined(ck[r], nk[r])
            values = joined(cv[r], nv[r])
            scores = lax.dot_general(
                by_head(q[r]).astype(jnp.bfloat16),
                keys,
                (((1,), (1,)), ((), ())),
                preferred_element_type=jnp.float32,
            )
            scores = scores * scaling
            scores = jnp.where((column < lengths[r]) | fresh_live, scores, -1e30)
            highest = jnp.max(scores, axis=1, keepdims=True)
            lift = jnp.exp(scores - highest)
            weights = (lift / jnp.sum(lift, axis=1, keepdims=True)).astype(jnp.bfloat16)
            result = jnp.dot(weights, values, preferred_element_type=jnp.float32)
            for j in range(heads):
                out[r, :, j * HD : (j + 1) * HD] = result[j * steps : (j + 1) * steps].astype(
                    jnp.bfloat16
                )
            scaled = (by_head(cot[r]) * advantage).astype(jnp.bfloat16)
            value_cot = lax.dot_general(
                weights, scaled, (((0,), (0,)), ((), ())), preferred_element_type=jnp.float32
            )
            rows[r * slots : (r + 1) * slots, :] = value_cot[:slots]
    cot_t[...] = rows[...].T.astype(jnp.bfloat16)


def attend(g, lengths, rewards, queries, ck, cv, nk, nv, cotangent, attended):
    rollouts, steps, width = queries.shape
    ctx = ck.shape[1]
    key_heads = ck.shape[2] // HD
    wide = width // key_heads
    slots = rollouts * (ctx + steps)

    def block(dims):
        return pl.BlockSpec(dims, lambda i: (0, 0, g))

    smem = pl.BlockSpec(memory_space=pltpu.SMEM)
    in_specs = [
        smem,
        smem,
        block((rollouts, steps, wide)),
        block((rollouts, ctx, HD)),
        block((rollouts, ctx, HD)),
        block((rollouts, steps, HD)),
        block((rollouts, steps, HD)),
        block((rollouts, steps, wide)),
    ]
    args = [lengths, rewards, queries, ck, cv, nk, nv, cotangent]
    aliases = {}
    if attended is not None:
        in_specs.append(pl.BlockSpec(memory_space=pl.ANY))
        args.append(attended)
        aliases = {8: 0}
    return pl.pallas_call(
        attend_kernel,
        grid=(1,),
        in_specs=in_specs,
        out_specs=[
            block((rollouts, steps, wide)),
            pl.BlockSpec((HD, slots), lambda i: (0, 0)),
        ],
        out_shape=[
            jax.ShapeDtypeStruct(queries.shape, jnp.bfloat16),
            jax.ShapeDtypeStruct((HD, slots), jnp.bfloat16),
        ],
        scratch_shapes=[pltpu.VMEM((slots, HD), jnp.float32)],
        input_output_aliases=aliases,
        compiler_params=pltpu.CompilerParams(vmem_limit_bytes=VMEM_BYTES),
        cost_estimate=pl.CostEstimate(
            flops=6 * rollouts * steps * wide * HD,
            bytes_accessed=rollouts * (3 * steps * wide + 2 * ctx * HD) * 2,
            transcendentals=rollouts * steps * wide,
        ),
        name="attend",
    )(*args)


def chunk_kernel(where, features, *refs):
    count = len(refs) // 2
    left = jnp.concatenate([ref[...] for ref in refs[:count]], axis=0)
    result = jnp.dot(left, features[...], preferred_element_type=jnp.float32)
    for i in range(count):
        refs[count + i][...] = result[i * BUCKET : (i + 1) * BUCKET]


def chunks(where, slot, features, cots, width):
    depth = features.shape[0]
    count = len(cots)
    return pl.pallas_call(
        chunk_kernel,
        grid_spec=pltpu.PrefetchScalarGridSpec(
            num_scalar_prefetch=1,
            grid=(1,),
            in_specs=[pl.BlockSpec((depth, width), lambda i, where: (0, where[slot]))]
            + [pl.BlockSpec((BUCKET, depth), lambda i, where: (0, 0))] * count,
            out_specs=[pl.BlockSpec((BUCKET, width), lambda i, where: (0, 0))] * count,
        ),
        out_shape=[jax.ShapeDtypeStruct((BUCKET, width), jnp.float32)] * count,
        compiler_params=pltpu.CompilerParams(vmem_limit_bytes=VMEM_BYTES),
        cost_estimate=pl.CostEstimate(
            flops=2 * depth * width * BUCKET * count,
            bytes_accessed=2 * depth * (width + BUCKET * count) + 4 * BUCKET * width * count,
            transcendentals=0,
        ),
        name="chunk",
    )(where, features, *cots)


def finish_kernel(bucket, count, *refs):
    total = refs[0][...]
    for ref in refs[1:count]:
        total = total + ref[...]
    grad, peaks = refs[-2:]
    grad[...] = total.T
    peak = jnp.max(jnp.max(jnp.abs(total), axis=0, keepdims=True), axis=1, keepdims=True)
    peak = jnp.broadcast_to(peak, peaks.shape)
    if len(refs) > count + 2:
        lane = lax.broadcasted_iota(jnp.int32, peaks.shape, 1)
        peak = jnp.where(lane == bucket, peak, refs[count + 1][...])
    peaks[...] = peak


def finish(bucket, parts, grad, peaks, columns):
    width = parts[0].shape[1]
    count = len(parts)
    whole = pl.BlockSpec((BUCKET, width), lambda i: (0, 0))
    tile = pl.BlockSpec((8, 128), lambda i: (0, 0))
    in_specs = [whole] * count
    args = list(parts)
    aliases = {}
    if grad is not None:
        in_specs += [pl.BlockSpec(memory_space=pl.ANY), tile]
        args += [grad, peaks]
        aliases = {count: 0}
    return pl.pallas_call(
        functools.partial(finish_kernel, bucket, count),
        grid=(1,),
        in_specs=in_specs,
        out_specs=[pl.BlockSpec((width, BUCKET), lambda i: (0, bucket)), tile],
        out_shape=[
            jax.ShapeDtypeStruct((width, columns), jnp.float32),
            jax.ShapeDtypeStruct((8, 128), jnp.float32),
        ],
        input_output_aliases=aliases,
        compiler_params=pltpu.CompilerParams(vmem_limit_bytes=VMEM_BYTES),
        name="finish",
    )(*args)


def reduce_on_grid(features, cots, dp):
    width = features.shape[1] // dp
    rank = lax.axis_index("dp")
    edge = (rank < 2) | (rank >= 6)

    table = []
    for r in range(dp):
        z, y = r // 2, r % 2
        planes = [3, 2] if z < 2 else [0, 1]
        planes += [z ^ 1, z]
        table.append([p * 2 + 1 - y for p in planes] + [p * 2 + y for p in planes])
    where = jnp.asarray(table, jnp.int32)[rank]

    def across(x):
        return lax.ppermute(x, "dp", [(r, r ^ 1) for r in range(dp)])

    def pair(x):
        return lax.ppermute(x, "dp", [(r, r ^ 2) for r in range(dp)])

    def outward(x):
        return lax.ppermute(x, "dp", [(r, r ^ 2) for r in (0, 1, 6, 7)])

    def middle(x):
        return lax.ppermute(x, "dp", [(r, r ^ 6) for r in (2, 3, 4, 5)])

    count = len(cots)
    first = {}
    for s in range(0, count, 2):
        first[s] = chunks(where, 0, features, [cots[s]], width)[0]
        first[s + 1] = chunks(where, 2, features, [cots[s + 1]], width)[0]
    own3 = chunks(where, 4, features, cots, width)
    cross3 = chunks(where, 0, features, cots[1::2], width)
    cross2 = chunks(where, 1, features, cots, width)
    own2 = chunks(where, 5, features, cots, width)
    crossp = chunks(where, 2, features, cots[0::2], width)
    ownp = chunks(where, 6, features, cots, width)
    crosso = chunks(where, 3, features, cots, width)
    owno = chunks(where, 7, features, cots, width)

    streams = []
    for s in range(0, count, 2):
        streams.append({"a": s, "b": s + 1, "half": s // 2})
    y, e, m = {}, {}, {}
    for t in range(7):
        for s in streams:
            a, b, h = s["a"], s["b"], s["half"]
            k = (h, t)
            send = [first[a], cross3[h], cross2[a], cross2[b], crossp[h], crosso[a], None][t]
            if t == 6:
                send = crosso[b] + e[h, 0]
            y[k] = across(send)
            if t == 0:
                e[k] = pair(first[b])
            elif t == 1:
                e[k] = outward(own3[a] + y[h, 0])
            elif t == 2:
                e[k] = outward(own3[b] + y[h, 1])
            elif t == 3:
                e[k] = outward(own2[a] + y[h, 2])
            elif t == 4:
                e[k] = pair(jnp.where(edge, own2[b] + y[h, 3], ownp[b] + m[h, 3]))
            elif t == 5:
                e[k] = pair(ownp[a] + y[h, 4] + m[h, 2])
            else:
                e[k] = outward(ownp[b])
            if t == 2:
                m[k] = middle(own3[a] + y[h, 0] + e[h, 1])
            elif t == 3:
                m[k] = middle(own3[b] + y[h, 1] + e[h, 2])
            elif t == 4:
                m[k] = middle(own2[a] + y[h, 2] + e[h, 3])
            elif t == 5:
                m[k] = middle(own2[b] + y[h, 3] + e[h, 4])
    grad = peaks = None
    for s in streams:
        a, h = s["a"], s["half"]
        grad, peaks = finish(
            a, [owno[a], y[h, 5], e[h, 5], m[h, 4]], grad, peaks, count * BUCKET
        )
    for s in streams:
        b, h = s["b"], s["half"]
        early = jnp.where(edge, e[h, 4], 0.0)
        grad, peaks = finish(
            b, [owno[b] + early, y[h, 6], e[h, 6], m[h, 5]], grad, peaks, count * BUCKET
        )
    for hop in (1, 2, 4):
        peaks = jnp.maximum(
            peaks, lax.ppermute(peaks, "dp", [(r, r ^ hop) for r in range(dp)])
        )
    return grad, peaks[0, :count]


def reduce_plain(features, cots):
    partial_grad = lax.dot_general(
        features,
        jnp.concatenate(cots, axis=0),
        (((0,), (1,)), ((), ())),
        preferred_element_type=jnp.float32,
    )
    grad = lax.psum_scatter(partial_grad, "dp", scatter_dimension=0, tiled=True)
    peaks = jnp.max(jnp.abs(grad).reshape(-1, len(cots), BUCKET), axis=(0, 2))
    return grad, lax.pmax(peaks, "dp")


def per_device(
    dp,
    queries,
    cache_keys,
    cache_values,
    new_keys,
    new_values,
    features,
    cotangent,
    rewards,
    lengths,
):
    key_heads = cache_keys.shape[2] // HD
    attended, cots = None, []
    for g in range(key_heads):
        attended, cot = attend(
            g,
            lengths,
            rewards,
            queries,
            cache_keys,
            cache_values,
            new_keys,
            new_values,
            cotangent,
            attended,
        )
        cots.append(cot)
    flat = features.reshape(-1, features.shape[2])
    if dp == 8 and key_heads % 2 == 0 and features.shape[2] % (8 * BUCKET) == 0:
        grad, peaks = reduce_on_grid(flat, cots, dp)
    else:
        grad, peaks = reduce_plain(flat, cots)
    return attended, grad, peaks


def solution(mesh):
    split = P(("groups", "dp"), None, "tensor")
    rows = P(("groups", "dp"))
    in_specs = (
        split,
        split,
        split,
        split,
        split,
        P(("groups", "dp"), None, None),
        split,
        rows,
        rows,
    )
    out_specs = (split, P(("groups", "dp"), "tensor"), P(("groups", "tensor")))
    return jax.shard_map(
        functools.partial(per_device, mesh.shape["dp"]),
        mesh=mesh,
        in_specs=in_specs,
        out_specs=out_specs,
        check_vma=False,
    )
```

time: 358 us -> 184 us (0.51)
  waiting for transfers between devices: 288 us -> 55.6 us
  starting transfers between devices: 0.16 us -> 64.1 us
  Pallas kernels: 0 us -> 36.6 us
  blocking collectives: 20 us -> 0 us
  between operations: 15.3 us -> 1.25 us
  matrix products: 12.6 us -> 0 us
  local copies, waits for them, and re-layouts: 10.8 us -> 19.5 us
  other arithmetic: 10.1 us -> 6.33 us
    reduce_scatter x4 -> x0, waiting for transfers between devices: 286 us -> none  [per_device(): lax.psum_scatter(partial_value[:, bucket * BUCKET:(bucket + 1) * BUCKET],...]
    ppermute x0 -> x39, starting transfers between devices: none -> 64.1 us  [the longest x8 23.5 us: outward(): return lax.ppermute(x, 'dp', [(r, r ^ 2) for r in (0, 1, 6, 7)])]
    ppermute x0 -> x39, waiting for transfers between devices: none -> 55.6 us  [the longest x14 26.6 us: across(): return lax.ppermute(x, 'dp', [(r, r ^ 1) for r in range(dp)])]
    pallas_call x0 -> x20, Pallas kernels: none -> 36.6 us  [the longest x4 17.1 us: attend(): pl.pallas_call(attend_kernel, grid=(1,), in_specs=in_specs, out_specs=[bl...]
    pmax x1 -> x0, blocking collectives: 20 us -> none  [per_device(): peak_list.append(lax.pmax(local_peaks[bucket:bucket + 1], 'dp'))]
    unnamed x13 -> x82, local copies, waits for them, and re-layouts: 2.36 us -> 18.3 us
    dot_general x7 -> x0, matrix products: 12.6 us -> none  [the longest x1 8.11 us: per_device(): lax.dot_general(flat_features, flat_cot, (((0,), (0,)), ((), ())), prefer...]
    slice x2 -> x0, local copies, waits for them, and re-layouts: 4.77 us -> none  [the longest x1 4.11 us: per_device(): partial_value[:, bucket * BUCKET:(bucket + 1) * BUCKET]]
  transfers between devices with their start and end apart: 4 -> 39, of which waited for: 4 -> 17; matrix products, arithmetic and copies ran while one was open for 1% -> 3% of each run, Pallas kernels for 0% -> 17%
where the time goes in v1:
time: 184 us; the launch traced here: 183 us
  starting transfers between devices  64.1 us (35%)
  waiting for transfers between devices  55.6 us (30%)
  Pallas kernels  36.6 us (20%)
  local copies, waits for them, and re-layouts  19.5 us (11%)
  other arithmetic  6.33 us (3%)
    ppermute x14, waiting for transfers between devices, across(): return lax.ppermute(x, 'dp', [(r, r ^ 1) for r in range(dp)])  26.6 us
    ppermute x8, starting transfers between devices, outward(): return lax.ppermute(x, 'dp', [(r, r ^ 2) for r in (0, 1, 6, 7)])  23.5 us
    unnamed x82, local copies, waits for them, and re-layouts  18.3 us
    ppermute x8, waiting for transfers between devices, outward(): return lax.ppermute(x, 'dp', [(r, r ^ 2) for r in (0, 1, 6, 7)])  17.4 us
    pallas_call x4, Pallas kernels, attend(): pl.pallas_call(attend_kernel, grid=(1,), in_specs=in_specs, out_specs=[bl...  17.1 us
    pallas_call x12, Pallas kernels, chunks(): pl.pallas_call(chunk_kernel, grid_spec=pltpu.PrefetchScalarGridSpec(num_s...  15.8 us
    ppermute x14, starting transfers between devices, across(): return lax.ppermute(x, 'dp', [(r, r ^ 1) for r in range(dp)])  14 us
    ppermute x6, starting transfers between devices, pair(): return lax.ppermute(x, 'dp', [(r, r ^ 2) for r in range(dp)])  12.1 us
  transfers between devices with their start and end apart: 39, of which 17 were waited for; matrix products, arithmetic and copies ran while one was open for 3% of the time, Pallas kernels for 17%

profile of v1, /device:TPU:0, one launch (start us, length us, event | category | flops | bytes accessed | tf_op | source)
XLA Modules:
  0.0 183.4 jit_solution(6488930649218707698)
XLA Ops:
  8.7 4.3 %attend.4 = (bf16[8,8,4096]{2,1,0:T(8,128)(2,1)}, bf16[128,832]{1,0:T(8,128)(2,1)S(1)}) custom-call(s32[8]{0:T(128)S(1)} %copy-done.15, f32[8]{0:T(128)S(1)} %copy-done.16, bf16[8,8,4096]{2,1,0:T(8,128)(2,1)S(1)} %copy-done.7, bf16[8,96,512]{2,1,0:T(8,128)(2,1)S(1)} %copy-done.3, bf16[8,96,512]{2,1,0:T(8,128)(2,1)S(1)} %copy-done.5, ...), custom_call_target="tpu_custom_call" | custom-call | flops 50331648 | bytes 786432 | tf_op jit(solution)/shard_map/attend/pallas_call | solution.py:107
  13.0 3.4 %copy-done = bf16[8,104,5120]{2,1,0:T(8,128)(2,1)S(1)} copy-done((bf16[8,104,5120]{2,1,0:T(8,128)(2,1)S(1)}, bf16[8,104,5120]{2,1,0:T(8,128)(2,1)}, u32[]{:S(2)}) %copy-start) | copy-done | bytes 8519704
  17.3 3.0 %collective-permute-start.29 = (f32[128,640]{1,0:T(8,128)S(1)}, f32[128,640]{1,0:T(8,128)S(1)}, u32[]{:S(2)}, u32[]{:S(2)}) collective-permute-start(f32[128,640]{1,0:T(8,128)S(1)} %chunk.23), channel_id=1, source_target_pairs={{0,2},{2,0},{4,6},{6,4},{8,10},{10,8},{12,14},{14,12},{1,3},{3,1},... | collective-permute-start | bytes 983048 | tf_op jit(solution)/shard_map/ppermute | solution.py:217
  20.4 4.3 %attend.5 = (bf16[8,8,4096]{2,1,0:T(8,128)(2,1)}, bf16[128,832]{1,0:T(8,128)(2,1)S(1)}) custom-call(s32[8]{0:T(128)S(1)} %copy-done.15, f32[8]{0:T(128)S(1)} %copy-done.16, bf16[8,8,4096]{2,1,0:T(8,128)(2,1)S(1)} %copy-done.8, bf16[8,96,512]{2,1,0:T(8,128)(2,1)S(1)} %copy-done.4, bf16[8,96,512]{2,1,0:T(8,128)(2,1)S(1)} %copy-done.6, ...), custom_call_target="tpu_custom_call", output_to_operand_aliasing={{0}: (8, {})} | custom-call | flops 50331648 | bytes 786432 | tf_op jit(solution)/shard_map/attend/pallas_call | solution.py:107
  27.2 4.3 %attend.6 = (bf16[8,8,4096]{2,1,0:T(8,128)(2,1)}, bf16[128,832]{1,0:T(8,128)(2,1)S(1)}) custom-call(s32[8]{0:T(128)S(1)} %copy-done.15, f32[8]{0:T(128)S(1)} %copy-done.16, bf16[8,8,4096]{2,1,0:T(8,128)(2,1)S(1)} %copy-done.8, bf16[8,96,512]{2,1,0:T(8,128)(2,1)S(1)} %copy-done.4, bf16[8,96,512]{2,1,0:T(8,128)(2,1)S(1)} %copy-done.6, ...), custom_call_target="tpu_custom_call", output_to_operand_aliasing={{0}: (8, {})} | custom-call | flops 50331648 | bytes 786432 | tf_op jit(solution)/shard_map/attend/pallas_call | solution.py:107
  31.4 4.3 %attend.7 = (bf16[8,8,4096]{2,1,0:T(8,128)(2,1)}, bf16[128,832]{1,0:T(8,128)(2,1)S(1)}) custom-call(s32[8]{0:T(128)S(1)} %copy-done.15, f32[8]{0:T(128)S(1)} %copy-done.16, bf16[8,8,4096]{2,1,0:T(8,128)(2,1)S(1)} %copy-done.8, bf16[8,96,512]{2,1,0:T(8,128)(2,1)S(1)} %copy-done.4, bf16[8,96,512]{2,1,0:T(8,128)(2,1)S(1)} %copy-done.6, ...), custom_call_target="tpu_custom_call", output_to_operand_aliasing={{0}: (8, {})} | custom-call | flops 50331648 | bytes 786432 | tf_op jit(solution)/shard_map/attend/pallas_call | solution.py:107
  41.4 2.3 %chunk.14 = (f32[128,640]{1,0:T(8,128)S(1)}, f32[128,640]{1,0:T(8,128)}, f32[128,640]{1,0:T(8,128)S(1)}, f32[128,640]{1,0:T(8,128)}) custom-call(s32[8]{0:T(128)S(1)} %dynamic-slice_bitcast_fusion.where, bf16[832,5120]{1,0:T(8,128)(2,1)S(1)} %bitcast.10, bf16[128,832]{1,0:T(8,128)(2,1)S(1)} %get-tuple-element.51.refs_0_, ...), custom_call_target="tpu_custom_call" | custom-call | flops 545259520 | bytes 3227648 | tf_op jit(solution)/shard_map/chunk/pallas_call | solution.py:142
  43.8 2.0 %collective-permute-start.24 = (f32[128,640]{1,0:T(8,128)S(1)}, f32[128,640]{1,0:T(8,128)S(1)}, u32[]{:S(2)}, u32[]{:S(2)}) collective-permute-start(f32[128,640]{1,0:T(8,128)S(1)} %get-tuple-element.75), channel_id=1, source_target_pairs={{0,2},{2,0},{4,6},{6,4},{8,10},{10,8},{12,14},{14,12},{1,3},{3,1},... | collective-permute-start | bytes 983048 | tf_op jit(solution)/shard_map/ppermute | solution.py:217
  45.7 1.8 %collective-permute-done.10 = f32[128,640]{1,0:T(8,128)S(1)} collective-permute-done((f32[128,640]{1,0:T(8,128)S(1)}, f32[128,640]{1,0:T(8,128)S(1)}, u32[]{:S(2)}, u32[]{:S(2)}) %collective-permute-start.10) | collective-permute-done | bytes 327712 | tf_op jit(solution)/shard_map/ppermute | solution.py:217
  49.6 12.0 %collective-permute-done.1 = f32[128,640]{1,0:T(8,128)S(1)} collective-permute-done((f32[128,640]{1,0:T(8,128)S(1)}, f32[128,640]{1,0:T(8,128)S(1)}, u32[]{:S(2)}, u32[]{:S(2)}) %collective-permute-start.1) | collective-permute-done | bytes 327712 | tf_op jit(solution)/shard_map/ppermute | solution.py:217
  61.6 2.4 %collective-permute-start.11 = (f32[128,640]{1,0:T(8,128)S(1)}, f32[128,640]{1,0:T(8,128)S(1)}, u32[]{:S(2)}, u32[]{:S(2)}) collective-permute-start(f32[128,640]{1,0:T(8,128)S(1)} %add.98), channel_id=1, source_target_pairs={{0,4},{2,6},{12,8},{14,10},{1,5},{3,7},{13,9},{15,11},{16,20},{18,... | collective-permute-start | bytes 983048 | tf_op jit(solution)/shard_map/ppermute | solution.py:223
  68.6 2.4 %collective-permute-start.30 = (f32[128,640]{1,0:T(8,128)S(1)}, f32[128,640]{1,0:T(8,128)S(1)}, u32[]{:S(2)}, u32[]{:S(2)}) collective-permute-start(f32[128,640]{1,0:T(8,128)S(1)} %add.111), channel_id=1, source_target_pairs={{0,4},{2,6},{12,8},{14,10},{1,5},{3,7},{13,9},{15,11},{16,20},{18,... | collective-permute-start | bytes 983048 | tf_op jit(solution)/shard_map/ppermute | solution.py:223
  71.1 2.8 %collective-permute-done.33 = f32[128,640]{1,0:T(8,128)S(1)} collective-permute-done((f32[128,640]{1,0:T(8,128)S(1)}, f32[128,640]{1,0:T(8,128)S(1)}, u32[]{:S(2)}, u32[]{:S(2)}) %collective-permute-start.33) | collective-permute-done | bytes 327712 | tf_op jit(solution)/shard_map/ppermute | solution.py:217
  73.9 2.4 %collective-permute-start.25 = (f32[128,640]{1,0:T(8,128)S(1)}, f32[128,640]{1,0:T(8,128)S(1)}, u32[]{:S(2)}, u32[]{:S(2)}) collective-permute-start(f32[128,640]{1,0:T(8,128)S(1)} %add.108), channel_id=1, source_target_pairs={{0,4},{2,6},{12,8},{14,10},{1,5},{3,7},{13,9},{15,11},{16,20},{18,... | collective-permute-start | bytes 983048 | tf_op jit(solution)/shard_map/ppermute | solution.py:223
  77.0 2.0 %collective-permute-start.34 = (f32[128,640]{1,0:T(8,128)}, f32[128,640]{1,0:T(8,128)}, u32[]{:S(2)}, u32[]{:S(2)}) collective-permute-start(f32[128,640]{1,0:T(8,128)} %add.114), channel_id=1, source_target_pairs={{0,4},{2,6},{12,8},{14,10},{1,5},{3,7},{13,9},{15,11},{16,20},{18,... | collective-permute-start | bytes 983048 | tf_op jit(solution)/shard_map/ppermute | solution.py:223
  80.2 6.0 %collective-permute-done.21 = f32[128,640]{1,0:T(8,128)S(1)} collective-permute-done((f32[128,640]{1,0:T(8,128)S(1)}, f32[128,640]{1,0:T(8,128)S(1)}, u32[]{:S(2)}, u32[]{:S(2)}) %collective-permute-start.21) | collective-permute-done | bytes 327712 | tf_op jit(solution)/shard_map/ppermute | solution.py:223
  93.2 6.0 %collective-permute-done.25 = f32[128,640]{1,0:T(8,128)S(1)} collective-permute-done((f32[128,640]{1,0:T(8,128)S(1)}, f32[128,640]{1,0:T(8,128)S(1)}, u32[]{:S(2)}, u32[]{:S(2)}) %collective-permute-start.25) | collective-permute-done | bytes 327712 | tf_op jit(solution)/shard_map/ppermute | solution.py:223
  103.3 3.4 %copy-done.2 = bf16[8,104,5120]{2,1,0:T(8,128)(2,1)S(1)} copy-done((bf16[8,104,5120]{2,1,0:T(8,128)(2,1)S(1)}, bf16[8,104,5120]{2,1,0:T(8,128)(2,1)}, u32[]{:S(2)}) %copy-start.2) | copy-done | bytes 8519704
  118.1 3.0 %collective-permute-done.19 = f32[128,640]{1,0:T(8,128)S(1)} collective-permute-done((f32[128,640]{1,0:T(8,128)S(1)}, f32[128,640]{1,0:T(8,128)S(1)}, u32[]{:S(2)}, u32[]{:S(2)}) %collective-permute-start.19) | collective-permute-done | bytes 327712 | tf_op jit(solution)/shard_map/ppermute | solution.py:217
  121.7 4.5 %collective-permute-done.28 = f32[128,640]{1,0:T(8,128)S(1)} collective-permute-done((f32[128,640]{1,0:T(8,128)S(1)}, f32[128,640]{1,0:T(8,128)S(1)}, u32[]{:S(2)}, u32[]{:S(2)}) %collective-permute-start.28) | collective-permute-done | bytes 327712 | tf_op jit(solution)/shard_map/ppermute | solution.py:217
  126.2 5.7 %collective-permute-start.4 = (f32[128,640]{1,0:T(8,128)S(1)}, f32[128,640]{1,0:T(8,128)S(1)}, u32[]{:S(2)}, u32[]{:S(2)}) collective-permute-start(f32[128,640]{1,0:T(8,128)S(1)} %get-tuple-element.93), channel_id=1, source_target_pairs={{0,4},{2,6},{4,0},{6,2},{8,12},{10,14},{12,8},{14,10},{1,5},{3,7},... | collective-permute-start | bytes 983048 | tf_op jit(solution)/shard_map/ppermute | solution.py:220
  132.0 5.6 %collective-permute-start.16 = (f32[128,640]{1,0:T(8,128)S(1)}, f32[128,640]{1,0:T(8,128)S(1)}, u32[]{:S(2)}, u32[]{:S(2)}) collective-permute-start(f32[128,640]{1,0:T(8,128)S(1)} %get-tuple-element.65), channel_id=1, source_target_pairs={{0,4},{2,6},{12,8},{14,10},{1,5},{3,7},{13,9},{15,11},{16,20},{18,... | collective-permute-start | bytes 983048 | tf_op jit(solution)/shard_map/ppermute | solution.py:223
  140.4 2.6 %collective-permute-start.23 = (f32[128,640]{1,0:T(8,128)S(1)}, f32[128,640]{1,0:T(8,128)S(1)}, u32[]{:S(2)}, u32[]{:S(2)}) collective-permute-start(f32[128,640]{1,0:T(8,128)S(1)} %add_add_fusion.1), channel_id=1, source_target_pairs={{0,4},{2,6},{4,0},{6,2},{8,12},{10,14},{12,8},{14,10},{1,5},{3,7},... | collective-permute-start | bytes 983048 | tf_op jit(solution)/shard_map/ppermute | solution.py:220
  143.0 4.4 %collective-permute-done.13 = f32[128,640]{1,0:T(8,128)S(1)} collective-permute-done((f32[128,640]{1,0:T(8,128)S(1)}, f32[128,640]{1,0:T(8,128)S(1)}, u32[]{:S(2)}, u32[]{:S(2)}) %collective-permute-start.13) | collective-permute-done | bytes 327712 | tf_op jit(solution)/shard_map/ppermute | solution.py:220
  147.4 2.1 %collective-permute-start.32 = (f32[128,640]{1,0:T(8,128)S(1)}, f32[128,640]{1,0:T(8,128)S(1)}, u32[]{:S(2)}, u32[]{:S(2)}) collective-permute-start(f32[128,640]{1,0:T(8,128)S(1)} %add_add_fusion), channel_id=1, source_target_pairs={{0,4},{2,6},{4,0},{6,2},{8,12},{10,14},{12,8},{14,10},{1,5},{3,7},... | collective-permute-start | bytes 983048 | tf_op jit(solution)/shard_map/ppermute | solution.py:220
  149.6 4.2 %collective-permute-done.16.refs_2_ = f32[128,640]{1,0:T(8,128)S(1)} collective-permute-done((f32[128,640]{1,0:T(8,128)S(1)}, f32[128,640]{1,0:T(8,128)S(1)}, u32[]{:S(2)}, u32[]{:S(2)}) %collective-permute-start.16) | collective-permute-done | bytes 327712 | tf_op jit(solution)/shard_map/ppermute | solution.py:223
  155.0 6.2 %collective-permute-start.7 = (f32[128,640]{1,0:T(8,128)S(1)}, f32[128,640]{1,0:T(8,128)S(1)}, u32[]{:S(2)}, u32[]{:S(2)}) collective-permute-start(f32[128,640]{1,0:T(8,128)S(1)} %get-tuple-element.58), channel_id=1, source_target_pairs={{0,4},{2,6},{12,8},{14,10},{1,5},{3,7},{13,9},{15,11},{16,20},{18,... | collective-permute-start | bytes 983048 | tf_op jit(solution)/shard_map/ppermute | solution.py:223
  166.3 2.1 %collective-permute-done.6.refs_1_ = f32[128,640]{1,0:T(8,128)S(1)} collective-permute-done((f32[128,640]{1,0:T(8,128)S(1)}, f32[128,640]{1,0:T(8,128)S(1)}, u32[]{:S(2)}, u32[]{:S(2)}) %collective-permute-start.6) | collective-permute-done | bytes 327712 | tf_op jit(solution)/shard_map/ppermute | solution.py:217
  170.8 2.1 %collective-permute-done.36 = f32[8,128]{1,0:T(8,128)S(1)} collective-permute-done((f32[8,128]{1,0:T(8,128)S(1)}, f32[8,128]{1,0:T(8,128)S(1)}, u32[]{:S(2)}, u32[]{:S(2)}) %collective-permute-start.36) | collective-permute-done | bytes 4128 | tf_op jit(solution)/shard_map/ppermute | solution.py:290
  172.9 3.9 %collective-permute-start.37 = (f32[8,128]{1,0:T(8,128)S(1)}, f32[8,128]{1,0:T(8,128)S(1)}, u32[]{:S(2)}, u32[]{:S(2)}) collective-permute-start(f32[8,128]{1,0:T(8,128)S(1)} %max.9), channel_id=1, source_target_pairs={{0,4},{2,6},{4,0},{6,2},{8,12},{10,14},{12,8},{14,10},{1,5},{3,7},... | collective-permute-start | bytes 12296 | tf_op jit(solution)/shard_map/ppermute | solution.py:290
  178.4 2.2 %collective-permute-start.38 = (f32[8,128]{1,0:T(8,128)S(1)}, f32[8,128]{1,0:T(8,128)S(1)}, u32[]{:S(2)}, u32[]{:S(2)}) collective-permute-start(f32[8,128]{1,0:T(8,128)S(1)} %max.10), channel_id=1, source_target_pairs={{0,8},{2,10},{4,12},{6,14},{8,0},{10,2},{12,4},{14,6},{1,9},{3,11}... | collective-permute-start | bytes 12296 | tf_op jit(solution)/shard_map/ppermute | solution.py:290
  180.6 2.3 %collective-permute-done.38 = f32[8,128]{1,0:T(8,128)S(1)} collective-permute-done((f32[8,128]{1,0:T(8,128)S(1)}, f32[8,128]{1,0:T(8,128)S(1)}, u32[]{:S(2)}, u32[]{:S(2)}) %collective-permute-start.38) | collective-permute-done | bytes 4128 | tf_op jit(solution)/shard_map/ppermute | solution.py:290
  (173 shorter events, 62.3 us)
Async XLA Ops:
  17.3 24.0 %collective-permute-start.29 = (f32[128,640]{1,0:T(8,128)S(1)}, f32[128,640]{1,0:T(8,128)S(1)}, u32[]{:S(2)}, u32[]{:S(2)}) collective-permute-start(f32[128,640]{1,0:T(8,128)S(1)} %chunk.23), channel_id=1, source_target_pairs={{0,2},{2,0},{4,6},{6,4},{8,10},{10,8},{12,14},{14,12},{1,3},{3,1},... | collective-permute-start | bytes 983048 | tf_op jit(solution)/shard_map/ppermute | solution.py:217
  25.5 18.2 %collective-permute-start.14 = (f32[128,640]{1,0:T(8,128)S(1)}, f32[128,640]{1,0:T(8,128)S(1)}, u32[]{:S(2)}, u32[]{:S(2)}) collective-permute-start(f32[128,640]{1,0:T(8,128)S(1)} %chunk.20), channel_id=1, source_target_pairs={{0,4},{2,6},{4,0},{6,2},{8,12},{10,14},{12,8},{14,10},{1,5},{3,7},... | collective-permute-start | bytes 983048 | tf_op jit(solution)/shard_map/ppermute | solution.py:220
  38.3 25.7 %collective-permute-start.20 = (f32[128,640]{1,0:T(8,128)S(1)}, f32[128,640]{1,0:T(8,128)S(1)}, u32[]{:S(2)}, u32[]{:S(2)}) collective-permute-start(f32[128,640]{1,0:T(8,128)S(1)} %chunk.22), channel_id=1, source_target_pairs={{0,2},{2,0},{4,6},{6,4},{8,10},{10,8},{12,14},{14,12},{1,3},{3,1},... | collective-permute-start | bytes 983048 | tf_op jit(solution)/shard_map/ppermute | solution.py:217
  39.9 21.7 %collective-permute-start.1 = (f32[128,640]{1,0:T(8,128)S(1)}, f32[128,640]{1,0:T(8,128)S(1)}, u32[]{:S(2)}, u32[]{:S(2)}) collective-permute-start(f32[128,640]{1,0:T(8,128)S(1)} %get-tuple-element.60), channel_id=1, source_target_pairs={{0,2},{2,0},{4,6},{6,4},{8,10},{10,8},{12,14},{14,12},{1,3},{3,1},... | collective-permute-start | bytes 983048 | tf_op jit(solution)/shard_map/ppermute | solution.py:217
  41.3 24.1 %collective-permute-start.5 = (f32[128,640]{1,0:T(8,128)S(1)}, f32[128,640]{1,0:T(8,128)S(1)}, u32[]{:S(2)}, u32[]{:S(2)}) collective-permute-start(f32[128,640]{1,0:T(8,128)S(1)} %chunk.19), channel_id=1, source_target_pairs={{0,4},{2,6},{4,0},{6,2},{8,12},{10,14},{12,8},{14,10},{1,5},{3,7},... | collective-permute-start | bytes 983048 | tf_op jit(solution)/shard_map/ppermute | solution.py:220
  43.8 24.9 %collective-permute-start.24 = (f32[128,640]{1,0:T(8,128)S(1)}, f32[128,640]{1,0:T(8,128)S(1)}, u32[]{:S(2)}, u32[]{:S(2)}) collective-permute-start(f32[128,640]{1,0:T(8,128)S(1)} %get-tuple-element.75), channel_id=1, source_target_pairs={{0,2},{2,0},{4,6},{6,4},{8,10},{10,8},{12,14},{14,12},{1,3},{3,1},... | collective-permute-start | bytes 983048 | tf_op jit(solution)/shard_map/ppermute | solution.py:217
  47.6 26.3 %collective-permute-start.33 = (f32[128,640]{1,0:T(8,128)S(1)}, f32[128,640]{1,0:T(8,128)S(1)}, u32[]{:S(2)}, u32[]{:S(2)}) collective-permute-start(f32[128,640]{1,0:T(8,128)S(1)} %get-tuple-element.82), channel_id=1, source_target_pairs={{0,2},{2,0},{4,6},{6,4},{8,10},{10,8},{12,14},{14,12},{1,3},{3,1},... | collective-permute-start | bytes 983048 | tf_op jit(solution)/shard_map/ppermute | solution.py:217
  61.6 15.4 %collective-permute-start.11 = (f32[128,640]{1,0:T(8,128)S(1)}, f32[128,640]{1,0:T(8,128)S(1)}, u32[]{:S(2)}, u32[]{:S(2)}) collective-permute-start(f32[128,640]{1,0:T(8,128)S(1)} %add.98), channel_id=1, source_target_pairs={{0,4},{2,6},{12,8},{14,10},{1,5},{3,7},{13,9},{15,11},{16,20},{18,... | collective-permute-start | bytes 983048 | tf_op jit(solution)/shard_map/ppermute | solution.py:223
  64.0 15.1 %collective-permute-start.2 = (f32[128,640]{1,0:T(8,128)S(1)}, f32[128,640]{1,0:T(8,128)S(1)}, u32[]{:S(2)}, u32[]{:S(2)}) collective-permute-start(f32[128,640]{1,0:T(8,128)S(1)} %add.91), channel_id=1, source_target_pairs={{0,4},{2,6},{12,8},{14,10},{1,5},{3,7},{13,9},{15,11},{16,20},{18,... | collective-permute-start | bytes 983048 | tf_op jit(solution)/shard_map/ppermute | solution.py:223
  65.4 20.7 %collective-permute-start.21 = (f32[128,640]{1,0:T(8,128)S(1)}, f32[128,640]{1,0:T(8,128)S(1)}, u32[]{:S(2)}, u32[]{:S(2)}) collective-permute-start(f32[128,640]{1,0:T(8,128)S(1)} %add.105), channel_id=1, source_target_pairs={{0,4},{2,6},{12,8},{14,10},{1,5},{3,7},{13,9},{15,11},{16,20},{18,... | collective-permute-start | bytes 983048 | tf_op jit(solution)/shard_map/ppermute | solution.py:223
  68.6 24.5 %collective-permute-start.30 = (f32[128,640]{1,0:T(8,128)S(1)}, f32[128,640]{1,0:T(8,128)S(1)}, u32[]{:S(2)}, u32[]{:S(2)}) collective-permute-start(f32[128,640]{1,0:T(8,128)S(1)} %add.111), channel_id=1, source_target_pairs={{0,4},{2,6},{12,8},{14,10},{1,5},{3,7},{13,9},{15,11},{16,20},{18,... | collective-permute-start | bytes 983048 | tf_op jit(solution)/shard_map/ppermute | solution.py:223
  73.9 25.4 %collective-permute-start.25 = (f32[128,640]{1,0:T(8,128)S(1)}, f32[128,640]{1,0:T(8,128)S(1)}, u32[]{:S(2)}, u32[]{:S(2)}) collective-permute-start(f32[128,640]{1,0:T(8,128)S(1)} %add.108), channel_id=1, source_target_pairs={{0,4},{2,6},{12,8},{14,10},{1,5},{3,7},{13,9},{15,11},{16,20},{18,... | collective-permute-start | bytes 983048 | tf_op jit(solution)/shard_map/ppermute | solution.py:223
  77.0 32.8 %collective-permute-start.34 = (f32[128,640]{1,0:T(8,128)}, f32[128,640]{1,0:T(8,128)}, u32[]{:S(2)}, u32[]{:S(2)}) collective-permute-start(f32[128,640]{1,0:T(8,128)} %add.114), channel_id=1, source_target_pairs={{0,4},{2,6},{12,8},{14,10},{1,5},{3,7},{13,9},{15,11},{16,20},{18,... | collective-permute-start | bytes 983048 | tf_op jit(solution)/shard_map/ppermute | solution.py:223
  79.1 33.0 %collective-permute-start = (f32[128,640]{1,0:T(8,128)}, f32[128,640]{1,0:T(8,128)}, u32[]{:S(2)}, u32[]{:S(2)}) collective-permute-start(f32[128,640]{1,0:T(8,128)} %get-tuple-element.57), channel_id=1, source_target_pairs={{0,2},{2,0},{4,6},{6,4},{8,10},{10,8},{12,14},{14,12},{1,3},{3,1},... | collective-permute-start | bytes 983048 | tf_op jit(solution)/shard_map/ppermute | solution.py:217
  86.2 27.5 %collective-permute-start.3 = (f32[128,640]{1,0:T(8,128)}, f32[128,640]{1,0:T(8,128)}, u32[]{:S(2)}, u32[]{:S(2)}) collective-permute-start(f32[128,640]{1,0:T(8,128)} %add.92), channel_id=1, source_target_pairs={{4,8},{6,10},{8,4},{10,6},{5,9},{7,11},{9,5},{11,7},{20,24},{22,26... | collective-permute-start | bytes 983048 | tf_op jit(solution)/shard_map/ppermute | solution.py:226
  93.2 22.3 %collective-permute-start.9 = (f32[128,640]{1,0:T(8,128)}, f32[128,640]{1,0:T(8,128)}, u32[]{:S(2)}, u32[]{:S(2)}) collective-permute-start(f32[128,640]{1,0:T(8,128)} %get-tuple-element.64), channel_id=1, source_target_pairs={{0,2},{2,0},{4,6},{6,4},{8,10},{10,8},{12,14},{14,12},{1,3},{3,1},... | collective-permute-start | bytes 983048 | tf_op jit(solution)/shard_map/ppermute | solution.py:217
  99.3 16.9 %collective-permute-start.12 = (f32[128,640]{1,0:T(8,128)}, f32[128,640]{1,0:T(8,128)}, u32[]{:S(2)}, u32[]{:S(2)}) collective-permute-start(f32[128,640]{1,0:T(8,128)} %add.99), channel_id=1, source_target_pairs={{4,8},{6,10},{8,4},{10,6},{5,9},{7,11},{9,5},{11,7},{20,24},{22,26... | collective-permute-start | bytes 983048 | tf_op jit(solution)/shard_map/ppermute | solution.py:226
  112.2 14.0 %collective-permute-start.28 = (f32[128,640]{1,0:T(8,128)S(1)}, f32[128,640]{1,0:T(8,128)S(1)}, u32[]{:S(2)}, u32[]{:S(2)}) collective-permute-start(f32[128,640]{1,0:T(8,128)S(1)} %copy-done.22), channel_id=1, source_target_pairs={{0,2},{2,0},{4,6},{6,4},{8,10},{10,8},{12,14},{14,12},{1,3},{3,1},... | collective-permute-start | bytes 983048 | tf_op jit(solution)/shard_map/ppermute | solution.py:217
  113.7 18.3 %collective-permute-start.31 = (f32[128,640]{1,0:T(8,128)S(1)}, f32[128,640]{1,0:T(8,128)S(1)}, u32[]{:S(2)}, u32[]{:S(2)}) collective-permute-start(f32[128,640]{1,0:T(8,128)S(1)} %add.112), channel_id=1, source_target_pairs={{4,8},{6,10},{8,4},{10,6},{5,9},{7,11},{9,5},{11,7},{20,24},{22,26... | collective-permute-start | bytes 983048 | tf_op jit(solution)/shard_map/ppermute | solution.py:226
  115.5 22.2 %collective-permute-start.18 = (f32[128,640]{1,0:T(8,128)S(1)}, f32[128,640]{1,0:T(8,128)S(1)}, u32[]{:S(2)}, u32[]{:S(2)}) collective-permute-start(f32[128,640]{1,0:T(8,128)S(1)} %copy-done.20), channel_id=1, source_target_pairs={{0,2},{2,0},{4,6},{6,4},{8,10},{10,8},{12,14},{14,12},{1,3},{3,1},... | collective-permute-start | bytes 983048 | tf_op jit(solution)/shard_map/ppermute | solution.py:217
  116.2 15.8 %collective-permute-start.22 = (f32[128,640]{1,0:T(8,128)S(1)}, f32[128,640]{1,0:T(8,128)S(1)}, u32[]{:S(2)}, u32[]{:S(2)}) collective-permute-start(f32[128,640]{1,0:T(8,128)S(1)} %add.106), channel_id=1, source_target_pairs={{4,8},{6,10},{8,4},{10,6},{5,9},{7,11},{9,5},{11,7},{20,24},{22,26... | collective-permute-start | bytes 983048 | tf_op jit(solution)/shard_map/ppermute | solution.py:226
  121.1 17.3 %collective-permute-start.27 = (f32[128,640]{1,0:T(8,128)S(1)}, f32[128,640]{1,0:T(8,128)S(1)}, u32[]{:S(2)}, u32[]{:S(2)}) collective-permute-start(f32[128,640]{1,0:T(8,128)S(1)} %copy-done.18), channel_id=1, source_target_pairs={{0,2},{2,0},{4,6},{6,4},{8,10},{10,8},{12,14},{14,12},{1,3},{3,1},... | collective-permute-start | bytes 983048 | tf_op jit(solution)/shard_map/ppermute | solution.py:217
  126.2 14.1 %collective-permute-start.4 = (f32[128,640]{1,0:T(8,128)S(1)}, f32[128,640]{1,0:T(8,128)S(1)}, u32[]{:S(2)}, u32[]{:S(2)}) collective-permute-start(f32[128,640]{1,0:T(8,128)S(1)} %get-tuple-element.93), channel_id=1, source_target_pairs={{0,4},{2,6},{4,0},{6,2},{8,12},{10,14},{12,8},{14,10},{1,5},{3,7},... | collective-permute-start | bytes 983048 | tf_op jit(solution)/shard_map/ppermute | solution.py:220
  131.9 15.5 %collective-permute-start.13 = (f32[128,640]{1,0:T(8,128)S(1)}, f32[128,640]{1,0:T(8,128)S(1)}, u32[]{:S(2)}, u32[]{:S(2)}) collective-permute-start(f32[128,640]{1,0:T(8,128)S(1)} %get-tuple-element.91), channel_id=1, source_target_pairs={{0,4},{2,6},{4,0},{6,2},{8,12},{10,14},{12,8},{14,10},{1,5},{3,7},... | collective-permute-start | bytes 983048 | tf_op jit(solution)/shard_map/ppermute | solution.py:220
  132.0 21.8 %collective-permute-start.16 = (f32[128,640]{1,0:T(8,128)S(1)}, f32[128,640]{1,0:T(8,128)S(1)}, u32[]{:S(2)}, u32[]{:S(2)}) collective-permute-start(f32[128,640]{1,0:T(8,128)S(1)} %get-tuple-element.65), channel_id=1, source_target_pairs={{0,4},{2,6},{12,8},{14,10},{1,5},{3,7},{13,9},{15,11},{16,20},{18,... | collective-permute-start | bytes 983048 | tf_op jit(solution)/shard_map/ppermute | solution.py:223
  137.7 16.6 %collective-permute-start.26 = (f32[128,640]{1,0:T(8,128)S(1)}, f32[128,640]{1,0:T(8,128)S(1)}, u32[]{:S(2)}, u32[]{:S(2)}) collective-permute-start(f32[128,640]{1,0:T(8,128)S(1)} %add.109), channel_id=1, source_target_pairs={{4,8},{6,10},{8,4},{10,6},{5,9},{7,11},{9,5},{11,7},{20,24},{22,26... | collective-permute-start | bytes 983048 | tf_op jit(solution)/shard_map/ppermute | solution.py:226
  138.4 16.6 %collective-permute-start.35 = (f32[128,640]{1,0:T(8,128)S(1)}, f32[128,640]{1,0:T(8,128)S(1)}, u32[]{:S(2)}, u32[]{:S(2)}) collective-permute-start(f32[128,640]{1,0:T(8,128)S(1)} %add.115), channel_id=1, source_target_pairs={{4,8},{6,10},{8,4},{10,6},{5,9},{7,11},{9,5},{11,7},{20,24},{22,26... | collective-permute-start | bytes 983048 | tf_op jit(solution)/shard_map/ppermute | solution.py:226
  140.4 20.8 %collective-permute-start.23 = (f32[128,640]{1,0:T(8,128)S(1)}, f32[128,640]{1,0:T(8,128)S(1)}, u32[]{:S(2)}, u32[]{:S(2)}) collective-permute-start(f32[128,640]{1,0:T(8,128)S(1)} %add_add_fusion.1), channel_id=1, source_target_pairs={{0,4},{2,6},{4,0},{6,2},{8,12},{10,14},{12,8},{14,10},{1,5},{3,7},... | collective-permute-start | bytes 983048 | tf_op jit(solution)/shard_map/ppermute | solution.py:220
  147.4 15.4 %collective-permute-start.32 = (f32[128,640]{1,0:T(8,128)S(1)}, f32[128,640]{1,0:T(8,128)S(1)}, u32[]{:S(2)}, u32[]{:S(2)}) collective-permute-start(f32[128,640]{1,0:T(8,128)S(1)} %add_add_fusion), channel_id=1, source_target_pairs={{0,4},{2,6},{4,0},{6,2},{8,12},{10,14},{12,8},{14,10},{1,5},{3,7},... | collective-permute-start | bytes 983048 | tf_op jit(solution)/shard_map/ppermute | solution.py:220
  153.8 11.5 %collective-permute-start.15 = (f32[128,640]{1,0:T(8,128)S(1)}, f32[128,640]{1,0:T(8,128)S(1)}, u32[]{:S(2)}, u32[]{:S(2)}) collective-permute-start(f32[128,640]{1,0:T(8,128)S(1)} %add.102), channel_id=1, source_target_pairs={{0,2},{2,0},{4,6},{6,4},{8,10},{10,8},{12,14},{14,12},{1,3},{3,1},... | collective-permute-start | bytes 983048 | tf_op jit(solution)/shard_map/ppermute | solution.py:217
  154.3 11.0 %collective-permute-start.17 = (f32[128,640]{1,0:T(8,128)S(1)}, f32[128,640]{1,0:T(8,128)S(1)}, u32[]{:S(2)}, u32[]{:S(2)}) collective-permute-start(f32[128,640]{1,0:T(8,128)S(1)} %get-tuple-element.95), channel_id=1, source_target_pairs={{4,8},{6,10},{8,4},{10,6},{5,9},{7,11},{9,5},{11,7},{20,24},{22,26... | collective-permute-start | bytes 983048 | tf_op jit(solution)/shard_map/ppermute | solution.py:226
  155.0 11.2 %collective-permute-start.7 = (f32[128,640]{1,0:T(8,128)S(1)}, f32[128,640]{1,0:T(8,128)S(1)}, u32[]{:S(2)}, u32[]{:S(2)}) collective-permute-start(f32[128,640]{1,0:T(8,128)S(1)} %get-tuple-element.58), channel_id=1, source_target_pairs={{0,4},{2,6},{12,8},{14,10},{1,5},{3,7},{13,9},{15,11},{16,20},{18,... | collective-permute-start | bytes 983048 | tf_op jit(solution)/shard_map/ppermute | solution.py:223
  (48 other events, 212.6 us)

commit v2 on v1

v2 whole, which is shorter than its diff:
```python
import functools
import math

import jax
import jax.numpy as jnp
from jax import lax
from jax.experimental import pallas as pl
from jax.experimental.pallas import tpu as pltpu
from jax.sharding import PartitionSpec as P

HD = 128
GROUP = 8
BUCKET = 128
BATCH = 16
VMEM_BYTES = 60 * 1024 * 1024
HBM = pl.BlockSpec(memory_space=pltpu.HBM)
PARAMS = pltpu.CompilerParams(vmem_limit_bytes=VMEM_BYTES)
FAR3, FAR2, PAIR, OWN = range(4)
CROSS, SAME = True, False


def attend_heads(lengths, rewards, q, ck, cv, nk, nv, cot, out, rows):
    rollouts, steps, width = q.shape
    key_heads = ck.shape[2] // HD
    heads = width // HD // key_heads
    ctx = ck.shape[1]
    slots = ctx + steps
    padded = -(-slots // HD) * HD
    pad = padded - slots
    scaling = 1.0 / math.sqrt(HD)

    def by_head(ref, r, g):
        return jnp.concatenate(
            [
                ref[r, :, (g * heads + j) * HD : (g * heads + j + 1) * HD].astype(jnp.float32)
                for j in range(heads)
            ],
            axis=0,
        )

    def joined(past, fresh, r, g):
        lanes = slice(g * HD, (g + 1) * HD)
        fresh = jnp.concatenate(
            [fresh[r, :, lanes].astype(jnp.float32), jnp.zeros((pad, HD), jnp.float32)], axis=0
        ).astype(jnp.bfloat16)
        return jnp.concatenate([past[r, :, lanes], fresh], axis=0)

    shape = (heads * steps, padded)
    column = lax.broadcasted_iota(jnp.int32, shape, 1)
    step = lax.broadcasted_iota(jnp.int32, shape, 0) % steps
    fresh_live = (column >= ctx) & (column - ctx <= step)
    advantages, lives = [], []
    for base in range(0, rollouts, GROUP):
        centre = rewards[base]
        for i in range(1, GROUP):
            centre = centre + rewards[base + i]
        centre = centre * (1.0 / GROUP)
        spread = (rewards[base] - centre) * (rewards[base] - centre)
        for i in range(1, GROUP):
            spread = spread + (rewards[base + i] - centre) * (rewards[base + i] - centre)
        spread = jnp.sqrt(jnp.full((1, HD), spread * (1.0 / GROUP), jnp.float32))
        spread = jnp.maximum(spread, 1.0)
        for r in range(base, base + GROUP):
            advantages.append(jnp.full((1, HD), rewards[r] - centre, jnp.float32) / spread)
    for r in range(rollouts):
        lives.append((column < lengths[r]) | fresh_live)
    units = [(r, g) for g in range(key_heads) for r in range(rollouts)]
    for start in range(0, len(units), BATCH):
        batch = units[start : start + BATCH]
        scores = [
            lax.dot_general(
                by_head(q, r, g).astype(jnp.bfloat16),
                joined(ck, nk, r, g),
                (((1,), (1,)), ((), ())),
                preferred_element_type=jnp.float32,
            )
            for r, g in batch
        ]
        scores = [
            jnp.where(lives[r], x * scaling, -1e30) for (r, g), x in zip(batch, scores)
        ]
        highest = [jnp.max(x, axis=1, keepdims=True) for x in scores]
        lift = [jnp.exp(x - top) for x, top in zip(scores, highest)]
        totals = [jnp.sum(x, axis=1, keepdims=True) for x in lift]
        weights = [(x / total).astype(jnp.bfloat16) for x, total in zip(lift, totals)]
        results = [
            jnp.dot(w, joined(cv, nv, r, g), preferred_element_type=jnp.float32)
            for (r, g), w in zip(batch, weights)
        ]
        value_cots = [
            lax.dot_general(
                w,
                (by_head(cot, r, g) * advantages[r]).astype(jnp.bfloat16),
                (((0,), (0,)), ((), ())),
                preferred_element_type=jnp.float32,
            )
            for (r, g), w in zip(batch, weights)
        ]
        for (r, g), result, value_cot in zip(batch, results, value_cots):
            for j in range(heads):
                out[r, :, (g * heads + j) * HD : (g * heads + j + 1) * HD] = result[
                    j * steps : (j + 1) * steps
                ].astype(jnp.bfloat16)
            rows[r * slots : (r + 1) * slots, g * HD : (g + 1) * HD] = value_cot[:slots]


def block_of(kind):
    plane_kind, cross = kind
    rank = lax.axis_index("dp")
    plane = rank // 2
    row = rank - plane * 2
    low = plane < 2
    if plane_kind == FAR3:
        target = jnp.where(low, 3, 0)
    elif plane_kind == FAR2:
        target = jnp.where(low, 2, 1)
    elif plane_kind == PAIR:
        target = plane + 1 - 2 * (plane - (plane // 2) * 2)
    else:
        target = plane
    return target * 2 + (1 - row if cross else row)


def start_features(features, kinds, buffers, sems):
    copies = []
    for i, kind in enumerate(kinds):
        width = buffers.shape[2]
        first = pl.multiple_of(block_of(kind) * width, HD)
        copy = pltpu.make_async_copy(
            features.at[:, pl.ds(first, width)], buffers.at[i], sems.at[i]
        )
        copy.start()
        copies.append(copy)
    return copies


def begin_kernel(kinds, *refs):
    ins, refs = refs[:8], refs[8:]
    features, refs = refs[0], refs[1:]
    out, halves, refs = refs[0], refs[1:3], refs[3:]
    firsts, refs = refs[: len(kinds)], refs[len(kinds) :]
    bufs, (rows, blocks, sems, block_sems) = refs[:8], refs[8:]
    copies = []
    for i in range(8):
        copy = pltpu.make_async_copy(ins[i], bufs[i], sems.at[i])
        copy.start()
        copies.append(copy)
    block_copies = start_features(features, kinds, blocks, block_sems)
    for copy in copies:
        copy.wait()
    attend_heads(*bufs, out, rows)
    cots = rows[...].T.astype(jnp.bfloat16)
    half = cots.shape[0] // 2
    halves[0][...] = cots[:half]
    halves[1][...] = cots[half:]
    for i in range(len(kinds)):
        block_copies[i].wait()
        firsts[i][...] = jnp.dot(cots[:half], blocks[i], preferred_element_type=jnp.float32)


def begin(arrays, features, kinds, width):
    lengths, rewards, queries, ck = arrays[:4]
    depth = features.shape[0]
    columns = ck.shape[2]
    half = columns // 2
    shapes = (
        [jax.ShapeDtypeStruct(queries.shape, jnp.bfloat16)]
        + [jax.ShapeDtypeStruct((half, depth), jnp.bfloat16)] * 2
        + [jax.ShapeDtypeStruct((half, width), jnp.float32)] * len(kinds)
    )
    return pl.pallas_call(
        functools.partial(begin_kernel, kinds),
        in_specs=[HBM] * 9,
        out_specs=[pl.BlockSpec(memory_space=pltpu.VMEM)] * len(shapes),
        out_shape=shapes,
        scratch_shapes=[pltpu.SMEM(x.shape, x.dtype) for x in arrays[:2]]
        + [pltpu.VMEM(x.shape, x.dtype) for x in arrays[2:]]
        + [
            pltpu.VMEM((depth, columns), jnp.float32),
            pltpu.VMEM((max(len(kinds), 1), depth, width), jnp.bfloat16),
            pltpu.SemaphoreType.DMA((8,)),
            pltpu.SemaphoreType.DMA((max(len(kinds), 1),)),
        ],
        compiler_params=PARAMS,
        cost_estimate=pl.CostEstimate(
            flops=6 * queries.size * HD, bytes_accessed=10 << 20, transcendentals=queries.size
        ),
        name="attend",
    )(*arrays, features)


def chunk_kernel(jobs, features, half_a, half_b, *refs):
    kinds = [kind for kind, _ in jobs]
    count = sum(len(which) for _, which in jobs)
    outs, (blocks, sems) = refs[:count], refs[count:]
    copies = start_features(features, kinds, blocks, sems)
    cots = (half_a, half_b)
    place = 0
    for i, (_, which) in enumerate(jobs):
        copies[i].wait()
        for h in which:
            outs[place][...] = jnp.dot(
                cots[h][...], blocks[i], preferred_element_type=jnp.float32
            )
            place += 1


def chunks(jobs, features, halves, width):
    depth = features.shape[0]
    half = halves[0].shape[0]
    count = sum(len(which) for _, which in jobs)
    vmem = pl.BlockSpec(memory_space=pltpu.VMEM)
    return pl.pallas_call(
        functools.partial(chunk_kernel, jobs),
        in_specs=[HBM, vmem, vmem],
        out_specs=[vmem] * count,
        out_shape=[jax.ShapeDtypeStruct((half, width), jnp.float32)] * count,
        scratch_shapes=[
            pltpu.VMEM((len(jobs), depth, width), jnp.bfloat16),
            pltpu.SemaphoreType.DMA((len(jobs),)),
        ],
        compiler_params=PARAMS,
        cost_estimate=pl.CostEstimate(
            flops=2 * depth * width * half * count,
            bytes_accessed=2 * depth * width * len(jobs) + 4 * half * width * count,
            transcendentals=0,
        ),
        name="chunk",
    )(features, *halves)


def finish_kernel(half, count, *refs):
    grad, peaks = refs[-2:]
    total = refs[0][...]
    for ref in refs[1:count]:
        total = total + ref[...]
    buckets = total.shape[0] // BUCKET
    lane = lax.broadcasted_iota(jnp.int32, peaks.shape, 1)
    peak = refs[count + 1][...] if len(refs) > count + 2 else jnp.zeros(peaks.shape, jnp.float32)
    for b in range(buckets):
        top = jnp.abs(total[b * BUCKET : (b + 1) * BUCKET])
        top = jnp.max(jnp.max(top, axis=0, keepdims=True), axis=1, keepdims=True)
        peak = jnp.where(lane == half * buckets + b, top, peak)
    peaks[...] = peak
    grad[...] = total.T


def finish(half, parts, grad, peaks, columns):
    size, width = parts[0].shape
    count = len(parts)
    whole = pl.BlockSpec((size, width), lambda i: (0, 0))
    tile = pl.BlockSpec((8, 128), lambda i: (0, 0))
    in_specs = [whole] * count
    args = list(parts)
    aliases = {}
    if grad is not None:
        in_specs += [pl.BlockSpec(memory_space=pl.ANY), tile]
        args += [grad, peaks]
        aliases = {count: 0}
    return pl.pallas_call(
        functools.partial(finish_kernel, half, count),
        grid=(1,),
        in_specs=in_specs,
        out_specs=[pl.BlockSpec((width, size), lambda i: (0, half)), tile],
        out_shape=[
            jax.ShapeDtypeStruct((width, columns), jnp.float32),
            jax.ShapeDtypeStruct((8, 128), jnp.float32),
        ],
        input_output_aliases=aliases,
        compiler_params=PARAMS,
        name="finish",
    )(*args)


def reduce_on_grid(features, halves, firsts, dp):
    width = features.shape[1] // dp
    columns = 2 * halves[0].shape[0]
    rank = lax.axis_index("dp")
    edge = (rank < 2) | (rank >= 6)

    def across(x):
        return lax.ppermute(x, "dp", [(r, r ^ 1) for r in range(dp)])

    def pair(x):
        return lax.ppermute(x, "dp", [(r, r ^ 2) for r in range(dp)])

    def outward(x):
        return lax.ppermute(x, "dp", [(r, r ^ 2) for r in (0, 1, 6, 7)])

    def middle(x):
        return lax.ppermute(x, "dp", [(r, r ^ 6) for r in (2, 3, 4, 5)])

    def make(*jobs):
        return chunks(jobs, features, halves, width)

    a, b = 0, 1
    cross3a, crosspa = firsts
    cross3b, ownpa = make(((FAR3, CROSS), (b,)), ((PAIR, SAME), (a,)))
    cross2a, cross2b, own3a, own3b = make(((FAR2, CROSS), (a, b)), ((FAR3, SAME), (a, b)))
    crosspb, own2a, own2b = make(((PAIR, CROSS), (b,)), ((FAR2, SAME), (a, b)))
    crossoa, crossob, ownpb = make(((OWN, CROSS), (a, b)), ((PAIR, SAME), (b,)))
    ownoa, ownob = make(((OWN, SAME), (a, b)))

    y0 = across(cross3a)
    e0 = pair(crosspa)
    y1 = across(cross3b)
    e1 = outward(ownpa)
    y2 = across(cross2a)
    e2 = outward(own3a + y0)
    y3 = across(cross2b)
    e3 = outward(own3b + y1)
    m3 = middle(own3a + y0 + e2)
    y4 = across(crosspb)
    e4 = outward(own2a + y2)
    m4 = middle(own3b + y1 + e3)
    y5 = across(crossoa + e0)
    cut = own2b.shape[0] // 2
    e5 = []
    for part in (slice(0, cut), slice(cut, None)):
        e5.append(
            pair(jnp.where(edge, own2b[part] + y3[part], ownpa[part] + m3[part]))
        )
    m5 = middle(own2a + y2 + e4)
    y6 = across(crossob)
    e6 = pair(ownpb + y4 + m4)
    m6 = []
    for i, part in enumerate((slice(0, cut), slice(cut, None))):
        m6.append(middle(own2b[part] + y3[part] + e5[i]))
    arrived = jnp.where(edge, jnp.concatenate(e5, axis=0), e1)
    grad, peaks = finish(a, [ownoa, y5, arrived, m5], None, None, columns)
    grad, peaks = finish(b, [ownob, y6, e6, jnp.concatenate(m6, axis=0)], grad, peaks, columns)
    for hop in (1, 2, 4):
        peaks = jnp.maximum(
            peaks, lax.ppermute(peaks, "dp", [(r, r ^ hop) for r in range(dp)])
        )
    return grad, peaks[0, : columns // BUCKET]


def reduce_plain(features, halves):
    cots = jnp.concatenate(halves, axis=0)
    partial_grad = lax.dot_general(
        features, cots, (((0,), (1,)), ((), ())), preferred_element_type=jnp.float32
    )
    grad = lax.psum_scatter(partial_grad, "dp", scatter_dimension=0, tiled=True)
    peaks = jnp.max(jnp.abs(grad).reshape(-1, cots.shape[0] // BUCKET, BUCKET), axis=(0, 2))
    return grad, lax.pmax(peaks, "dp")


def per_device(
    dp,
    queries,
    cache_keys,
    cache_values,
    new_keys,
    new_values,
    features,
    cotangent,
    rewards,
    lengths,
):
    flat = features.reshape(-1, features.shape[2])
    arrays = (
        lengths,
        rewards,
        queries,
        cache_keys,
        cache_values,
        new_keys,
        new_values,
        cotangent,
    )
    on_grid = dp == 8
    kinds = ((FAR3, CROSS), (PAIR, CROSS)) if on_grid else ()
    width = features.shape[2] // 8 if on_grid else BUCKET
    attended, half_a, half_b, *firsts = begin(arrays, flat, kinds, width)
    if on_grid:
        grad, peaks = reduce_on_grid(flat, (half_a, half_b), firsts, dp)
    else:
        grad, peaks = reduce_plain(flat, (half_a, half_b))
    return attended, grad, peaks


def solution(mesh):
    split = P(("groups", "dp"), None, "tensor")
    rows = P(("groups", "dp"))
    in_specs = (
        split,
        split,
        split,
        split,
        split,
        P(("groups", "dp"), None, None),
        split,
        rows,
        rows,
    )
    out_specs = (split, P(("groups", "dp"), "tensor"), P(("groups", "tensor")))
    return jax.shard_map(
        functools.partial(per_device, mesh.shape["dp"]),
        mesh=mesh,
        in_specs=in_specs,
        out_specs=out_specs,
        check_vma=False,
    )
```

time: 184 us -> 151 us (0.82)
  local copies, waits for them, and re-layouts: 19.5 us -> 1.39 us
  waiting for transfers between devices: 55.6 us -> 44 us
  starting transfers between devices: 64.1 us -> 53.4 us
  other arithmetic: 6.33 us -> 15 us
    unnamed x82 -> x18, local copies, waits for them, and re-layouts: 18.3 us -> 0.88 us
    ppermute x6 -> x4, waiting for transfers between devices: 5.72 us -> 22.1 us  [pair(): return lax.ppermute(x, 'dp', [(r, r ^ 2) for r in range(dp)])]
    ppermute x8 -> x4, waiting for transfers between devices: 17.4 us -> 1.82 us  [outward(): return lax.ppermute(x, 'dp', [(r, r ^ 2) for r in (0, 1, 6, 7)])]
    ppermute x14 -> x7, waiting for transfers between devices: 26.6 us -> 14.6 us  [across(): return lax.ppermute(x, 'dp', [(r, r ^ 1) for r in range(dp)])]
    ppermute x6 -> x4, starting transfers between devices: 12.1 us -> 4.56 us  [pair(): return lax.ppermute(x, 'dp', [(r, r ^ 2) for r in range(dp)])]
    add x18 -> x9, other arithmetic: 4.03 us -> 10.2 us  [the longest x2 3.35 us: reduce_on_grid(): m5 = middle(own2a + y2 + e4)]
    ppermute x8 -> x4, starting transfers between devices: 23.5 us -> 20.7 us  [outward(): return lax.ppermute(x, 'dp', [(r, r ^ 2) for r in (0, 1, 6, 7)])]
    ppermute x14 -> x7, starting transfers between devices: 14 us -> 11.3 us  [across(): return lax.ppermute(x, 'dp', [(r, r ^ 1) for r in range(dp)])]
  transfers between devices with their start and end apart: 39 -> 23, of which waited for: 17 -> 10; matrix products, arithmetic and copies ran while one was open for 3% -> 10% of each run, Pallas kernels for 17% -> 17%
where the time goes in v2:
time: 151 us; the launch traced here: 150 us
  starting transfers between devices  53.4 us (35%)
  waiting for transfers between devices  44 us (29%)
  Pallas kernels  35.3 us (23%)
  other arithmetic  15 us (10%)
    pallas_call x5, Pallas kernels, chunks(): pl.pallas_call(functools.partial(chunk_kernel, jobs), in_specs=[HBM, vmem...  23.3 us
    ppermute x4, waiting for transfers between devices, pair(): return lax.ppermute(x, 'dp', [(r, r ^ 2) for r in range(dp)])  22.1 us
    ppermute x4, starting transfers between devices, outward(): return lax.ppermute(x, 'dp', [(r, r ^ 2) for r in (0, 1, 6, 7)])  20.7 us
    ppermute x7, waiting for transfers between devices, across(): return lax.ppermute(x, 'dp', [(r, r ^ 1) for r in range(dp)])  14.6 us
    ppermute x7, starting transfers between devices, across(): return lax.ppermute(x, 'dp', [(r, r ^ 1) for r in range(dp)])  11.3 us
    ppermute x3, starting transfers between devices, reduce_on_grid(): lax.ppermute(peaks, 'dp', [(r, r ^ hop) for r in range(dp)])  9.31 us
    ppermute x5, starting transfers between devices, middle(): return lax.ppermute(x, 'dp', [(r, r ^ 6) for r in (2, 3, 4, 5)])  7.45 us
    pallas_call x1, Pallas kernels, begin(): pl.pallas_call(functools.partial(begin_kernel, kinds), in_specs=[HBM] * 9...  6.18 us
  transfers between devices with their start and end apart: 23, of which 10 were waited for; matrix products, arithmetic and copies ran while one was open for 10% of the time, Pallas kernels for 17%

profile of v2, /device:TPU:0, one launch (start us, length us, event | category | flops | bytes accessed | tf_op | source)
XLA Modules:
  0.0 149.9 jit_solution(8917207191291199597)
XLA Ops:
  0.6 6.2 %attend.1 = (bf16[8,8,4096]{2,1,0:T(8,128)(2,1)}, bf16[256,832]{1,0:T(8,128)(2,1)}, bf16[256,832]{1,0:T(8,128)(2,1)}, f32[256,640]{1,0:T(8,128)}, f32[256,640]{1,0:T(8,128)}) custom-call(s32[8]{0:T(128)} %refs_0_.1, f32[8]{0:T(128)} %refs_1_.1, bf16[8,8,4096]{2,1,0:T(8,128)(2,1)} %refs_2_.1, bf16[8,96,512]{2,1,0:T(8,128)(2,1)} %refs_3_.1, ...), custom_call_target="tpu_custom_call" | custom-call | flops 201326592 | bytes 10485760 | tf_op jit(solution)/shard_map/attend/pallas_call | solution.py:171
  6.8 3.0 %collective-permute-start.7 = (f32[256,640]{1,0:T(8,128)}, f32[256,640]{1,0:T(8,128)S(1)}, u32[]{:S(2)}, u32[]{:S(2)}) collective-permute-start(f32[256,640]{1,0:T(8,128)} %get-tuple-element.39), channel_id=1, source_target_pairs={{0,2},{2,0},{4,6},{6,4},{8,10},{10,8},{12,14},{14,12},{1,3},{3,1},... | collective-permute-start | bytes 1966088 | tf_op jit(solution)/shard_map/ppermute | solution.py:282
  9.9 4.4 %chunk.9 = (f32[256,640]{1,0:T(8,128)}, f32[256,640]{1,0:T(8,128)}) custom-call(bf16[832,5120]{1,0:T(8,128)(2,1)} %bitcast.4, bf16[256,832]{1,0:T(8,128)(2,1)} %get-tuple-element.27.half_a, bf16[256,832]{1,0:T(8,128)(2,1)} %get-tuple-element.28.half_b), custom_call_target="tpu_custom_call" | custom-call | flops 545259520 | bytes 3440640 | tf_op jit(solution)/shard_map/chunk/pallas_call | solution.py:213
  14.4 5.1 %chunk.8 = (f32[256,640]{1,0:T(8,128)}, f32[256,640]{1,0:T(8,128)}, f32[256,640]{1,0:T(8,128)}, f32[256,640]{1,0:T(8,128)}) custom-call(bf16[832,5120]{1,0:T(8,128)(2,1)} %bitcast.5, bf16[256,832]{1,0:T(8,128)(2,1)} %get-tuple-element.27.half_a, bf16[256,832]{1,0:T(8,128)(2,1)} %get-tuple-element.28.half_b), custom_call_target="tpu_custom_call" | custom-call | flops 1090519040 | bytes 4751360 | tf_op jit(solution)/shard_map/chunk/pallas_call | solution.py:213
  19.5 6.1 %collective-permute-done.7 = f32[256,640]{1,0:T(8,128)S(1)} collective-permute-done((f32[256,640]{1,0:T(8,128)}, f32[256,640]{1,0:T(8,128)S(1)}, u32[]{:S(2)}, u32[]{:S(2)}) %collective-permute-start.7) | collective-permute-done | bytes 655392 | tf_op jit(solution)/shard_map/ppermute | solution.py:282
  26.8 4.1 %collective-permute-start.8 = (f32[256,640]{1,0:T(8,128)S(1)}, f32[256,640]{1,0:T(8,128)S(1)}, u32[]{:S(2)}, u32[]{:S(2)}) collective-permute-start(f32[256,640]{1,0:T(8,128)S(1)} %add.55), channel_id=1, source_target_pairs={{0,4},{2,6},{12,8},{14,10},{1,5},{3,7},{13,9},{15,11},{16,20},{18,... | collective-permute-start | bytes 1966088 | tf_op jit(solution)/shard_map/ppermute | solution.py:288
  30.9 1.6 %collective-permute-start.17 = (f32[256,640]{1,0:T(8,128)}, f32[256,640]{1,0:T(8,128)S(1)}, u32[]{:S(2)}, u32[]{:S(2)}) collective-permute-start(f32[256,640]{1,0:T(8,128)} %get-tuple-element.44), channel_id=1, source_target_pairs={{0,2},{2,0},{4,6},{6,4},{8,10},{10,8},{12,14},{14,12},{1,3},{3,1},... | collective-permute-start | bytes 1966088 | tf_op jit(solution)/shard_map/ppermute | solution.py:282
  32.4 7.2 %collective-permute-done.2 = f32[256,640]{1,0:T(8,128)S(1)} collective-permute-done((f32[256,640]{1,0:T(8,128)}, f32[256,640]{1,0:T(8,128)S(1)}, u32[]{:S(2)}, u32[]{:S(2)}) %collective-permute-start.2) | collective-permute-done | bytes 655392 | tf_op jit(solution)/shard_map/ppermute | solution.py:282
  39.7 4.9 %collective-permute-start.3 = (f32[256,640]{1,0:T(8,128)S(1)}, f32[256,640]{1,0:T(8,128)}, u32[]{:S(2)}, u32[]{:S(2)}) collective-permute-start(f32[256,640]{1,0:T(8,128)S(1)} %add.51), channel_id=1, source_target_pairs={{0,4},{2,6},{12,8},{14,10},{1,5},{3,7},{13,9},{15,11},{16,20},{18,... | collective-permute-start | bytes 1966088 | tf_op jit(solution)/shard_map/ppermute | solution.py:288
  47.7 4.7 %chunk.7 = (f32[256,640]{1,0:T(8,128)}, f32[256,640]{1,0:T(8,128)}, f32[256,640]{1,0:T(8,128)}) custom-call(bf16[832,5120]{1,0:T(8,128)(2,1)} %bitcast.6, bf16[256,832]{1,0:T(8,128)(2,1)} %get-tuple-element.27.half_a, bf16[256,832]{1,0:T(8,128)(2,1)} %get-tuple-element.28.half_b), custom_call_target="tpu_custom_call" | custom-call | flops 817889280 | bytes 4096000 | tf_op jit(solution)/shard_map/chunk/pallas_call | solution.py:213
  53.7 2.1 %collective-permute-start.1 = (f32[256,640]{1,0:T(8,128)}, f32[256,640]{1,0:T(8,128)S(1)}, u32[]{:S(2)}, u32[]{:S(2)}) collective-permute-start(f32[256,640]{1,0:T(8,128)} %get-tuple-element.32), channel_id=1, source_target_pairs={{0,2},{2,0},{4,6},{6,4},{8,10},{10,8},{12,14},{14,12},{1,3},{3,1},... | collective-permute-start | bytes 1966088 | tf_op jit(solution)/shard_map/ppermute | solution.py:282
  57.1 1.8 %collective-permute-done.3 = f32[256,640]{1,0:T(8,128)} collective-permute-done((f32[256,640]{1,0:T(8,128)S(1)}, f32[256,640]{1,0:T(8,128)}, u32[]{:S(2)}, u32[]{:S(2)}) %collective-permute-start.3) | collective-permute-done | bytes 655392 | tf_op jit(solution)/shard_map/ppermute | solution.py:288
  58.9 5.3 %collective-permute-start.18 = (f32[256,640]{1,0:T(8,128)S(1)}, f32[256,640]{1,0:T(8,128)}, u32[]{:S(2)}, u32[]{:S(2)}) collective-permute-start(f32[256,640]{1,0:T(8,128)S(1)} %add.63), channel_id=1, source_target_pairs={{0,4},{2,6},{12,8},{14,10},{1,5},{3,7},{13,9},{15,11},{16,20},{18,... | collective-permute-start | bytes 1966088 | tf_op jit(solution)/shard_map/ppermute | solution.py:288
  64.3 2.0 %add.52 = f32[256,640]{1,0:T(8,128)} add(f32[256,640]{1,0:T(8,128)S(1)} %add.51, f32[256,640]{1,0:T(8,128)} %collective-permute-done.3) | non-fusion elementwise | flops 163840 | bytes 1966080 | tf_op jit(solution)/shard_map/add | solution.py:315
  66.3 6.8 %collective-permute-done.14 = f32[256,640]{1,0:T(8,128)} collective-permute-done((f32[256,640]{1,0:T(8,128)}, f32[256,640]{1,0:T(8,128)}, u32[]{:S(2)}, u32[]{:S(2)}) %collective-permute-start.14) | collective-permute-done | bytes 655392 | tf_op jit(solution)/shard_map/ppermute | solution.py:285
  74.6 4.8 %chunk.6 = (f32[256,640]{1,0:T(8,128)}, f32[256,640]{1,0:T(8,128)}, f32[256,640]{1,0:T(8,128)}) custom-call(bf16[832,5120]{1,0:T(8,128)(2,1)} %bitcast.7, bf16[256,832]{1,0:T(8,128)(2,1)} %get-tuple-element.27.half_a, bf16[256,832]{1,0:T(8,128)(2,1)} %get-tuple-element.28.half_b), custom_call_target="tpu_custom_call" | custom-call | flops 817889280 | bytes 4096000 | tf_op jit(solution)/shard_map/chunk/pallas_call | solution.py:213
  80.9 6.4 %collective-permute-start.16 = (f32[256,640]{1,0:T(8,128)S(1)}, f32[256,640]{1,0:T(8,128)S(1)}, u32[]{:S(2)}, u32[]{:S(2)}) collective-permute-start(f32[256,640]{1,0:T(8,128)S(1)} %copy-done.5), channel_id=1, source_target_pairs={{0,4},{2,6},{12,8},{14,10},{1,5},{3,7},{13,9},{15,11},{16,20},{18,... | collective-permute-start | bytes 1966088 | tf_op jit(solution)/shard_map/ppermute | solution.py:288
  87.4 1.6 %collective-permute-start.15 = (f32[256,640]{1,0:T(8,128)S(1)}, f32[256,640]{1,0:T(8,128)S(1)}, u32[]{:S(2)}, u32[]{:S(2)}) collective-permute-start(f32[256,640]{1,0:T(8,128)S(1)} %add.62), channel_id=1, source_target_pairs={{0,2},{2,0},{4,6},{6,4},{8,10},{10,8},{12,14},{14,12},{1,3},{3,1},... | collective-permute-start | bytes 1966088 | tf_op jit(solution)/shard_map/ppermute | solution.py:282
  90.3 2.0 %collective-permute-start.12 = (f32[128,640]{1,0:T(8,128)S(1)}, f32[128,640]{1,0:T(8,128)S(1)}, u32[]{:S(2)}, u32[]{:S(2)}) collective-permute-start(f32[128,640]{1,0:T(8,128)S(1)} %get-tuple-element.50), channel_id=1, source_target_pairs={{0,4},{2,6},{4,0},{6,2},{8,12},{10,14},{12,8},{14,10},{1,5},{3,7},... | collective-permute-start | bytes 983048 | tf_op jit(solution)/shard_map/ppermute | solution.py:285
  92.3 2.0 %add.64 = f32[256,640]{1,0:T(8,128)} add(f32[256,640]{1,0:T(8,128)S(1)} %add.63, f32[256,640]{1,0:T(8,128)} %collective-permute-done.18) | non-fusion elementwise | flops 163840 | bytes 1966080 | tf_op jit(solution)/shard_map/add | solution.py:323
  97.0 12.5 %collective-permute-done.10 = f32[128,640]{1,0:T(8,128)S(1)} collective-permute-done((f32[128,640]{1,0:T(8,128)S(1)}, f32[128,640]{1,0:T(8,128)S(1)}, u32[]{:S(2)}, u32[]{:S(2)}) %collective-permute-start.10) | collective-permute-done | bytes 327712 | tf_op jit(solution)/shard_map/ppermute | solution.py:285
  111.0 2.8 %collective-permute-done.12 = f32[128,640]{1,0:T(8,128)S(1)} collective-permute-done((f32[128,640]{1,0:T(8,128)S(1)}, f32[128,640]{1,0:T(8,128)S(1)}, u32[]{:S(2)}, u32[]{:S(2)}) %collective-permute-start.12) | collective-permute-done | bytes 327712 | tf_op jit(solution)/shard_map/ppermute | solution.py:285
  113.7 2.5 %collective-permute-start.5 = (f32[256,640]{1,0:T(8,128)S(1)}, f32[256,640]{1,0:T(8,128)}, u32[]{:S(2)}, u32[]{:S(2)}) collective-permute-start(f32[256,640]{1,0:T(8,128)S(1)} %add_add_fusion), channel_id=1, source_target_pairs={{0,4},{2,6},{4,0},{6,2},{8,12},{10,14},{12,8},{14,10},{1,5},{3,7},... | collective-permute-start | bytes 1966088 | tf_op jit(solution)/shard_map/ppermute | solution.py:285
  120.1 4.2 %chunk.5 = (f32[256,640]{1,0:T(8,128)}, f32[256,640]{1,0:T(8,128)}) custom-call(bf16[832,5120]{1,0:T(8,128)(2,1)} %bitcast.8, bf16[256,832]{1,0:T(8,128)(2,1)} %get-tuple-element.27.half_a, bf16[256,832]{1,0:T(8,128)(2,1)} %get-tuple-element.28.half_b), custom_call_target="tpu_custom_call" | custom-call | flops 545259520 | bytes 2375680 | tf_op jit(solution)/shard_map/chunk/pallas_call | solution.py:213
  125.2 2.9 %finish.2 = (f32[640,512]{1,0:T(8,128)}, f32[8,128]{1,0:T(8,128)}) custom-call(f32[256,640]{1,0:T(8,128)} %get-tuple-element.40.refs_0_, f32[256,640]{1,0:T(8,128)} %copy-done.1, f32[256,640]{1,0:T(8,128)} %maximum_select_fusion.refs_2_, f32[256,640]{1,0:T(8,128)} %collective-permute-done.19.refs_3_), custom_call_target="tpu_custom_call" | custom-call | tf_op jit(solution)/shard_map/finish/pallas_call | solution.py:260
  128.1 2.0 %pad_maximum_fusion.refs_3_ = f32[256,640]{1,0:T(8,128)} fusion(f32[128,640]{1,0:T(8,128)} %collective-permute-done.13, f32[128,640]{1,0:T(8,128)} %collective-permute-done.11), kind=kLoop, calls=%fused_computation | loop fusion | flops 163840 | bytes 1310720 | tf_op jit(solution)/shard_map/concatenate | solution.py:331
  131.0 2.9 %finish.3 = (f32[640,512]{1,0:T(8,128)}, f32[8,128]{1,0:T(8,128)}) custom-call(f32[256,640]{1,0:T(8,128)} %get-tuple-element.29.refs_0_, f32[256,640]{1,0:T(8,128)} %copy-done.6, f32[256,640]{1,0:T(8,128)} %collective-permute-done.5.refs_2_, f32[256,640]{1,0:T(8,128)} %pad_maximum_fusion.refs_3_, ...), custom_call_target="tpu_custom_call", output_to_operand_aliasing={{0}: (4, {})} | custom-call | tf_op jit(solution)/shard_map/finish/pallas_call | solution.py:260
  135.4 2.3 %collective-permute-done.20 = f32[8,128]{1,0:T(8,128)S(1)} collective-permute-done((f32[8,128]{1,0:T(8,128)}, f32[8,128]{1,0:T(8,128)S(1)}, u32[]{:S(2)}, u32[]{:S(2)}) %collective-permute-start.20) | collective-permute-done | bytes 4128 | tf_op jit(solution)/shard_map/ppermute | solution.py:334
  138.4 4.6 %collective-permute-start.21 = (f32[8,128]{1,0:T(8,128)S(1)}, f32[8,128]{1,0:T(8,128)S(1)}, u32[]{:S(2)}, u32[]{:S(2)}) collective-permute-start(f32[8,128]{1,0:T(8,128)S(1)} %max.9), channel_id=1, source_target_pairs={{0,4},{2,6},{4,0},{6,2},{8,12},{10,14},{12,8},{14,10},{1,5},{3,7},... | collective-permute-start | bytes 12296 | tf_op jit(solution)/shard_map/ppermute | solution.py:334
  143.0 1.6 %collective-permute-done.21 = f32[8,128]{1,0:T(8,128)S(1)} collective-permute-done((f32[8,128]{1,0:T(8,128)S(1)}, f32[8,128]{1,0:T(8,128)S(1)}, u32[]{:S(2)}, u32[]{:S(2)}) %collective-permute-start.21) | collective-permute-done | bytes 4128 | tf_op jit(solution)/shard_map/ppermute | solution.py:334
  144.6 3.2 %collective-permute-start.22 = (f32[8,128]{1,0:T(8,128)S(1)}, f32[8,128]{1,0:T(8,128)S(1)}, u32[]{:S(2)}, u32[]{:S(2)}) collective-permute-start(f32[8,128]{1,0:T(8,128)S(1)} %max.10), channel_id=1, source_target_pairs={{0,8},{2,10},{4,12},{6,14},{8,0},{10,2},{12,4},{14,6},{1,9},{3,11}... | collective-permute-start | bytes 12296 | tf_op jit(solution)/shard_map/ppermute | solution.py:334
  147.8 1.6 %collective-permute-done.22 = f32[8,128]{1,0:T(8,128)S(1)} collective-permute-done((f32[8,128]{1,0:T(8,128)S(1)}, f32[8,128]{1,0:T(8,128)S(1)}, u32[]{:S(2)}, u32[]{:S(2)}) %collective-permute-start.22) | collective-permute-done | bytes 4128 | tf_op jit(solution)/shard_map/ppermute | solution.py:334
  (56 shorter events, 23.8 us)
Async XLA Ops:
  6.8 18.8 %collective-permute-start.7 = (f32[256,640]{1,0:T(8,128)}, f32[256,640]{1,0:T(8,128)S(1)}, u32[]{:S(2)}, u32[]{:S(2)}) collective-permute-start(f32[256,640]{1,0:T(8,128)} %get-tuple-element.39), channel_id=1, source_target_pairs={{0,2},{2,0},{4,6},{6,4},{8,10},{10,8},{12,14},{14,12},{1,3},{3,1},... | collective-permute-start | bytes 1966088 | tf_op jit(solution)/shard_map/ppermute | solution.py:282
  14.3 25.4 %collective-permute-start.2 = (f32[256,640]{1,0:T(8,128)}, f32[256,640]{1,0:T(8,128)S(1)}, u32[]{:S(2)}, u32[]{:S(2)}) collective-permute-start(f32[256,640]{1,0:T(8,128)} %get-tuple-element.34), channel_id=1, source_target_pairs={{0,2},{2,0},{4,6},{6,4},{8,10},{10,8},{12,14},{14,12},{1,3},{3,1},... | collective-permute-start | bytes 1966088 | tf_op jit(solution)/shard_map/ppermute | solution.py:282
  19.5 20.2 %copy-start.8 = (f32[256,640]{1,0:T(8,128)S(1)}, f32[256,640]{1,0:T(8,128)}, u32[]{:S(2)}) copy-start(f32[256,640]{1,0:T(8,128)} %get-tuple-element.33) | copy-start | bytes 1966084
  26.8 19.4 %collective-permute-start.8 = (f32[256,640]{1,0:T(8,128)S(1)}, f32[256,640]{1,0:T(8,128)S(1)}, u32[]{:S(2)}, u32[]{:S(2)}) collective-permute-start(f32[256,640]{1,0:T(8,128)S(1)} %add.55), channel_id=1, source_target_pairs={{0,4},{2,6},{12,8},{14,10},{1,5},{3,7},{13,9},{15,11},{16,20},{18,... | collective-permute-start | bytes 1966088 | tf_op jit(solution)/shard_map/ppermute | solution.py:288
  30.9 22.9 %collective-permute-start.17 = (f32[256,640]{1,0:T(8,128)}, f32[256,640]{1,0:T(8,128)S(1)}, u32[]{:S(2)}, u32[]{:S(2)}) collective-permute-start(f32[256,640]{1,0:T(8,128)} %get-tuple-element.44), channel_id=1, source_target_pairs={{0,2},{2,0},{4,6},{6,4},{8,10},{10,8},{12,14},{14,12},{1,3},{3,1},... | collective-permute-start | bytes 1966088 | tf_op jit(solution)/shard_map/ppermute | solution.py:282
  39.7 19.2 %collective-permute-start.3 = (f32[256,640]{1,0:T(8,128)S(1)}, f32[256,640]{1,0:T(8,128)}, u32[]{:S(2)}, u32[]{:S(2)}) collective-permute-start(f32[256,640]{1,0:T(8,128)S(1)} %add.51), channel_id=1, source_target_pairs={{0,4},{2,6},{12,8},{14,10},{1,5},{3,7},{13,9},{15,11},{16,20},{18,... | collective-permute-start | bytes 1966088 | tf_op jit(solution)/shard_map/ppermute | solution.py:288
  44.6 28.5 %collective-permute-start.14 = (f32[256,640]{1,0:T(8,128)}, f32[256,640]{1,0:T(8,128)}, u32[]{:S(2)}, u32[]{:S(2)}) collective-permute-start(f32[256,640]{1,0:T(8,128)} %get-tuple-element.42), channel_id=1, source_target_pairs={{0,4},{2,6},{4,0},{6,2},{8,12},{10,14},{12,8},{14,10},{1,5},{3,7},... | collective-permute-start | bytes 1966088 | tf_op jit(solution)/shard_map/ppermute | solution.py:285
  44.6 36.2 %collective-permute-start.6 = (f32[256,640]{1,0:T(8,128)}, f32[256,640]{1,0:T(8,128)S(1)}, u32[]{:S(2)}, u32[]{:S(2)}) collective-permute-start(f32[256,640]{1,0:T(8,128)} %get-tuple-element.36), channel_id=1, source_target_pairs={{0,2},{2,0},{4,6},{6,4},{8,10},{10,8},{12,14},{14,12},{1,3},{3,1},... | collective-permute-start | bytes 1966088 | tf_op jit(solution)/shard_map/ppermute | solution.py:282
  46.2 41.1 %collective-permute-start.9 = (f32[256,640]{1,0:T(8,128)S(1)}, f32[256,640]{1,0:T(8,128)}, u32[]{:S(2)}, u32[]{:S(2)}) collective-permute-start(f32[256,640]{1,0:T(8,128)S(1)} %add.56), channel_id=1, source_target_pairs={{4,8},{6,10},{8,4},{10,6},{5,9},{7,11},{9,5},{11,7},{20,24},{22,26... | collective-permute-start | bytes 1966088 | tf_op jit(solution)/shard_map/ppermute | solution.py:291
  53.7 2.1 %copy-start.7 = (f32[256,640]{1,0:T(8,128)}, f32[256,640]{1,0:T(8,128)S(1)}, u32[]{:S(2)}) copy-start(f32[256,640]{1,0:T(8,128)S(1)} %collective-permute-done.17) | copy-start | bytes 1966084
  53.7 36.5 %collective-permute-start.1 = (f32[256,640]{1,0:T(8,128)}, f32[256,640]{1,0:T(8,128)S(1)}, u32[]{:S(2)}, u32[]{:S(2)}) collective-permute-start(f32[256,640]{1,0:T(8,128)} %get-tuple-element.32), channel_id=1, source_target_pairs={{0,2},{2,0},{4,6},{6,4},{8,10},{10,8},{12,14},{14,12},{1,3},{3,1},... | collective-permute-start | bytes 1966088 | tf_op jit(solution)/shard_map/ppermute | solution.py:282
  58.9 31.3 %collective-permute-start.18 = (f32[256,640]{1,0:T(8,128)S(1)}, f32[256,640]{1,0:T(8,128)}, u32[]{:S(2)}, u32[]{:S(2)}) collective-permute-start(f32[256,640]{1,0:T(8,128)S(1)} %add.63), channel_id=1, source_target_pairs={{0,4},{2,6},{12,8},{14,10},{1,5},{3,7},{13,9},{15,11},{16,20},{18,... | collective-permute-start | bytes 1966088 | tf_op jit(solution)/shard_map/ppermute | solution.py:288
  73.1 21.2 %collective-permute-start.4 = (f32[256,640]{1,0:T(8,128)}, f32[256,640]{1,0:T(8,128)}, u32[]{:S(2)}, u32[]{:S(2)}) collective-permute-start(f32[256,640]{1,0:T(8,128)} %add.52), channel_id=1, source_target_pairs={{4,8},{6,10},{8,4},{10,6},{5,9},{7,11},{9,5},{11,7},{20,24},{22,26... | collective-permute-start | bytes 1966088 | tf_op jit(solution)/shard_map/ppermute | solution.py:291
  79.4 1.5 copy-start.5
  79.4 9.5 %copy-start = (f32[256,640]{1,0:T(8,128)S(1)}, f32[256,640]{1,0:T(8,128)}, u32[]{:S(2)}) copy-start(f32[256,640]{1,0:T(8,128)} %get-tuple-element.35) | copy-start | bytes 1966084
  80.9 36.2 %collective-permute-start.16 = (f32[256,640]{1,0:T(8,128)S(1)}, f32[256,640]{1,0:T(8,128)S(1)}, u32[]{:S(2)}, u32[]{:S(2)}) collective-permute-start(f32[256,640]{1,0:T(8,128)S(1)} %copy-done.5), channel_id=1, source_target_pairs={{0,4},{2,6},{12,8},{14,10},{1,5},{3,7},{13,9},{15,11},{16,20},{18,... | collective-permute-start | bytes 1966088 | tf_op jit(solution)/shard_map/ppermute | solution.py:288
  87.4 31.2 %collective-permute-start.15 = (f32[256,640]{1,0:T(8,128)S(1)}, f32[256,640]{1,0:T(8,128)S(1)}, u32[]{:S(2)}, u32[]{:S(2)}) collective-permute-start(f32[256,640]{1,0:T(8,128)S(1)} %add.62), channel_id=1, source_target_pairs={{0,2},{2,0},{4,6},{6,4},{8,10},{10,8},{12,14},{14,12},{1,3},{3,1},... | collective-permute-start | bytes 1966088 | tf_op jit(solution)/shard_map/ppermute | solution.py:282
  90.2 5.6 %copy-start.2 = (f32[256,640]{1,0:T(8,128)S(1)}, f32[256,640]{1,0:T(8,128)}, u32[]{:S(2)}) copy-start(f32[256,640]{1,0:T(8,128)} %get-tuple-element.31) | copy-start | bytes 1966084
  90.2 19.3 %collective-permute-start.10 = (f32[128,640]{1,0:T(8,128)S(1)}, f32[128,640]{1,0:T(8,128)S(1)}, u32[]{:S(2)}, u32[]{:S(2)}) collective-permute-start(f32[128,640]{1,0:T(8,128)S(1)} %get-tuple-element.49), channel_id=1, source_target_pairs={{0,4},{2,6},{4,0},{6,2},{8,12},{10,14},{12,8},{14,10},{1,5},{3,7},... | collective-permute-start | bytes 983048 | tf_op jit(solution)/shard_map/ppermute | solution.py:285
  90.3 23.5 %collective-permute-start.12 = (f32[128,640]{1,0:T(8,128)S(1)}, f32[128,640]{1,0:T(8,128)S(1)}, u32[]{:S(2)}, u32[]{:S(2)}) collective-permute-start(f32[128,640]{1,0:T(8,128)S(1)} %get-tuple-element.50), channel_id=1, source_target_pairs={{0,4},{2,6},{4,0},{6,2},{8,12},{10,14},{12,8},{14,10},{1,5},{3,7},... | collective-permute-start | bytes 983048 | tf_op jit(solution)/shard_map/ppermute | solution.py:285
  94.3 30.9 %collective-permute-start.19 = (f32[256,640]{1,0:T(8,128)}, f32[256,640]{1,0:T(8,128)}, u32[]{:S(2)}, u32[]{:S(2)}) collective-permute-start(f32[256,640]{1,0:T(8,128)} %add.64), channel_id=1, source_target_pairs={{4,8},{6,10},{8,4},{10,6},{5,9},{7,11},{9,5},{11,7},{20,24},{22,26... | collective-permute-start | bytes 1966088 | tf_op jit(solution)/shard_map/ppermute | solution.py:291
  109.5 20.6 %collective-permute-start = (f32[256,640]{1,0:T(8,128)}, f32[256,640]{1,0:T(8,128)S(1)}, u32[]{:S(2)}, u32[]{:S(2)}) collective-permute-start(f32[256,640]{1,0:T(8,128)} %get-tuple-element.30), channel_id=1, source_target_pairs={{0,2},{2,0},{4,6},{6,4},{8,10},{10,8},{12,14},{14,12},{1,3},{3,1},... | collective-permute-start | bytes 1966088 | tf_op jit(solution)/shard_map/ppermute | solution.py:282
  113.7 16.4 %collective-permute-start.5 = (f32[256,640]{1,0:T(8,128)S(1)}, f32[256,640]{1,0:T(8,128)}, u32[]{:S(2)}, u32[]{:S(2)}) collective-permute-start(f32[256,640]{1,0:T(8,128)S(1)} %add_add_fusion), channel_id=1, source_target_pairs={{0,4},{2,6},{4,0},{6,2},{8,12},{10,14},{12,8},{14,10},{1,5},{3,7},... | collective-permute-start | bytes 1966088 | tf_op jit(solution)/shard_map/ppermute | solution.py:285
  117.1 1.4 copy-start.3
  117.1 11.0 %collective-permute-start.11 = (f32[128,640]{1,0:T(8,128)}, f32[128,640]{1,0:T(8,128)}, u32[]{:S(2)}, u32[]{:S(2)}) collective-permute-start(f32[128,640]{1,0:T(8,128)} %get-tuple-element.51), channel_id=1, source_target_pairs={{4,8},{6,10},{8,4},{10,6},{5,9},{7,11},{9,5},{11,7},{20,24},{22,26... | collective-permute-start | bytes 983048 | tf_op jit(solution)/shard_map/ppermute | solution.py:291
  118.5 5.7 %copy-start.1 = (f32[256,640]{1,0:T(8,128)}, f32[256,640]{1,0:T(8,128)S(1)}, u32[]{:S(2)}) copy-start(f32[256,640]{1,0:T(8,128)S(1)} %collective-permute-done.15.refs_1_) | copy-start | bytes 1966084
  118.5 5.7 %copy-start.4 = (f32[256,640]{1,0:T(8,128)S(1)}, f32[256,640]{1,0:T(8,128)}, u32[]{:S(2)}) copy-start(f32[256,640]{1,0:T(8,128)} %copy-done.3) | copy-start | bytes 1966084
  118.5 9.6 %collective-permute-start.13 = (f32[128,640]{1,0:T(8,128)S(1)}, f32[128,640]{1,0:T(8,128)}, u32[]{:S(2)}, u32[]{:S(2)}) collective-permute-start(f32[128,640]{1,0:T(8,128)S(1)} %get-tuple-element.52), channel_id=1, source_target_pairs={{4,8},{6,10},{8,4},{10,6},{5,9},{7,11},{9,5},{11,7},{20,24},{22,26... | collective-permute-start | bytes 983048 | tf_op jit(solution)/shard_map/ppermute | solution.py:291
  130.1 0.9 copy-start.6
  133.9 3.8 %collective-permute-start.20 = (f32[8,128]{1,0:T(8,128)}, f32[8,128]{1,0:T(8,128)S(1)}, u32[]{:S(2)}, u32[]{:S(2)}) collective-permute-start(f32[8,128]{1,0:T(8,128)} %get-tuple-element.48), channel_id=1, source_target_pairs={{0,2},{2,0},{4,6},{6,4},{8,10},{10,8},{12,14},{14,12},{1,3},{3,1},... | collective-permute-start | bytes 12296 | tf_op jit(solution)/shard_map/ppermute | solution.py:334
  138.4 6.2 %collective-permute-start.21 = (f32[8,128]{1,0:T(8,128)S(1)}, f32[8,128]{1,0:T(8,128)S(1)}, u32[]{:S(2)}, u32[]{:S(2)}) collective-permute-start(f32[8,128]{1,0:T(8,128)S(1)} %max.9), channel_id=1, source_target_pairs={{0,4},{2,6},{4,0},{6,2},{8,12},{10,14},{12,8},{14,10},{1,5},{3,7},... | collective-permute-start | bytes 12296 | tf_op jit(solution)/shard_map/ppermute | solution.py:334
  144.6 4.8 %collective-permute-start.22 = (f32[8,128]{1,0:T(8,128)S(1)}, f32[8,128]{1,0:T(8,128)S(1)}, u32[]{:S(2)}, u32[]{:S(2)}) collective-permute-start(f32[8,128]{1,0:T(8,128)S(1)} %max.10), channel_id=1, source_target_pairs={{0,8},{2,10},{4,12},{6,14},{8,0},{10,2},{12,4},{14,6},{1,9},{3,11}... | collective-permute-start | bytes 12296 | tf_op jit(solution)/shard_map/ppermute | solution.py:334

commit v3 on v2

v3 whole, which is shorter than its diff:
```python
import functools
import math

import jax
import jax.numpy as jnp
from jax import lax
from jax.experimental import pallas as pl
from jax.experimental.pallas import tpu as pltpu
from jax.sharding import PartitionSpec as P

HD = 128
GROUP = 8
BUCKET = 128
BATCH = 16
VMEM_BYTES = 20 * 1024 * 1024
HBM = pl.BlockSpec(memory_space=pltpu.HBM)
PARAMS = pltpu.CompilerParams(vmem_limit_bytes=VMEM_BYTES)
MIDDLE = pltpu.CompilerParams(vmem_limit_bytes=46 * 1024 * 1024)
WIDE = pltpu.CompilerParams(vmem_limit_bytes=60 * 1024 * 1024)
SMALL = pl.CostEstimate(flops=1000, bytes_accessed=1000, transcendentals=0)
FAR3, FAR2, PAIR, OWN = range(4)
CROSS, SAME = True, False


def advantage_rows(rewards):
    advantages = []
    for base in range(0, rewards.shape[0], GROUP):
        centre = rewards[base]
        for i in range(1, GROUP):
            centre = centre + rewards[base + i]
        centre = centre * (1.0 / GROUP)
        spread = (rewards[base] - centre) * (rewards[base] - centre)
        for i in range(1, GROUP):
            spread = spread + (rewards[base + i] - centre) * (rewards[base + i] - centre)
        spread = jnp.sqrt(jnp.full((1, HD), spread * (1.0 / GROUP), jnp.float32))
        spread = jnp.maximum(spread, 1.0)
        for r in range(base, base + GROUP):
            advantages.append(jnp.full((1, HD), rewards[r] - centre, jnp.float32) / spread)
    return advantages


def attend_heads(lengths, rewards, q, ck, nk, cv=None, nv=None, out=None, cot=None, rows=None):
    rollouts, steps, width = q.shape
    key_heads = ck.shape[2] // HD
    heads = width // HD // key_heads
    ctx = ck.shape[1]
    slots = ctx + steps
    padded = -(-slots // HD) * HD
    pad = padded - slots
    scaling = 1.0 / math.sqrt(HD)

    def by_head(ref, r, g):
        return jnp.concatenate(
            [
                ref[r, :, (g * heads + j) * HD : (g * heads + j + 1) * HD].astype(jnp.float32)
                for j in range(heads)
            ],
            axis=0,
        )

    def joined(past, fresh, r, g):
        lanes = slice(g * HD, (g + 1) * HD)
        fresh = jnp.concatenate(
            [fresh[r, :, lanes].astype(jnp.float32), jnp.zeros((pad, HD), jnp.float32)], axis=0
        ).astype(jnp.bfloat16)
        return jnp.concatenate([past[r, :, lanes], fresh], axis=0)

    shape = (heads * steps, padded)
    column = lax.broadcasted_iota(jnp.int32, shape, 1)
    step = lax.broadcasted_iota(jnp.int32, shape, 0) % steps
    fresh_live = (column >= ctx) & (column - ctx <= step)
    advantages = advantage_rows(rewards) if rows is not None else None
    lives = []
    for r in range(rollouts):
        lives.append((column < lengths[r]) | fresh_live)
    units = [(r, g) for g in range(key_heads) for r in range(rollouts)]
    for start in range(0, len(units), BATCH):
        batch = units[start : start + BATCH]
        scores = [
            lax.dot_general(
                by_head(q, r, g).astype(jnp.bfloat16),
                joined(ck, nk, r, g),
                (((1,), (1,)), ((), ())),
                preferred_element_type=jnp.float32,
            )
            for r, g in batch
        ]
        scores = [
            jnp.where(lives[r], x * scaling, -1e30) for (r, g), x in zip(batch, scores)
        ]
        highest = [jnp.max(x, axis=1, keepdims=True) for x in scores]
        lift = [jnp.exp(x - top) for x, top in zip(scores, highest)]
        totals = [jnp.sum(x, axis=1, keepdims=True) for x in lift]
        weights = [(x / total).astype(jnp.bfloat16) for x, total in zip(lift, totals)]
        if out is not None:
            results = [
                jnp.dot(w, joined(cv, nv, r, g), preferred_element_type=jnp.float32)
                for (r, g), w in zip(batch, weights)
            ]
            for (r, g), result in zip(batch, results):
                for j in range(heads):
                    out[r, :, (g * heads + j) * HD : (g * heads + j + 1) * HD] = result[
                        j * steps : (j + 1) * steps
                    ].astype(jnp.bfloat16)
        if rows is not None:
            value_cots = [
                lax.dot_general(
                    w,
                    (by_head(cot, r, g) * advantages[r]).astype(jnp.bfloat16),
                    (((0,), (0,)), ((), ())),
                    preferred_element_type=jnp.float32,
                )
                for (r, g), w in zip(batch, weights)
            ]
            for (r, g), value_cot in zip(batch, value_cots):
                rows[r * slots : (r + 1) * slots, g * HD : (g + 1) * HD] = value_cot[:slots]


def block_of(kind):
    plane_kind, cross = kind
    rank = lax.axis_index("dp")
    plane = rank // 2
    row = rank - plane * 2
    low = plane < 2
    if plane_kind == FAR3:
        target = jnp.where(low, 3, 0)
    elif plane_kind == FAR2:
        target = jnp.where(low, 2, 1)
    elif plane_kind == PAIR:
        target = plane + 1 - 2 * (plane - (plane // 2) * 2)
    else:
        target = plane
    return target * 2 + (1 - row if cross else row)


def start_features(features, kinds, buffers, sems):
    copies = []
    for i, kind in enumerate(kinds):
        width = buffers.shape[2]
        first = pl.multiple_of(block_of(kind) * width, HD)
        copy = pltpu.make_async_copy(
            features.at[:, pl.ds(first, width)], buffers.at[i], sems.at[i]
        )
        copy.start()
        copies.append(copy)
    return copies


def copy_all(sources, buffers, sems):
    copies = []
    for i, (source, buffer) in enumerate(zip(sources, buffers)):
        copy = pltpu.make_async_copy(source, buffer, sems.at[i])
        copy.start()
        copies.append(copy)
    return copies


def lanes_of(ref, half):
    size = ref.shape[-1] // 2
    return ref.at[:, :, pl.ds(half * size, size)]


def begin_kernel(half, jobs, *refs):
    ins, refs = refs[:6], refs[6:]
    features, refs = refs[0], refs[1:]
    cots = []
    if half:
        cots.append(refs[0])
        refs = refs[1:]
    cot_half, refs = refs[0], refs[1:]
    outs, refs = refs[: len(jobs)], refs[len(jobs) :]
    bufs, (rows, blocks, sems, block_sems) = refs[:6], refs[6:]
    sources = list(ins[:2]) + [lanes_of(ref, half) for ref in ins[2:]]
    copies = copy_all(sources, bufs, sems)
    kinds = [kind for kind, _ in jobs]
    block_copies = start_features(features, kinds, blocks, block_sems)
    for copy in copies:
        copy.wait()
    lengths, rewards, q, ck, nk, cot = bufs
    attend_heads(lengths, rewards, q, ck, nk, cot=cot, rows=rows)
    cot_half[...] = rows[...].T.astype(jnp.bfloat16)
    cots.append(cot_half)
    for i, (_, h) in enumerate(jobs):
        block_copies[i].wait()
        outs[i][...] = jnp.dot(cots[h][...], blocks[i], preferred_element_type=jnp.float32)


def begin(half, jobs, arrays, features, cots, width):
    lengths, rewards, queries, ck, _, _ = arrays
    depth = features.shape[0]
    columns = ck.shape[2] // 2
    shapes = [jax.ShapeDtypeStruct((columns, depth), jnp.bfloat16)]
    shapes += [jax.ShapeDtypeStruct((columns, width), jnp.float32)] * len(jobs)
    vmem = pl.BlockSpec(memory_space=pltpu.VMEM)
    return pl.pallas_call(
        functools.partial(begin_kernel, half, jobs),
        in_specs=[HBM] * 7 + [vmem] * len(cots),
        out_specs=[vmem] * len(shapes),
        out_shape=shapes,
        scratch_shapes=[pltpu.SMEM(x.shape, x.dtype) for x in arrays[:2]]
        + [pltpu.VMEM(x.shape[:2] + (x.shape[2] // 2,), x.dtype) for x in arrays[2:]]
        + [
            pltpu.VMEM((depth, columns), jnp.float32),
            pltpu.VMEM((max(len(jobs), 1), depth, width), jnp.bfloat16),
            pltpu.SemaphoreType.DMA((6,)),
            pltpu.SemaphoreType.DMA((max(len(jobs), 1),)),
        ],
        compiler_params=WIDE,
        cost_estimate=SMALL,
        name="value_cot",
    )(*arrays, features, *cots)


def attended_kernel(*refs):
    ins, out, bufs, sems = refs[:6], refs[6], refs[7:13], refs[13]
    for copy in copy_all(ins, bufs, sems):
        copy.wait()
    lengths, queries, ck, nk, cv, nv = bufs
    attend_heads(lengths, None, queries, ck, nk, cv=cv, nv=nv, out=out)


def attend(*arrays):
    queries = arrays[1]
    return pl.pallas_call(
        attended_kernel,
        in_specs=[HBM] * 6,
        out_specs=pl.BlockSpec(memory_space=pltpu.VMEM),
        out_shape=jax.ShapeDtypeStruct(queries.shape, jnp.bfloat16),
        scratch_shapes=[pltpu.SMEM(arrays[0].shape, arrays[0].dtype)]
        + [pltpu.VMEM(x.shape, x.dtype) for x in arrays[1:]]
        + [pltpu.SemaphoreType.DMA((6,))],
        compiler_params=MIDDLE,
        cost_estimate=SMALL,
        name="attend",
    )(*arrays)


def chunk_kernel(jobs, features, half_a, half_b, *refs):
    kinds = [kind for kind, _ in jobs]
    count = sum(len(which) for _, which in jobs)
    outs, (blocks, sems) = refs[:count], refs[count:]
    copies = start_features(features, kinds, blocks, sems)
    cots = (half_a, half_b)
    place = 0
    for i, (_, which) in enumerate(jobs):
        copies[i].wait()
        for h in which:
            outs[place][...] = jnp.dot(
                cots[h][...], blocks[i], preferred_element_type=jnp.float32
            )
            place += 1


def chunks(jobs, features, halves, width):
    depth = features.shape[0]
    half = halves[0].shape[0]
    count = sum(len(which) for _, which in jobs)
    vmem = pl.BlockSpec(memory_space=pltpu.VMEM)
    return pl.pallas_call(
        functools.partial(chunk_kernel, jobs),
        in_specs=[HBM, vmem, vmem],
        out_specs=[vmem] * count,
        out_shape=[jax.ShapeDtypeStruct((half, width), jnp.float32)] * count,
        scratch_shapes=[
            pltpu.VMEM((len(jobs), depth, width), jnp.bfloat16),
            pltpu.SemaphoreType.DMA((len(jobs),)),
        ],
        compiler_params=MIDDLE,
        cost_estimate=SMALL,
        name="chunk",
    )(features, *halves)


def add_kernel(half, edge_first, *refs):
    count = len(refs) - 3
    total, peaks = refs[-2:]
    size = total.shape[0]
    cut = size // 2
    for b in range(2):
        rows = slice(b * cut, (b + 1) * cut)
        part = None
        for ref in refs[:2]:
            part = ref[rows] if part is None else part + ref[rows]
        if edge_first:
            rank = lax.axis_index("dp")
            edge = (rank < 2) | (rank >= 6)
            part = part + jnp.where(edge, refs[2 + b][...], refs[4][rows])
            part = part + refs[5][rows]
        else:
            part = part + refs[2][rows] + refs[3 + b][...]
        total[rows] = part
    buckets = size // BUCKET
    lane = lax.broadcasted_iota(jnp.int32, peaks.shape, 1)
    peak = refs[count][...]
    for b in range(buckets):
        top = jnp.abs(total[b * BUCKET : (b + 1) * BUCKET])
        top = jnp.max(jnp.max(top, axis=0, keepdims=True), axis=1, keepdims=True)
        peak = jnp.where(lane == half * buckets + b, top, peak)
    peaks[...] = peak


def add_parts(half, edge_first, parts, peaks):
    vmem = pl.BlockSpec(memory_space=pltpu.VMEM)
    return pl.pallas_call(
        functools.partial(add_kernel, half, edge_first),
        in_specs=[vmem] * (len(parts) + 1),
        out_specs=[vmem] * 2,
        out_shape=[
            jax.ShapeDtypeStruct(parts[0].shape, jnp.float32),
            jax.ShapeDtypeStruct(peaks.shape, jnp.float32),
        ],
        compiler_params=PARAMS,
        cost_estimate=SMALL,
        name="add_parts",
    )(*parts, peaks)


def place_kernel(total, *refs):
    refs[-1][...] = total[...].T


def place(half, total, grad, columns):
    size, width = total.shape
    in_specs = [pl.BlockSpec(memory_space=pltpu.VMEM)]
    args = [total]
    aliases = {}
    if grad is not None:
        in_specs.append(pl.BlockSpec(memory_space=pl.ANY))
        args.append(grad)
        aliases = {1: 0}
    return pl.pallas_call(
        place_kernel,
        grid=(1,),
        in_specs=in_specs,
        out_specs=pl.BlockSpec((width, size), lambda i: (0, half)),
        out_shape=jax.ShapeDtypeStruct((width, columns), jnp.float32),
        input_output_aliases=aliases,
        compiler_params=PARAMS,
        cost_estimate=SMALL,
        name="place",
    )(*args)


def reduce_on_grid(features, halves, firsts, attended, dp):
    width = features.shape[1] // dp
    columns = 2 * halves[0].shape[0]
    rank = lax.axis_index("dp")
    edge = (rank < 2) | (rank >= 6)

    def across(x):
        return lax.ppermute(x, "dp", [(r, r ^ 1) for r in range(dp)])

    def pair(x):
        return lax.ppermute(x, "dp", [(r, r ^ 2) for r in range(dp)])

    def outward(x):
        return lax.ppermute(x, "dp", [(r, r ^ 2) for r in (0, 1, 6, 7)])

    def middle(x):
        return lax.ppermute(x, "dp", [(r, r ^ 6) for r in (2, 3, 4, 5)])

    def together(*arrays):
        return lax.optimization_barrier(arrays)

    def make(*jobs):
        return chunks(jobs, features, halves, width)

    a, b = 0, 1
    cross3a, crosspa, cross3b, ownpa = firsts
    (own3a, own3b, cross2a, cross2b, own2a, own2b, crosspb, crossoa, crossob, ownpb, ownoa, ownob) = (
        make(
            ((FAR3, SAME), (a, b)),
            ((FAR2, CROSS), (a, b)),
            ((FAR2, SAME), (a, b)),
            ((PAIR, CROSS), (b,)),
            ((OWN, CROSS), (a, b)),
            ((PAIR, SAME), (b,)),
            ((OWN, SAME), (a, b)),
        )
    )

    y0, e0 = together(across(cross3a), pair(crosspa))
    y1, e1 = together(across(cross3b), outward(ownpa))
    y2, e2, attended = together(across(cross2a), outward(own3a + y0), attended)
    y3, e3 = together(across(cross2b), outward(own3b + y1))
    m3 = middle(own3a + y0 + e2)
    y4, e4 = together(across(crosspb), outward(own2a + y2))
    m4 = middle(own3b + y1 + e3)
    y5 = across(crossoa + e0)
    cut = own2b.shape[0] // 2
    e5 = []
    for part in (slice(0, cut), slice(cut, None)):
        e5.append(
            pair(jnp.where(edge, own2b[part] + y3[part], ownpa[part] + m3[part]))
        )
    m5 = middle(own2a + y2 + e4)
    y6 = across(crossob)
    e6 = pair(ownpb + y4 + m4)
    m6 = []
    for i, part in enumerate((slice(0, cut), slice(cut, None))):
        (send,) = together(own2b[part] + y3[part] + e5[i])
        m6.append(middle(send))
    peaks = jnp.zeros((8, HD), jnp.float32)
    total, peaks = add_parts(a, True, [ownoa, y5, *e5, e1, m5], peaks)
    grad, peaks = together(place(a, total, None, columns), peaks)
    total, peaks = add_parts(b, False, [ownob, y6, e6, *m6], peaks)
    grad = place(b, total, grad, columns)
    for hop in (1, 2, 4):
        peaks = jnp.maximum(
            peaks, lax.ppermute(peaks, "dp", [(r, r ^ hop) for r in range(dp)])
        )
    return attended, grad, peaks[0, : columns // BUCKET]


def reduce_plain(features, halves):
    cots = jnp.concatenate(halves, axis=0)
    partial_grad = lax.dot_general(
        features, cots, (((0,), (1,)), ((), ())), preferred_element_type=jnp.float32
    )
    grad = lax.psum_scatter(partial_grad, "dp", scatter_dimension=0, tiled=True)
    peaks = jnp.max(jnp.abs(grad).reshape(-1, cots.shape[0] // BUCKET, BUCKET), axis=(0, 2))
    return grad, lax.pmax(peaks, "dp")


def per_device(
    dp,
    queries,
    cache_keys,
    cache_values,
    new_keys,
    new_values,
    features,
    cotangent,
    rewards,
    lengths,
):
    flat = features.reshape(-1, features.shape[2])
    arrays = (lengths, rewards, queries, cache_keys, new_keys, cotangent)
    on_grid = dp == 8
    width = features.shape[2] // 8 if on_grid else BUCKET
    jobs_a = (((FAR3, CROSS), 0), ((PAIR, CROSS), 0)) if on_grid else ()
    jobs_b = (((FAR3, CROSS), 1), ((PAIR, SAME), 0)) if on_grid else ()
    half_a, *firsts = begin(0, jobs_a, arrays, flat, [], width)
    half_b, *seconds = begin(1, jobs_b, arrays, flat, [half_a], width)
    attended = attend(lengths, queries, cache_keys, new_keys, cache_values, new_values)
    firsts += seconds
    if on_grid:
        attended, grad, peaks = reduce_on_grid(
            flat, (half_a, half_b), firsts, attended, dp
        )
    else:
        grad, peaks = reduce_plain(flat, (half_a, half_b))
    return attended, grad, peaks


def solution(mesh):
    split = P(("groups", "dp"), None, "tensor")
    rows = P(("groups", "dp"))
    in_specs = (
        split,
        split,
        split,
        split,
        split,
        P(("groups", "dp"), None, None),
        split,
        rows,
        rows,
    )
    out_specs = (split, P(("groups", "dp"), "tensor"), P(("groups", "tensor")))
    return jax.shard_map(
        functools.partial(per_device, mesh.shape["dp"]),
        mesh=mesh,
        in_specs=in_specs,
        out_specs=out_specs,
        check_vma=False,
    )
```

time: 151 us -> 126 us (0.83)
  Pallas kernels: 35.3 us -> 23.5 us
  waiting for transfers between devices: 44 us -> 37.1 us
  other arithmetic: 15 us -> 9.41 us
  local copies, waits for them, and re-layouts: 1.39 us -> 3.31 us
  starting transfers between devices: 53.4 us -> 51.5 us
    pallas_call x5 -> x1, Pallas kernels: 23.3 us -> 8.13 us  [chunks(): pl.pallas_call(functools.partial(chunk_kernel, jobs), in_specs=[HBM, vmem...]
    ppermute x4, waiting for transfers between devices: 22.1 us -> 7.74 us  [pair(): return lax.ppermute(x, 'dp', [(r, r ^ 2) for r in range(dp)])]
    ppermute x4, waiting for transfers between devices: 1.82 us -> 8.07 us  [outward(): return lax.ppermute(x, 'dp', [(r, r ^ 2) for r in (0, 1, 6, 7)])]
    ppermute x4, starting transfers between devices: 20.7 us -> 15.1 us  [outward(): return lax.ppermute(x, 'dp', [(r, r ^ 2) for r in (0, 1, 6, 7)])]
    ppermute x4, starting transfers between devices: 4.56 us -> 9.74 us  [pair(): return lax.ppermute(x, 'dp', [(r, r ^ 2) for r in range(dp)])]
    pallas_call x3 -> x7, Pallas kernels: 12 us -> 15.4 us  [the longest x2 9.91 us: begin(): pl.pallas_call(functools.partial(begin_kernel, half, jobs), in_specs=[HBM...]
    ppermute x5, starting transfers between devices: 7.45 us -> 5.1 us  [middle(): return lax.ppermute(x, 'dp', [(r, r ^ 6) for r in (2, 3, 4, 5)])]
    ppermute x3, starting transfers between devices: 9.31 us -> 11.6 us  [reduce_on_grid(): lax.ppermute(peaks, 'dp', [(r, r ^ hop) for r in range(dp)])]
  transfers between devices with their start and end apart: 23 -> 23, of which waited for: 10 -> 12; matrix products, arithmetic and copies ran while one was open for 10% -> 7% of each run, Pallas kernels for 17% -> 15%
where the time goes in v3:
time: 126 us
  starting transfers between devices  51.5 us (41%)
  waiting for transfers between devices  37.1 us (29%)
  Pallas kernels  23.5 us (19%)
  other arithmetic  9.41 us (7%)
  local copies, waits for them, and re-layouts  3.31 us (3%)
    ppermute x7, waiting for transfers between devices, across(): return lax.ppermute(x, 'dp', [(r, r ^ 1) for r in range(dp)])  16.8 us
    ppermute x4, starting transfers between devices, outward(): return lax.ppermute(x, 'dp', [(r, r ^ 2) for r in (0, 1, 6, 7)])  15.1 us
    ppermute x3, starting transfers between devices, reduce_on_grid(): lax.ppermute(peaks, 'dp', [(r, r ^ hop) for r in range(dp)])  11.6 us
    ppermute x7, starting transfers between devices, across(): return lax.ppermute(x, 'dp', [(r, r ^ 1) for r in range(dp)])  10 us
    pallas_call x2, Pallas kernels, begin(): pl.pallas_call(functools.partial(begin_kernel, half, jobs), in_specs=[HBM...  9.91 us
    ppermute x4, starting transfers between devices, pair(): return lax.ppermute(x, 'dp', [(r, r ^ 2) for r in range(dp)])  9.74 us
    pallas_call x1, Pallas kernels, chunks(): pl.pallas_call(functools.partial(chunk_kernel, jobs), in_specs=[HBM, vmem...  8.13 us
    ppermute x4, waiting for transfers between devices, outward(): return lax.ppermute(x, 'dp', [(r, r ^ 2) for r in (0, 1, 6, 7)])  8.07 us
  transfers between devices with their start and end apart: 23, of which 12 were waited for; matrix products, arithmetic and copies ran while one was open for 7% of the time, Pallas kernels for 15%

profile of v3, /device:TPU:0, one launch (start us, length us, event | category | flops | bytes accessed | tf_op | source)
XLA Modules:
  0.0 125.8 jit_solution(7613673933915595801)
XLA Ops:
  0.6 4.4 %value_cot.2 = (bf16[256,832]{1,0:T(8,128)(2,1)}, f32[256,640]{1,0:T(8,128)}, f32[256,640]{1,0:T(8,128)}) custom-call(s32[8]{0:T(128)} %refs_0_.5, f32[8]{0:T(128)} %refs_1_.4, bf16[8,8,4096]{2,1,0:T(8,128)(2,1)} %refs_1_.5, bf16[8,96,512]{2,1,0:T(8,128)(2,1)} %refs_2_.5, bf16[8,8,512]{2,1,0:T(8,128)(2,1)} %refs_3_.5, bf16[8,8,4096]{2,1,0:T(8,128)(2,1)} %refs_5_.4, ...), custom_call_target="tpu_custom_call" | custom-call | flops 1000 | bytes 1000 | tf_op jit(solution)/shard_map/value_cot/pallas_call | solution.py:195
  5.0 3.0 %collective-permute-start.1 = (f32[256,640]{1,0:T(8,128)}, f32[256,640]{1,0:T(8,128)}, u32[]{:S(2)}, u32[]{:S(2)}) collective-permute-start(f32[256,640]{1,0:T(8,128)} %get-tuple-element.42), channel_id=1, source_target_pairs={{0,2},{2,0},{4,6},{6,4},{8,10},{10,8},{12,14},{14,12},{1,3},{3,1},... | collective-permute-start | bytes 1966088 | tf_op jit(solution)/shard_map/ppermute | solution.py:351
  8.1 1.6 %collective-permute-start.2 = (f32[256,640]{1,0:T(8,128)}, f32[256,640]{1,0:T(8,128)}, u32[]{:S(2)}, u32[]{:S(2)}) collective-permute-start(f32[256,640]{1,0:T(8,128)} %get-tuple-element.43), channel_id=1, source_target_pairs={{0,4},{2,6},{4,0},{6,2},{8,12},{10,14},{12,8},{14,10},{1,5},{3,7},... | collective-permute-start | bytes 1966088 | tf_op jit(solution)/shard_map/ppermute | solution.py:354
  9.6 5.5 %value_cot.3 = (bf16[256,832]{1,0:T(8,128)(2,1)}, f32[256,640]{1,0:T(8,128)}, f32[256,640]{1,0:T(8,128)}) custom-call(s32[8]{0:T(128)} %refs_0_.5, f32[8]{0:T(128)} %refs_1_.4, bf16[8,8,4096]{2,1,0:T(8,128)(2,1)} %refs_1_.5, bf16[8,96,512]{2,1,0:T(8,128)(2,1)} %refs_2_.5, bf16[8,8,512]{2,1,0:T(8,128)(2,1)} %refs_3_.5, bf16[8,8,4096]{2,1,0:T(8,128)(2,1)} %refs_5_.4, ...), custom_call_target="tpu_custom_call" | custom-call | flops 1000 | bytes 1000 | tf_op jit(solution)/shard_map/value_cot/pallas_call | solution.py:195
  15.2 2.4 %collective-permute-start.8 = (f32[256,640]{1,0:T(8,128)}, f32[256,640]{1,0:T(8,128)S(1)}, u32[]{:S(2)}, u32[]{:S(2)}) collective-permute-start(f32[256,640]{1,0:T(8,128)} %get-tuple-element.55), channel_id=1, source_target_pairs={{0,4},{2,6},{12,8},{14,10},{1,5},{3,7},{13,9},{15,11},{16,20},{18,... | collective-permute-start | bytes 1966088 | tf_op jit(solution)/shard_map/ppermute | solution.py:357
  18.7 8.1 %chunk.1 = (f32[256,640]{1,0:T(8,128)S(1)}, f32[256,640]{1,0:T(8,128)S(1)}, f32[256,640]{1,0:T(8,128)S(1)}, f32[256,640]{1,0:T(8,128)S(1)}, f32[256,640]{1,0:T(8...) custom-call(bf16[832,5120]{1,0:T(8,128)(2,1)} %bitcast.5, ...), custom_call_target="tpu_custom_call" | custom-call | flops 1000 | bytes 1000 | tf_op jit(solution)/shard_map/chunk/pallas_call | solution.py:259
  27.7 1.9 %collective-permute-start = (f32[256,640]{1,0:T(8,128)S(1)}, f32[256,640]{1,0:T(8,128)S(1)}, u32[]{:S(2)}, u32[]{:S(2)}) collective-permute-start(f32[256,640]{1,0:T(8,128)S(1)} %get-tuple-element.40), channel_id=1, source_target_pairs={{0,2},{2,0},{4,6},{6,4},{8,10},{10,8},{12,14},{14,12},{1,3},{3,1},... | collective-permute-start | bytes 1966088 | tf_op jit(solution)/shard_map/ppermute | solution.py:351
  29.7 1.2 add.50
  31.0 1.5 %collective-permute-start.3 = (f32[256,640]{1,0:T(8,128)S(1)}, f32[256,640]{1,0:T(8,128)S(1)}, u32[]{:S(2)}, u32[]{:S(2)}) collective-permute-start(f32[256,640]{1,0:T(8,128)S(1)} %add.50), channel_id=1, source_target_pairs={{0,4},{2,6},{12,8},{14,10},{1,5},{3,7},{13,9},{15,11},{16,20},{18,... | collective-permute-start | bytes 1966088 | tf_op jit(solution)/shard_map/ppermute | solution.py:357
  32.6 6.6 %collective-permute-done.8.refs_4_ = f32[256,640]{1,0:T(8,128)S(1)} collective-permute-done((f32[256,640]{1,0:T(8,128)}, f32[256,640]{1,0:T(8,128)S(1)}, u32[]{:S(2)}, u32[]{:S(2)}) %collective-permute-start.8) | collective-permute-done | bytes 655392 | tf_op jit(solution)/shard_map/ppermute | solution.py:357
  39.2 4.3 %collective-permute-start.10 = (f32[256,640]{1,0:T(8,128)S(1)}, f32[256,640]{1,0:T(8,128)S(1)}, u32[]{:S(2)}, u32[]{:S(2)}) collective-permute-start(f32[256,640]{1,0:T(8,128)S(1)} %add.53), channel_id=1, source_target_pairs={{0,4},{2,6},{12,8},{14,10},{1,5},{3,7},{13,9},{15,11},{16,20},{18,... | collective-permute-start | bytes 1966088 | tf_op jit(solution)/shard_map/ppermute | solution.py:357
  43.6 2.8 %attend.1 = bf16[8,8,4096]{2,1,0:T(8,128)(2,1)} custom-call(s32[8]{0:T(128)S(1)} %copy-done.8, bf16[8,8,4096]{2,1,0:T(8,128)(2,1)S(1)} %copy-done.1, bf16[8,96,512]{2,1,0:T(8,128)(2,1)S(1)} %copy-done, bf16[8,8,512]{2,1,0:T(8,128)(2,1)S(1)} %copy-done.5, bf16[8,96,512]{2,1,0:T(8,128)(2,1)S(1)} %copy-done.3, bf16[8,8,512]{2,1,0:T(8,128)(2,1)S(1)} %copy-done.7), custom_call_target="tpu_custom_call" | custom-call | flops 1000 | bytes 1000 | tf_op jit(solution)/shard_map/attend/pallas_call | solution.py:224
  46.5 5.4 %collective-permute-done = f32[256,640]{1,0:T(8,128)S(1)} collective-permute-done((f32[256,640]{1,0:T(8,128)S(1)}, f32[256,640]{1,0:T(8,128)S(1)}, u32[]{:S(2)}, u32[]{:S(2)}) %collective-permute-start) | collective-permute-done | bytes 655392 | tf_op jit(solution)/shard_map/ppermute | solution.py:351
  54.0 1.5 %collective-permute-start.13 = (f32[256,640]{1,0:T(8,128)}, f32[256,640]{1,0:T(8,128)}, u32[]{:S(2)}, u32[]{:S(2)}) collective-permute-start(f32[256,640]{1,0:T(8,128)} %add.57), channel_id=1, source_target_pairs={{4,8},{6,10},{8,4},{10,6},{5,9},{7,11},{9,5},{11,7},{20,24},{22,26... | collective-permute-start | bytes 1966088 | tf_op jit(solution)/shard_map/ppermute | solution.py:360
  57.3 6.9 %collective-permute-start.6 = (f32[256,640]{1,0:T(8,128)}, f32[256,640]{1,0:T(8,128)}, u32[]{:S(2)}, u32[]{:S(2)}) collective-permute-start(f32[256,640]{1,0:T(8,128)} %add.51), channel_id=1, source_target_pairs={{0,4},{2,6},{12,8},{14,10},{1,5},{3,7},{13,9},{15,11},{16,20},{18,... | collective-permute-start | bytes 1966088 | tf_op jit(solution)/shard_map/ppermute | solution.py:357
  64.2 1.7 %collective-permute-done.9 = f32[256,640]{1,0:T(8,128)S(1)} collective-permute-done((f32[256,640]{1,0:T(8,128)S(1)}, f32[256,640]{1,0:T(8,128)S(1)}, u32[]{:S(2)}, u32[]{:S(2)}) %collective-permute-start.9) | collective-permute-done | bytes 655392 | tf_op jit(solution)/shard_map/ppermute | solution.py:351
  68.1 1.5 %collective-permute-start.11 = (f32[256,640]{1,0:T(8,128)}, f32[256,640]{1,0:T(8,128)}, u32[]{:S(2)}, u32[]{:S(2)}) collective-permute-start(f32[256,640]{1,0:T(8,128)} %add.54), channel_id=1, source_target_pairs={{4,8},{6,10},{8,4},{10,6},{5,9},{7,11},{9,5},{11,7},{20,24},{22,26... | collective-permute-start | bytes 1966088 | tf_op jit(solution)/shard_map/ppermute | solution.py:360
  69.6 1.3 add.63
  70.8 1.8 %collective-permute-start.18 = (f32[256,640]{1,0:T(8,128)S(1)}, f32[256,640]{1,0:T(8,128)S(1)}, u32[]{:S(2)}, u32[]{:S(2)}) collective-permute-start(f32[256,640]{1,0:T(8,128)S(1)} %add.63), channel_id=1, source_target_pairs={{0,2},{2,0},{4,6},{6,4},{8,10},{10,8},{12,14},{14,12},{1,3},{3,1},... | collective-permute-start | bytes 1966088 | tf_op jit(solution)/shard_map/ppermute | solution.py:351
  72.7 1.3 fusion
  74.0 3.6 %collective-permute-start.14 = (f32[128,640]{1,0:T(8,128)S(1)}, f32[128,640]{1,0:T(8,128)S(1)}, u32[]{:S(2)}, u32[]{:S(2)}) collective-permute-start(f32[128,640]{1,0:T(8,128)S(1)} %get-tuple-element.74), channel_id=1, source_target_pairs={{0,4},{2,6},{4,0},{6,2},{8,12},{10,14},{12,8},{14,10},{1,5},{3,7},... | collective-permute-start | bytes 983048 | tf_op jit(solution)/shard_map/ppermute | solution.py:354
  77.6 2.5 %collective-permute-done.5 = f32[256,640]{1,0:T(8,128)} collective-permute-done((f32[256,640]{1,0:T(8,128)}, f32[256,640]{1,0:T(8,128)}, u32[]{:S(2)}, u32[]{:S(2)}) %collective-permute-start.5) | collective-permute-done | bytes 655392 | tf_op jit(solution)/shard_map/ppermute | solution.py:351
  80.1 2.1 %collective-permute-start.4 = (f32[256,640]{1,0:T(8,128)S(1)}, f32[256,640]{1,0:T(8,128)S(1)}, u32[]{:S(2)}, u32[]{:S(2)}) collective-permute-start(f32[256,640]{1,0:T(8,128)S(1)} %copy-done.10), channel_id=1, source_target_pairs={{0,2},{2,0},{4,6},{6,4},{8,10},{10,8},{12,14},{14,12},{1,3},{3,1},... | collective-permute-start | bytes 1966088 | tf_op jit(solution)/shard_map/ppermute | solution.py:351
  82.2 1.4 %add.64 = f32[256,640]{1,0:T(8,128)S(1)} add(f32[256,640]{1,0:T(8,128)} %add.51, f32[256,640]{1,0:T(8,128)} %collective-permute-done.6) | non-fusion elementwise | flops 163840 | bytes 1966080 | tf_op jit(solution)/shard_map/add | solution.py:396
  84.3 4.5 %collective-permute-start.16 = (f32[128,640]{1,0:T(8,128)S(1)}, f32[128,640]{1,0:T(8,128)S(1)}, u32[]{:S(2)}, u32[]{:S(2)}) collective-permute-start(f32[128,640]{1,0:T(8,128)S(1)} %get-tuple-element.73), channel_id=1, source_target_pairs={{0,4},{2,6},{4,0},{6,2},{8,12},{10,14},{12,8},{14,10},{1,5},{3,7},... | collective-permute-start | bytes 983048 | tf_op jit(solution)/shard_map/ppermute | solution.py:354
  88.7 1.4 %add_add_fusion = f32[256,640]{1,0:T(8,128)S(1)} fusion(f32[256,640]{1,0:T(8,128)} %collective-permute-done.11, f32[256,640]{1,0:T(8,128)S(1)} %get-tuple-element.48, f32[256,640]{1,0:T(8,128)} %collective-permute-done.5), kind=kLoop, calls=%fused_computation | loop fusion | flops 327680 | bytes 2621440 | tf_op jit(solution)/shard_map/add | solution.py:398
  90.2 7.2 %collective-permute-done.16.refs_3_ = f32[128,640]{1,0:T(8,128)S(1)} collective-permute-done((f32[128,640]{1,0:T(8,128)S(1)}, f32[128,640]{1,0:T(8,128)S(1)}, u32[]{:S(2)}, u32[]{:S(2)}) %collective-permute-start.16) | collective-permute-done | bytes 327712 | tf_op jit(solution)/shard_map/ppermute | solution.py:354
  100.2 7.1 %collective-permute-done.4.refs_1_ = f32[256,640]{1,0:T(8,128)S(1)} collective-permute-done((f32[256,640]{1,0:T(8,128)S(1)}, f32[256,640]{1,0:T(8,128)S(1)}, u32[]{:S(2)}, u32[]{:S(2)}) %collective-permute-start.4) | collective-permute-done | bytes 655392 | tf_op jit(solution)/shard_map/ppermute | solution.py:351
  109.3 2.4 %collective-permute-done.20 = f32[8,128]{1,0:T(8,128)S(1)} collective-permute-done((f32[8,128]{1,0:T(8,128)S(1)}, f32[8,128]{1,0:T(8,128)S(1)}, u32[]{:S(2)}, u32[]{:S(2)}) %collective-permute-start.20) | collective-permute-done | bytes 4128 | tf_op jit(solution)/shard_map/ppermute | solution.py:410
  111.7 7.4 %collective-permute-start.21 = (f32[8,128]{1,0:T(8,128)S(1)}, f32[8,128]{1,0:T(8,128)S(1)}, u32[]{:S(2)}, u32[]{:S(2)}) collective-permute-start(f32[8,128]{1,0:T(8,128)S(1)} %max.9), channel_id=1, source_target_pairs={{0,4},{2,6},{4,0},{6,2},{8,12},{10,14},{12,8},{14,10},{1,5},{3,7},... | collective-permute-start | bytes 12296 | tf_op jit(solution)/shard_map/ppermute | solution.py:410
  119.1 1.6 %collective-permute-done.21 = f32[8,128]{1,0:T(8,128)S(1)} collective-permute-done((f32[8,128]{1,0:T(8,128)S(1)}, f32[8,128]{1,0:T(8,128)S(1)}, u32[]{:S(2)}, u32[]{:S(2)}) %collective-permute-start.21) | collective-permute-done | bytes 4128 | tf_op jit(solution)/shard_map/ppermute | solution.py:410
  120.7 3.0 %collective-permute-start.22 = (f32[8,128]{1,0:T(8,128)S(1)}, f32[8,128]{1,0:T(8,128)S(1)}, u32[]{:S(2)}, u32[]{:S(2)}) collective-permute-start(f32[8,128]{1,0:T(8,128)S(1)} %max.10), channel_id=1, source_target_pairs={{0,8},{2,10},{4,12},{6,14},{8,0},{10,2},{12,4},{14,6},{1,9},{3,11}... | collective-permute-start | bytes 12296 | tf_op jit(solution)/shard_map/ppermute | solution.py:410
  (65 shorter events, 16.0 us)
Async XLA Ops:
  5.0 24.6 %collective-permute-start.1 = (f32[256,640]{1,0:T(8,128)}, f32[256,640]{1,0:T(8,128)}, u32[]{:S(2)}, u32[]{:S(2)}) collective-permute-start(f32[256,640]{1,0:T(8,128)} %get-tuple-element.42), channel_id=1, source_target_pairs={{0,2},{2,0},{4,6},{6,4},{8,10},{10,8},{12,14},{14,12},{1,3},{3,1},... | collective-permute-start | bytes 1966088 | tf_op jit(solution)/shard_map/ppermute | solution.py:351
  8.1 21.6 %collective-permute-start.2 = (f32[256,640]{1,0:T(8,128)}, f32[256,640]{1,0:T(8,128)}, u32[]{:S(2)}, u32[]{:S(2)}) collective-permute-start(f32[256,640]{1,0:T(8,128)} %get-tuple-element.43), channel_id=1, source_target_pairs={{0,4},{2,6},{4,0},{6,2},{8,12},{10,14},{12,8},{14,10},{1,5},{3,7},... | collective-permute-start | bytes 1966088 | tf_op jit(solution)/shard_map/ppermute | solution.py:354
  9.6 8.1 %copy-start.2 = (bf16[256,832]{1,0:T(8,128)(2,1)S(1)}, bf16[256,832]{1,0:T(8,128)(2,1)}, u32[]{:S(2)}) copy-start(bf16[256,832]{1,0:T(8,128)(2,1)} %get-tuple-element.38.refs_7_.half_a) | copy-start | bytes 1277956
  15.2 24.0 %collective-permute-start.8 = (f32[256,640]{1,0:T(8,128)}, f32[256,640]{1,0:T(8,128)S(1)}, u32[]{:S(2)}, u32[]{:S(2)}) collective-permute-start(f32[256,640]{1,0:T(8,128)} %get-tuple-element.55), channel_id=1, source_target_pairs={{0,4},{2,6},{12,8},{14,10},{1,5},{3,7},{13,9},{15,11},{16,20},{18,... | collective-permute-start | bytes 1966088 | tf_op jit(solution)/shard_map/ppermute | solution.py:357
  17.6 21.6 %collective-permute-start.7 = (f32[256,640]{1,0:T(8,128)}, f32[256,640]{1,0:T(8,128)S(1)}, u32[]{:S(2)}, u32[]{:S(2)}) collective-permute-start(f32[256,640]{1,0:T(8,128)} %get-tuple-element.54), channel_id=1, source_target_pairs={{0,2},{2,0},{4,6},{6,4},{8,10},{10,8},{12,14},{14,12},{1,3},{3,1},... | collective-permute-start | bytes 1966088 | tf_op jit(solution)/shard_map/ppermute | solution.py:351
  27.7 24.2 %collective-permute-start = (f32[256,640]{1,0:T(8,128)S(1)}, f32[256,640]{1,0:T(8,128)S(1)}, u32[]{:S(2)}, u32[]{:S(2)}) collective-permute-start(f32[256,640]{1,0:T(8,128)S(1)} %get-tuple-element.40), channel_id=1, source_target_pairs={{0,2},{2,0},{4,6},{6,4},{8,10},{10,8},{12,14},{14,12},{1,3},{3,1},... | collective-permute-start | bytes 1966088 | tf_op jit(solution)/shard_map/ppermute | solution.py:351
  29.7 13.9 %copy-start.3 = (bf16[8,96,512]{2,1,0:T(8,128)(2,1)S(1)}, bf16[8,96,512]{2,1,0:T(8,128)(2,1)}, u32[]{:S(2)}) copy-start(bf16[8,96,512]{2,1,0:T(8,128)(2,1)} %refs_4_.5) | copy-start | bytes 2359300
  30.9 12.7 %copy-start = (bf16[8,96,512]{2,1,0:T(8,128)(2,1)S(1)}, bf16[8,96,512]{2,1,0:T(8,128)(2,1)}, u32[]{:S(2)}) copy-start(bf16[8,96,512]{2,1,0:T(8,128)(2,1)} %refs_2_.5) | copy-start | bytes 2359300
  30.9 12.7 %copy-start.1 = (bf16[8,8,4096]{2,1,0:T(8,128)(2,1)S(1)}, bf16[8,8,4096]{2,1,0:T(8,128)(2,1)}, u32[]{:S(2)}) copy-start(bf16[8,8,4096]{2,1,0:T(8,128)(2,1)} %refs_1_.5) | copy-start | bytes 1572868
  30.9 12.7 %copy-start.5 = (bf16[8,8,512]{2,1,0:T(8,128)(2,1)S(1)}, bf16[8,8,512]{2,1,0:T(8,128)(2,1)}, u32[]{:S(2)}) copy-start(bf16[8,8,512]{2,1,0:T(8,128)(2,1)} %refs_3_.5) | copy-start | bytes 196612
  30.9 12.7 %copy-start.7 = (bf16[8,8,512]{2,1,0:T(8,128)(2,1)S(1)}, bf16[8,8,512]{2,1,0:T(8,128)(2,1)}, u32[]{:S(2)}) copy-start(bf16[8,8,512]{2,1,0:T(8,128)(2,1)} %refs_5_.5) | copy-start | bytes 196612
  31.0 12.7 %copy-start.8 = (s32[8]{0:T(128)S(1)}, s32[8]{0:T(128)}, u32[]{:S(2)}) copy-start(s32[8]{0:T(128)} %refs_0_.5) | copy-start | bytes 100
  31.0 22.1 %collective-permute-start.3 = (f32[256,640]{1,0:T(8,128)S(1)}, f32[256,640]{1,0:T(8,128)S(1)}, u32[]{:S(2)}, u32[]{:S(2)}) collective-permute-start(f32[256,640]{1,0:T(8,128)S(1)} %add.50), channel_id=1, source_target_pairs={{0,4},{2,6},{12,8},{14,10},{1,5},{3,7},{13,9},{15,11},{16,20},{18,... | collective-permute-start | bytes 1966088 | tf_op jit(solution)/shard_map/ppermute | solution.py:357
  32.4 33.5 %collective-permute-start.9 = (f32[256,640]{1,0:T(8,128)S(1)}, f32[256,640]{1,0:T(8,128)S(1)}, u32[]{:S(2)}, u32[]{:S(2)}) collective-permute-start(f32[256,640]{1,0:T(8,128)S(1)} %get-tuple-element.57), channel_id=1, source_target_pairs={{0,2},{2,0},{4,6},{6,4},{8,10},{10,8},{12,14},{14,12},{1,3},{3,1},... | collective-permute-start | bytes 1966088 | tf_op jit(solution)/shard_map/ppermute | solution.py:351
  39.2 27.9 %collective-permute-start.10 = (f32[256,640]{1,0:T(8,128)S(1)}, f32[256,640]{1,0:T(8,128)S(1)}, u32[]{:S(2)}, u32[]{:S(2)}) collective-permute-start(f32[256,640]{1,0:T(8,128)S(1)} %add.53), channel_id=1, source_target_pairs={{0,4},{2,6},{12,8},{14,10},{1,5},{3,7},{13,9},{15,11},{16,20},{18,... | collective-permute-start | bytes 1966088 | tf_op jit(solution)/shard_map/ppermute | solution.py:357
  54.0 18.7 %collective-permute-start.13 = (f32[256,640]{1,0:T(8,128)}, f32[256,640]{1,0:T(8,128)}, u32[]{:S(2)}, u32[]{:S(2)}) collective-permute-start(f32[256,640]{1,0:T(8,128)} %add.57), channel_id=1, source_target_pairs={{4,8},{6,10},{8,4},{10,6},{5,9},{7,11},{9,5},{11,7},{20,24},{22,26... | collective-permute-start | bytes 1966088 | tf_op jit(solution)/shard_map/ppermute | solution.py:360
  55.5 24.6 %collective-permute-start.5 = (f32[256,640]{1,0:T(8,128)}, f32[256,640]{1,0:T(8,128)}, u32[]{:S(2)}, u32[]{:S(2)}) collective-permute-start(f32[256,640]{1,0:T(8,128)} %get-tuple-element.49), channel_id=1, source_target_pairs={{0,2},{2,0},{4,6},{6,4},{8,10},{10,8},{12,14},{14,12},{1,3},{3,1},... | collective-permute-start | bytes 1966088 | tf_op jit(solution)/shard_map/ppermute | solution.py:351
  57.3 24.8 %collective-permute-start.6 = (f32[256,640]{1,0:T(8,128)}, f32[256,640]{1,0:T(8,128)}, u32[]{:S(2)}, u32[]{:S(2)}) collective-permute-start(f32[256,640]{1,0:T(8,128)} %add.51), channel_id=1, source_target_pairs={{0,4},{2,6},{12,8},{14,10},{1,5},{3,7},{13,9},{15,11},{16,20},{18,... | collective-permute-start | bytes 1966088 | tf_op jit(solution)/shard_map/ppermute | solution.py:357
  68.1 16.2 %collective-permute-start.11 = (f32[256,640]{1,0:T(8,128)}, f32[256,640]{1,0:T(8,128)}, u32[]{:S(2)}, u32[]{:S(2)}) collective-permute-start(f32[256,640]{1,0:T(8,128)} %add.54), channel_id=1, source_target_pairs={{4,8},{6,10},{8,4},{10,6},{5,9},{7,11},{9,5},{11,7},{20,24},{22,26... | collective-permute-start | bytes 1966088 | tf_op jit(solution)/shard_map/ppermute | solution.py:360
  70.8 27.3 %collective-permute-start.18 = (f32[256,640]{1,0:T(8,128)S(1)}, f32[256,640]{1,0:T(8,128)S(1)}, u32[]{:S(2)}, u32[]{:S(2)}) collective-permute-start(f32[256,640]{1,0:T(8,128)S(1)} %add.63), channel_id=1, source_target_pairs={{0,2},{2,0},{4,6},{6,4},{8,10},{10,8},{12,14},{14,12},{1,3},{3,1},... | collective-permute-start | bytes 1966088 | tf_op jit(solution)/shard_map/ppermute | solution.py:351
  72.7 7.4 %copy-start.10 = (f32[256,640]{1,0:T(8,128)S(1)}, f32[256,640]{1,0:T(8,128)}, u32[]{:S(2)}) copy-start(f32[256,640]{1,0:T(8,128)} %copy-done.9) | copy-start | bytes 1966084
  74.0 16.1 %collective-permute-start.14 = (f32[128,640]{1,0:T(8,128)S(1)}, f32[128,640]{1,0:T(8,128)S(1)}, u32[]{:S(2)}, u32[]{:S(2)}) collective-permute-start(f32[128,640]{1,0:T(8,128)S(1)} %get-tuple-element.74), channel_id=1, source_target_pairs={{0,4},{2,6},{4,0},{6,2},{8,12},{10,14},{12,8},{14,10},{1,5},{3,7},... | collective-permute-start | bytes 983048 | tf_op jit(solution)/shard_map/ppermute | solution.py:354
  80.1 27.1 %collective-permute-start.4 = (f32[256,640]{1,0:T(8,128)S(1)}, f32[256,640]{1,0:T(8,128)S(1)}, u32[]{:S(2)}, u32[]{:S(2)}) collective-permute-start(f32[256,640]{1,0:T(8,128)S(1)} %copy-done.10), channel_id=1, source_target_pairs={{0,2},{2,0},{4,6},{6,4},{8,10},{10,8},{12,14},{14,12},{1,3},{3,1},... | collective-permute-start | bytes 1966088 | tf_op jit(solution)/shard_map/ppermute | solution.py:351
  83.5 15.3 %collective-permute-start.19 = (f32[256,640]{1,0:T(8,128)S(1)}, f32[256,640]{1,0:T(8,128)S(1)}, u32[]{:S(2)}, u32[]{:S(2)}) collective-permute-start(f32[256,640]{1,0:T(8,128)S(1)} %add.64), channel_id=1, source_target_pairs={{4,8},{6,10},{8,4},{10,6},{5,9},{7,11},{9,5},{11,7},{20,24},{22,26... | collective-permute-start | bytes 1966088 | tf_op jit(solution)/shard_map/ppermute | solution.py:360
  84.3 13.1 %collective-permute-start.16 = (f32[128,640]{1,0:T(8,128)S(1)}, f32[128,640]{1,0:T(8,128)S(1)}, u32[]{:S(2)}, u32[]{:S(2)}) collective-permute-start(f32[128,640]{1,0:T(8,128)S(1)} %get-tuple-element.73), channel_id=1, source_target_pairs={{0,4},{2,6},{4,0},{6,2},{8,12},{10,14},{12,8},{14,10},{1,5},{3,7},... | collective-permute-start | bytes 983048 | tf_op jit(solution)/shard_map/ppermute | solution.py:354
  90.1 17.8 %collective-permute-start.12 = (f32[256,640]{1,0:T(8,128)S(1)}, f32[256,640]{1,0:T(8,128)S(1)}, u32[]{:S(2)}, u32[]{:S(2)}) collective-permute-start(f32[256,640]{1,0:T(8,128)S(1)} %add_add_fusion), channel_id=1, source_target_pairs={{0,4},{2,6},{4,0},{6,2},{8,12},{10,14},{12,8},{14,10},{1,5},{3,7},... | collective-permute-start | bytes 1966088 | tf_op jit(solution)/shard_map/ppermute | solution.py:354
  97.5 9.8 %collective-permute-start.15 = (f32[128,640]{1,0:T(8,128)S(1)}, f32[128,640]{1,0:T(8,128)S(1)}, u32[]{:S(2)}, u32[]{:S(2)}) collective-permute-start(f32[128,640]{1,0:T(8,128)S(1)} %get-tuple-element.76), channel_id=1, source_target_pairs={{4,8},{6,10},{8,4},{10,6},{5,9},{7,11},{9,5},{11,7},{20,24},{22,26... | collective-permute-start | bytes 983048 | tf_op jit(solution)/shard_map/ppermute | solution.py:360
  98.2 9.1 %collective-permute-start.17 = (f32[128,640]{1,0:T(8,128)S(1)}, f32[128,640]{1,0:T(8,128)S(1)}, u32[]{:S(2)}, u32[]{:S(2)}) collective-permute-start(f32[128,640]{1,0:T(8,128)S(1)} %get-tuple-element.75), channel_id=1, source_target_pairs={{4,8},{6,10},{8,4},{10,6},{5,9},{7,11},{9,5},{11,7},{20,24},{22,26... | collective-permute-start | bytes 983048 | tf_op jit(solution)/shard_map/ppermute | solution.py:360
  99.1 8.7 %copy-start.4 = (f32[256,640]{1,0:T(8,128)S(1)}, f32[256,640]{1,0:T(8,128)}, u32[]{:S(2)}) copy-start(f32[256,640]{1,0:T(8,128)} %get-tuple-element.46.refs_0_) | copy-start | bytes 1966084
  108.1 3.6 %collective-permute-start.20 = (f32[8,128]{1,0:T(8,128)S(1)}, f32[8,128]{1,0:T(8,128)S(1)}, u32[]{:S(2)}, u32[]{:S(2)}) collective-permute-start(f32[8,128]{1,0:T(8,128)S(1)} %get-tuple-element.72), channel_id=1, source_target_pairs={{0,2},{2,0},{4,6},{6,4},{8,10},{10,8},{12,14},{14,12},{1,3},{3,1},... | collective-permute-start | bytes 12296 | tf_op jit(solution)/shard_map/ppermute | solution.py:410
  111.7 9.0 %collective-permute-start.21 = (f32[8,128]{1,0:T(8,128)S(1)}, f32[8,128]{1,0:T(8,128)S(1)}, u32[]{:S(2)}, u32[]{:S(2)}) collective-permute-start(f32[8,128]{1,0:T(8,128)S(1)} %max.9), channel_id=1, source_target_pairs={{0,4},{2,6},{4,0},{6,2},{8,12},{10,14},{12,8},{14,10},{1,5},{3,7},... | collective-permute-start | bytes 12296 | tf_op jit(solution)/shard_map/ppermute | solution.py:410
  120.7 4.6 %collective-permute-start.22 = (f32[8,128]{1,0:T(8,128)S(1)}, f32[8,128]{1,0:T(8,128)S(1)}, u32[]{:S(2)}, u32[]{:S(2)}) collective-permute-start(f32[8,128]{1,0:T(8,128)S(1)} %max.10), channel_id=1, source_target_pairs={{0,8},{2,10},{4,12},{6,14},{8,0},{10,2},{12,4},{14,6},{1,9},{3,11}... | collective-permute-start | bytes 12296 | tf_op jit(solution)/shard_map/ppermute | solution.py:410
  (5 other events, 9.0 us)

commit v4 on v3

--- a/solution.py
+++ b/solution.py
@@ -12,6 +12,7 @@
 GROUP = 8
 BUCKET = 128
 BATCH = 16
+EARLY = 2
 VMEM_BYTES = 20 * 1024 * 1024
 HBM = pl.BlockSpec(memory_space=pltpu.HBM)
 PARAMS = pltpu.CompilerParams(vmem_limit_bytes=VMEM_BYTES)
@@ -163,52 +164,57 @@
 def begin_kernel(half, jobs, *refs):
     ins, refs = refs[:6], refs[6:]
     features, refs = refs[0], refs[1:]
-    cots = []
-    if half:
-        cots.append(refs[0])
-        refs = refs[1:]
     cot_half, refs = refs[0], refs[1:]
     outs, refs = refs[: len(jobs)], refs[len(jobs) :]
     bufs, (rows, blocks, sems, block_sems) = refs[:6], refs[6:]
     sources = list(ins[:2]) + [lanes_of(ref, half) for ref in ins[2:]]
     copies = copy_all(sources, bufs, sems)
-    kinds = [kind for kind, _ in jobs]
+    kinds = [kind for job in jobs for kind, _ in job]
     block_copies = start_features(features, kinds, blocks, block_sems)
     for copy in copies:
         copy.wait()
     lengths, rewards, q, ck, nk, cot = bufs
     attend_heads(lengths, rewards, q, ck, nk, cot=cot, rows=rows)
-    cot_half[...] = rows[...].T.astype(jnp.bfloat16)
-    cots.append(cot_half)
-    for i, (_, h) in enumerate(jobs):
-        block_copies[i].wait()
-        outs[i][...] = jnp.dot(cots[h][...], blocks[i], preferred_element_type=jnp.float32)
-
-
-def begin(half, jobs, arrays, features, cots, width):
+    cots = rows[...].T.astype(jnp.bfloat16)
+    cot_half[...] = cots
+    place = 0
+    for out, job in zip(outs, jobs):
+        first = 0
+        for _, size in job:
+            block_copies[place].wait()
+            out[first : first + size] = jnp.dot(
+                cots[:size], blocks[place], preferred_element_type=jnp.float32
+            )
+            first += size
+            place += 1
+
+
+def begin(half, jobs, arrays, features, width):
     lengths, rewards, queries, ck, _, _ = arrays
     depth = features.shape[0]
     columns = ck.shape[2] // 2
+    count = max(sum(len(job) for job in jobs), 1)
     shapes = [jax.ShapeDtypeStruct((columns, depth), jnp.bfloat16)]
-    shapes += [jax.ShapeDtypeStruct((columns, width), jnp.float32)] * len(jobs)
+    for job in jobs:
+        shapes.append(jax.ShapeDtypeStruct((sum(size for _, size in job), width), jnp.float32))
     vmem = pl.BlockSpec(memory_space=pltpu.VMEM)
     return pl.pallas_call(
         functools.partial(begin_kernel, half, jobs),
-        in_specs=[HBM] * 7 + [vmem] * len(cots),
+        in_specs=[HBM] * 7,
         out_specs=[vmem] * len(shapes),
         out_shape=shapes,
         scratch_shapes=[pltpu.SMEM(x.shape, x.dtype) for x in arrays[:2]]
         + [pltpu.VMEM(x.shape[:2] + (x.shape[2] // 2,), x.dtype) for x in arrays[2:]]
         + [
             pltpu.VMEM((depth, columns), jnp.float32),
-            pltpu.VMEM((max(len(jobs), 1), depth, width), jnp.bfloat16),
+            pltpu.VMEM((count, depth, width), jnp.bfloat16),
             pltpu.SemaphoreType.DMA((6,)),
-            pltpu.SemaphoreType.DMA((max(len(jobs), 1),)),
+            pltpu.SemaphoreType.DMA((count,)),
         ],
         compiler_params=WIDE,
         cost_estimate=SMALL,
         name="value_cot",
-    )(*arrays, features, *cots)
+    )(*arrays, features)
 
 
 def attended_kernel(*refs):
@@ -271,24 +277,16 @@
     )(features, *halves)
 
 
-def add_kernel(half, edge_first, *refs):
+def add_kernel(half, cut, *refs):
     count = len(refs) - 3
     total, peaks = refs[-2:]
     size = total.shape[0]
-    cut = size // 2
-    for b in range(2):
-        rows = slice(b * cut, (b + 1) * cut)
-        part = None
-        for ref in refs[:2]:
-            part = ref[rows] if part is None else part + ref[rows]
-        if edge_first:
-            rank = lax.axis_index("dp")
-            edge = (rank < 2) | (rank >= 6)
-            part = part + jnp.where(edge, refs[2 + b][...], refs[4][rows])
-            part = part + refs[5][rows]
-        else:
-            part = part + refs[2][rows] + refs[3 + b][...]
-        total[rows] = part
+    last = refs[count - 1][...]
+    if not half:
+        piece = jnp.concatenate([refs[3][size:], refs[4][...]], axis=0)
+        rank = lax.axis_index("dp")
+        last = jnp.where((rank < 2) | (rank >= 6), last, piece)
+    total[...] = refs[0][...] + refs[1][half * size : (half + 1) * size] + refs[2][...] + last
     buckets = size // BUCKET
     lane = lax.broadcasted_iota(jnp.int32, peaks.shape, 1)
     peak = refs[count][...]
@@ -299,10 +297,10 @@
     peaks[...] = peak
 
 
-def add_parts(half, edge_first, parts, peaks):
+def add_parts(half, cut, parts, peaks):
     vmem = pl.BlockSpec(memory_space=pltpu.VMEM)
     return pl.pallas_call(
-        functools.partial(add_kernel, half, edge_first),
+        functools.partial(add_kernel, half, cut),
         in_specs=[vmem] * (len(parts) + 1),
         out_specs=[vmem] * 2,
         out_shape=[
@@ -356,54 +354,58 @@
     def outward(x):
         return lax.ppermute(x, "dp", [(r, r ^ 2) for r in (0, 1, 6, 7)])
 
+    def inward(x):
+        return lax.ppermute(x, "dp", [(r, r ^ 2) for r in (2, 3, 4, 5)])
+
     def middle(x):
         return lax.ppermute(x, "dp", [(r, r ^ 6) for r in (2, 3, 4, 5)])
 
     def together(*arrays):
         return lax.optimization_barrier(arrays)
 
+    def after(x, *others):
+        return together(x, *others)[0]
+
     def make(*jobs):
         return chunks(jobs, features, halves, width)
 
     a, b = 0, 1
-    cross3a, crosspa, cross3b, ownpa = firsts
-    (own3a, own3b, cross2a, cross2b, own2a, own2b, crosspb, crossoa, crossob, ownpb, ownoa, ownob) = (
+    edge0, cross3a, cross3b = firsts
+    (own3a, own3b, cross2a, cross2b, own2a, own2b, crosspb, crossoa, crossob, ownpa, ownpb, ownoa, ownob) = (
         make(
             ((FAR3, SAME), (a, b)),
             ((FAR2, CROSS), (a, b)),
             ((FAR2, SAME), (a, b)),
             ((PAIR, CROSS), (b,)),
             ((OWN, CROSS), (a, b)),
-            ((PAIR, SAME), (b,)),
+            ((PAIR, SAME), (a, b)),
             ((OWN, SAME), (a, b)),
         )
     )
 
-    y0, e0 = together(across(cross3a), pair(crosspa))
-    y1, e1 = together(across(cross3b), outward(ownpa))
-    y2, e2, attended = together(across(cross2a), outward(own3a + y0), attended)
-    y3, e3 = together(across(cross2b), outward(own3b + y1))
+    size = ownpa.shape[0]
+    cut = size // EARLY
+    e0 = pair(edge0)
+    y0 = across(cross3a)
+    y1 = after(across(cross3b), y0, e0)
+    e2 = after(outward(own3a + y0), y1)
+    y2 = after(across(after(cross2a, y0)), e2)
+    e3 = after(outward(own3b + y1), y2)
     m3 = middle(own3a + y0 + e2)
-    y4, e4 = together(across(crosspb), outward(own2a + y2))
+    y3 = after(across(after(cross2b, y1, attended)), e3)
+    e4 = after(outward(own2a + y2), y3)
     m4 = middle(own3b + y1 + e3)
-    y5 = across(crossoa + e0)
-    cut = own2b.shape[0] // 2
-    e5 = []
-    for part in (slice(0, cut), slice(cut, None)):
-        e5.append(
-            pair(jnp.where(edge, own2b[part] + y3[part], ownpa[part] + m3[part]))
-        )
+    y4 = after(across(after(crosspb, y2)), e4)
+    e5 = after(pair(jnp.where(edge, own2b + y3, ownpa + m3)), y4)
     m5 = middle(own2a + y2 + e4)
-    y6 = across(crossob)
+    y5 = across(after(jnp.concatenate([crossoa + e0[:size], crossob], axis=0), y3))
+    late = outward(ownpa[cut:])
     e6 = pair(ownpb + y4 + m4)
-    m6 = []
-    for i, part in enumerate((slice(0, cut), slice(cut, None))):
-        (send,) = together(own2b[part] + y3[part] + e5[i])
-        m6.append(middle(send))
+    m6 = middle(own2b + y3 + e5)
     peaks = jnp.zeros((8, HD), jnp.float32)
-    total, peaks = add_parts(a, True, [ownoa, y5, *e5, e1, m5], peaks)
+    total, peaks = add_parts(a, cut, [ownoa, y5, m5, e0, late, e5], peaks)
     grad, peaks = together(place(a, total, None, columns), peaks)
-    total, peaks = add_parts(b, False, [ownob, y6, e6, *m6], peaks)
+    total, peaks = add_parts(b, cut, [ownob, y5, m6, e6], peaks)
     grad = place(b, total, grad, columns)
     for hop in (1, 2, 4):
         peaks = jnp.maximum(
@@ -438,10 +440,16 @@
     arrays = (lengths, rewards, queries, cache_keys, new_keys, cotangent)
     on_grid = dp == 8
     width = features.shape[2] // 8 if on_grid else BUCKET
-    jobs_a = (((FAR3, CROSS), 0), ((PAIR, CROSS), 0)) if on_grid else ()
-    jobs_b = (((FAR3, CROSS), 1), ((PAIR, SAME), 0)) if on_grid else ()
-    half_a, *firsts = begin(0, jobs_a, arrays, flat, [], width)
-    half_b, *seconds = begin(1, jobs_b, arrays, flat, [half_a], width)
+    half = cache_keys.shape[2] // 2
+    jobs_a, jobs_b = (), ()
+    if on_grid:
+        jobs_a = (
+            (((PAIR, CROSS), half), ((PAIR, SAME), half // EARLY)),
+            (((FAR3, CROSS), half),),
+        )
+        jobs_b = ((((FAR3, CROSS), half),),)
+    half_a, *firsts = begin(0, jobs_a, arrays, flat, width)
+    half_b, *seconds = begin(1, jobs_b, arrays, flat, width)
     attended = attend(lengths, queries, cache_keys, new_keys, cache_values, new_values)
     firsts += seconds
     if on_grid:

time: 126 us -> 124 us (0.984)
  starting transfers between devices: 51.5 us -> 48.8 us
  waiting for transfers between devices: 37.1 us -> 39.3 us
    ppermute x4, waiting for transfers between devices: 8.07 us -> 15.7 us  [outward(): return lax.ppermute(x, 'dp', [(r, r ^ 2) for r in (0, 1, 6, 7)])]
    ppermute x4 -> x3, waiting for transfers between devices: 7.74 us -> 2.41 us  [pair(): return lax.ppermute(x, 'dp', [(r, r ^ 2) for r in range(dp)])]
    ppermute x4, starting transfers between devices: 15.1 us -> 19.3 us  [outward(): return lax.ppermute(x, 'dp', [(r, r ^ 2) for r in (0, 1, 6, 7)])]
    ppermute x3, starting transfers between devices: 11.6 us -> 7.47 us  [reduce_on_grid(): lax.ppermute(peaks, 'dp', [(r, r ^ hop) for r in range(dp)])]
    ppermute x4 -> x3, starting transfers between devices: 9.74 us -> 8.17 us  [pair(): return lax.ppermute(x, 'dp', [(r, r ^ 2) for r in range(dp)])]
    add x4 -> x5, other arithmetic: 3.55 us -> 5.07 us  [the longest x1 1.7 us: reduce_on_grid(): e2 = after(outward(own3a + y0), y1)]
    ppermute x5 -> x4, starting transfers between devices: 5.1 us -> 3.7 us  [middle(): return lax.ppermute(x, 'dp', [(r, r ^ 6) for r in (2, 3, 4, 5)])]
    pallas_call x2, Pallas kernels: 9.91 us -> 8.59 us  [begin(): pl.pallas_call(functools.partial(begin_kernel, half, jobs), in_specs=[HBM...]
  transfers between devices with their start and end apart: 23 -> 20, of which waited for: 12 -> 12; matrix products, arithmetic and copies ran while one was open for 7% -> 7% of each run, Pallas kernels for 15% -> 14%
where the time goes in v4:
time: 124 us; the launch traced here: 123 us
  starting transfers between devices  48.8 us (39%)
  waiting for transfers between devices  39.3 us (32%)
  Pallas kernels  22.9 us (18%)
  other arithmetic  9.15 us (7%)
  local copies, waits for them, and re-layouts  2.46 us (2%)
    ppermute x4, starting transfers between devices, outward(): return lax.ppermute(x, 'dp', [(r, r ^ 2) for r in (0, 1, 6, 7)])  19.3 us
    ppermute x6, waiting for transfers between devices, across(): return lax.ppermute(x, 'dp', [(r, r ^ 1) for r in range(dp)])  16.6 us
    ppermute x4, waiting for transfers between devices, outward(): return lax.ppermute(x, 'dp', [(r, r ^ 2) for r in (0, 1, 6, 7)])  15.7 us
    ppermute x6, starting transfers between devices, across(): return lax.ppermute(x, 'dp', [(r, r ^ 1) for r in range(dp)])  10.1 us
    pallas_call x1, Pallas kernels, chunks(): pl.pallas_call(functools.partial(chunk_kernel, jobs), in_specs=[HBM, vmem...  8.77 us
    pallas_call x2, Pallas kernels, begin(): pl.pallas_call(functools.partial(begin_kernel, half, jobs), in_specs=[HBM...  8.59 us
    ppermute x3, starting transfers between devices, pair(): return lax.ppermute(x, 'dp', [(r, r ^ 2) for r in range(dp)])  8.17 us
    ppermute x3, starting transfers between devices, reduce_on_grid(): lax.ppermute(peaks, 'dp', [(r, r ^ hop) for r in range(dp)])  7.47 us
  transfers between devices with their start and end apart: 20, of which 12 were waited for; matrix products, arithmetic and copies ran while one was open for 7% of the time, Pallas kernels for 14%

profile of v4, /device:TPU:0, one launch (start us, length us, event | category | flops | bytes accessed | tf_op | source)
XLA Modules:
  0.0 123.5 jit_solution(18421168079582672897)
XLA Ops:
  0.6 4.8 %value_cot.2 = (bf16[256,832]{1,0:T(8,128)(2,1)}, f32[384,640]{1,0:T(8,128)}, f32[256,640]{1,0:T(8,128)}) custom-call(s32[8]{0:T(128)} %refs_0_.5, f32[8]{0:T(128)} %refs_1_.5, bf16[8,8,4096]{2,1,0:T(8,128)(2,1)} %refs_2_.5, bf16[8,96,512]{2,1,0:T(8,128)(2,1)} %refs_3_.5, bf16[8,8,512]{2,1,0:T(8,128)(2,1)} %refs_4_.5, bf16[8,8,4096]{2,1,0:T(8,128)(2,1)} %refs_5_.5, ...), custom_call_target="tpu_custom_call" | custom-call | flops 1000 | bytes 1000 | tf_op jit(solution)/shard_map/value_cot/pallas_call | solution.py:201
  5.4 3.0 %collective-permute-start.2 = (f32[256,640]{1,0:T(8,128)}, f32[256,640]{1,0:T(8,128)}, u32[]{:S(2)}, u32[]{:S(2)}) collective-permute-start(f32[256,640]{1,0:T(8,128)} %get-tuple-element.47), channel_id=1, source_target_pairs={{0,2},{2,0},{4,6},{6,4},{8,10},{10,8},{12,14},{14,12},{1,3},{3,1},... | collective-permute-start | bytes 1966088 | tf_op jit(solution)/shard_map/ppermute | solution.py:349
  8.4 1.6 %collective-permute-start = (f32[384,640]{1,0:T(8,128)}, f32[384,640]{1,0:T(8,128)S(1)}, u32[]{:S(2)}, u32[]{:S(2)}) collective-permute-start(f32[384,640]{1,0:T(8,128)} %get-tuple-element.43), channel_id=1, source_target_pairs={{0,4},{2,6},{4,0},{6,2},{8,12},{10,14},{12,8},{14,10},{1,5},{3,7},... | collective-permute-start | bytes 2949128 | tf_op jit(solution)/shard_map/ppermute | solution.py:352
  10.0 3.8 %value_cot.3 = (bf16[256,832]{1,0:T(8,128)(2,1)}, f32[256,640]{1,0:T(8,128)}) custom-call(s32[8]{0:T(128)} %refs_0_.5, f32[8]{0:T(128)} %refs_1_.5, bf16[8,8,4096]{2,1,0:T(8,128)(2,1)} %refs_2_.5, bf16[8,96,512]{2,1,0:T(8,128)(2,1)} %refs_3_.5, bf16[8,8,512]{2,1,0:T(8,128)(2,1)} %refs_4_.5, bf16[8,8,4096]{2,1,0:T(8,128)(2,1)} %refs_5_.5, ...), custom_call_target="tpu_custom_call" | custom-call | flops 1000 | bytes 1000 | tf_op jit(solution)/shard_map/value_cot/pallas_call | solution.py:201
  15.4 8.8 %chunk.1 = (f32[256,640]{1,0:T(8,128)S(1)}, f32[256,640]{1,0:T(8,128)S(1)}, f32[256,640]{1,0:T(8,128)}, f32[256,640]{1,0:T(8,128)}, f32[256,640]{1,0:T(8,128)S(1...) custom-call(bf16[832,5120]{1,0:T(8,128)(2,1)} %bitcast.5, ...), custom_call_target="tpu_custom_call" | custom-call | flops 1000 | bytes 1000 | tf_op jit(solution)/shard_map/chunk/pallas_call | solution.py:265
  24.3 1.7 %add.42 = f32[256,640]{1,0:T(8,128)S(1)} add(f32[256,640]{1,0:T(8,128)S(1)} %get-tuple-element.53, f32[256,640]{1,0:T(8,128)} %collective-permute-done.2) | non-fusion elementwise | flops 163840 | bytes 1966080 | tf_op jit(solution)/shard_map/add | solution.py:391
  26.1 3.7 %collective-permute-start.6 = (f32[256,640]{1,0:T(8,128)S(1)}, f32[256,640]{1,0:T(8,128)S(1)}, u32[]{:S(2)}, u32[]{:S(2)}) collective-permute-start(f32[256,640]{1,0:T(8,128)S(1)} %add.42), channel_id=1, source_target_pairs={{0,4},{2,6},{12,8},{14,10},{1,5},{3,7},{13,9},{15,11},{16,20},{18,... | collective-permute-start | bytes 1966088 | tf_op jit(solution)/shard_map/ppermute | solution.py:355
  29.8 1.6 %collective-permute-start.5 = (f32[256,640]{1,0:T(8,128)}, f32[256,640]{1,0:T(8,128)}, u32[]{:S(2)}, u32[]{:S(2)}) collective-permute-start(f32[256,640]{1,0:T(8,128)} %get-tuple-element.52), channel_id=1, source_target_pairs={{0,2},{2,0},{4,6},{6,4},{8,10},{10,8},{12,14},{14,12},{1,3},{3,1},... | collective-permute-start | bytes 1966088 | tf_op jit(solution)/shard_map/ppermute | solution.py:349
  31.4 6.9 %collective-permute-done.1 = f32[256,640]{1,0:T(8,128)S(1)} collective-permute-done((f32[256,640]{1,0:T(8,128)}, f32[256,640]{1,0:T(8,128)S(1)}, u32[]{:S(2)}, u32[]{:S(2)}) %collective-permute-start.1) | collective-permute-done | bytes 655392 | tf_op jit(solution)/shard_map/ppermute | solution.py:349
  39.2 4.9 %collective-permute-start.4 = (f32[256,640]{1,0:T(8,128)}, f32[256,640]{1,0:T(8,128)}, u32[]{:S(2)}, u32[]{:S(2)}) collective-permute-start(f32[256,640]{1,0:T(8,128)} %add.41), channel_id=1, source_target_pairs={{0,4},{2,6},{12,8},{14,10},{1,5},{3,7},{13,9},{15,11},{16,20},{18,... | collective-permute-start | bytes 1966088 | tf_op jit(solution)/shard_map/ppermute | solution.py:355
  44.2 2.8 %attend.1 = bf16[8,8,4096]{2,1,0:T(8,128)(2,1)} custom-call(s32[8]{0:T(128)S(1)} %copy-done.14, bf16[8,8,4096]{2,1,0:T(8,128)(2,1)S(1)} %copy-done.1, bf16[8,96,512]{2,1,0:T(8,128)(2,1)S(1)} %copy-done, bf16[8,8,512]{2,1,0:T(8,128)(2,1)S(1)} %copy-done.10, bf16[8,96,512]{2,1,0:T(8,128)(2,1)S(1)} %copy-done.2, bf16[8,8,512]{2,1,0:T(8,128)(2,1)S(1)} %copy-done.13), custom_call_target="tpu_custom_call" | custom-call | flops 1000 | bytes 1000 | tf_op jit(solution)/shard_map/attend/pallas_call | solution.py:230
  47.0 1.6 %collective-permute-start.3 = (f32[256,640]{1,0:T(8,128)}, f32[256,640]{1,0:T(8,128)}, u32[]{:S(2)}, u32[]{:S(2)}) collective-permute-start(f32[256,640]{1,0:T(8,128)} %get-tuple-element.49), channel_id=1, source_target_pairs={{0,2},{2,0},{4,6},{6,4},{8,10},{10,8},{12,14},{14,12},{1,3},{3,1},... | collective-permute-start | bytes 1966088 | tf_op jit(solution)/shard_map/ppermute | solution.py:349
  49.5 1.5 %collective-permute-start.8 = (f32[256,640]{1,0:T(8,128)}, f32[256,640]{1,0:T(8,128)}, u32[]{:S(2)}, u32[]{:S(2)}) collective-permute-start(f32[256,640]{1,0:T(8,128)} %add.44), channel_id=1, source_target_pairs={{4,8},{6,10},{8,4},{10,6},{5,9},{7,11},{9,5},{11,7},{20,24},{22,26... | collective-permute-start | bytes 1966088 | tf_op jit(solution)/shard_map/ppermute | solution.py:361
  53.2 1.2 add.46
  54.4 1.3 %collective-permute-start.10 = (f32[256,640]{1,0:T(8,128)S(1)}, f32[256,640]{1,0:T(8,128)S(1)}, u32[]{:S(2)}, u32[]{:S(2)}) collective-permute-start(f32[256,640]{1,0:T(8,128)S(1)} %copy-done.16), channel_id=1, source_target_pairs={{0,2},{2,0},{4,6},{6,4},{8,10},{10,8},{12,14},{14,12},{1,3},{3,1},... | collective-permute-start | bytes 1966088 | tf_op jit(solution)/shard_map/ppermute | solution.py:349
  55.7 3.5 %collective-permute-start.11 = (f32[256,640]{1,0:T(8,128)S(1)}, f32[256,640]{1,0:T(8,128)S(1)}, u32[]{:S(2)}, u32[]{:S(2)}) collective-permute-start(f32[256,640]{1,0:T(8,128)S(1)} %add.46), channel_id=1, source_target_pairs={{0,4},{2,6},{12,8},{14,10},{1,5},{3,7},{13,9},{15,11},{16,20},{18,... | collective-permute-start | bytes 1966088 | tf_op jit(solution)/shard_map/ppermute | solution.py:355
  59.3 1.4 %collective-permute-done.4 = f32[256,640]{1,0:T(8,128)} collective-permute-done((f32[256,640]{1,0:T(8,128)}, f32[256,640]{1,0:T(8,128)}, u32[]{:S(2)}, u32[]{:S(2)}) %collective-permute-start.4) | collective-permute-done | bytes 655392 | tf_op jit(solution)/shard_map/ppermute | solution.py:355
  60.6 1.4 %add.49 = f32[256,640]{1,0:T(8,128)S(1)} add(f32[256,640]{1,0:T(8,128)} %add.41, f32[256,640]{1,0:T(8,128)} %collective-permute-done.4) | non-fusion elementwise | flops 163840 | bytes 1966080 | tf_op jit(solution)/shard_map/add | solution.py:397
  62.7 3.8 %collective-permute-done.3 = f32[256,640]{1,0:T(8,128)} collective-permute-done((f32[256,640]{1,0:T(8,128)}, f32[256,640]{1,0:T(8,128)}, u32[]{:S(2)}, u32[]{:S(2)}) %collective-permute-start.3) | collective-permute-done | bytes 655392 | tf_op jit(solution)/shard_map/ppermute | solution.py:349
  66.5 2.1 %collective-permute-start.7 = (f32[512,640]{1,0:T(8,128)S(1)}, f32[512,640]{1,0:T(8,128)S(1)}, u32[]{:S(2)}, u32[]{:S(2)}) collective-permute-start(f32[512,640]{1,0:T(8,128)S(1)} %pad_maximum_fusion), channel_id=1, source_target_pairs={{0,2},{2,0},{4,6},{6,4},{8,10},{10,8},{12,14},{14,12},{1,3},{3,1},... | collective-permute-start | bytes 3932168 | tf_op jit(solution)/shard_map/ppermute | solution.py:349
  68.5 1.5 %add_select_fusion = (f32[256,640]{1,0:T(8,128)S(1)}, f32[256,640]{1,0:T(8,128)S(1)}) fusion(f32[256,640]{1,0:T(8,128)S(1)} %get-tuple-element.60, f32[256,640]{1,0:T(8,128)} %collective-permute-done.8, pred[]{:T(512)S(6)} %or.3, f32[256,640]{1,0:T(8,128)S(1)} %copy-done.5, f32[256,640]{1,0:T(8,128)} %collective-permute-done.3), kind=kLoop, calls=%fused_computation.3 | loop fusion | flops 491520 | bytes 3932161 | tf_op jit(solution)/shard_map/jit(_where)/select_n | solution.py:399
  70.0 1.6 %collective-permute-start.9 = (f32[256,640]{1,0:T(8,128)S(1)}, f32[256,640]{1,0:T(8,128)S(1)}, u32[]{:S(2)}, u32[]{:S(2)}) collective-permute-start(f32[256,640]{1,0:T(8,128)S(1)} %get-tuple-element.75), channel_id=1, source_target_pairs={{0,4},{2,6},{4,0},{6,2},{8,12},{10,14},{12,8},{14,10},{1,5},{3,7},... | collective-permute-start | bytes 1966088 | tf_op jit(solution)/shard_map/ppermute | solution.py:352
  71.7 2.9 %collective-permute-done.11 = f32[256,640]{1,0:T(8,128)S(1)} collective-permute-done((f32[256,640]{1,0:T(8,128)S(1)}, f32[256,640]{1,0:T(8,128)S(1)}, u32[]{:S(2)}, u32[]{:S(2)}) %collective-permute-start.11) | collective-permute-done | bytes 655392 | tf_op jit(solution)/shard_map/ppermute | solution.py:355
  74.7 5.7 %collective-permute-done.10 = f32[256,640]{1,0:T(8,128)S(1)} collective-permute-done((f32[256,640]{1,0:T(8,128)S(1)}, f32[256,640]{1,0:T(8,128)S(1)}, u32[]{:S(2)}, u32[]{:S(2)}) %collective-permute-start.10) | collective-permute-done | bytes 655392 | tf_op jit(solution)/shard_map/ppermute | solution.py:349
  81.2 5.0 %collective-permute-start.14 = (f32[256,640]{1,0:T(8,128)S(1)}, f32[256,640]{1,0:T(8,128)S(1)}, u32[]{:S(2)}, u32[]{:S(2)}) collective-permute-start(f32[256,640]{1,0:T(8,128)S(1)} %add_add_fusion), channel_id=1, source_target_pairs={{0,4},{2,6},{4,0},{6,2},{8,12},{10,14},{12,8},{14,10},{1,5},{3,7},... | collective-permute-start | bytes 1966088 | tf_op jit(solution)/shard_map/ppermute | solution.py:352
  86.2 2.4 %collective-permute-done.9.refs_5_ = f32[256,640]{1,0:T(8,128)S(1)} collective-permute-done((f32[256,640]{1,0:T(8,128)S(1)}, f32[256,640]{1,0:T(8,128)S(1)}, u32[]{:S(2)}, u32[]{:S(2)}) %collective-permute-start.9) | collective-permute-done | bytes 655392 | tf_op jit(solution)/shard_map/ppermute | solution.py:352
  89.6 7.2 %collective-permute-start.16 = (f32[128,640]{1,0:T(8,128)S(1)}, f32[128,640]{1,0:T(8,128)S(1)}, u32[]{:S(2)}, u32[]{:S(2)}) collective-permute-start(f32[128,640]{1,0:T(8,128)S(1)} %slice.10), channel_id=1, source_target_pairs={{0,4},{2,6},{12,8},{14,10},{1,5},{3,7},{13,9},{15,11},{16,20},{18,... | collective-permute-start | bytes 983048 | tf_op jit(solution)/shard_map/ppermute | solution.py:355
  96.8 11.4 %collective-permute-done.16.refs_4_ = f32[128,640]{1,0:T(8,128)S(1)} collective-permute-done((f32[128,640]{1,0:T(8,128)S(1)}, f32[128,640]{1,0:T(8,128)S(1)}, u32[]{:S(2)}, u32[]{:S(2)}) %collective-permute-start.16) | collective-permute-done | bytes 327712 | tf_op jit(solution)/shard_map/ppermute | solution.py:355
  111.0 2.4 %collective-permute-done.17 = f32[8,128]{1,0:T(8,128)S(1)} collective-permute-done((f32[8,128]{1,0:T(8,128)S(1)}, f32[8,128]{1,0:T(8,128)S(1)}, u32[]{:S(2)}, u32[]{:S(2)}) %collective-permute-start.17) | collective-permute-done | bytes 4128 | tf_op jit(solution)/shard_map/ppermute | solution.py:412
  113.5 3.3 %collective-permute-start.18 = (f32[8,128]{1,0:T(8,128)S(1)}, f32[8,128]{1,0:T(8,128)S(1)}, u32[]{:S(2)}, u32[]{:S(2)}) collective-permute-start(f32[8,128]{1,0:T(8,128)S(1)} %max.9), channel_id=1, source_target_pairs={{0,4},{2,6},{4,0},{6,2},{8,12},{10,14},{12,8},{14,10},{1,5},{3,7},... | collective-permute-start | bytes 12296 | tf_op jit(solution)/shard_map/ppermute | solution.py:412
  116.7 1.6 %collective-permute-done.18 = f32[8,128]{1,0:T(8,128)S(1)} collective-permute-done((f32[8,128]{1,0:T(8,128)S(1)}, f32[8,128]{1,0:T(8,128)S(1)}, u32[]{:S(2)}, u32[]{:S(2)}) %collective-permute-start.18) | collective-permute-done | bytes 4128 | tf_op jit(solution)/shard_map/ppermute | solution.py:412
  118.3 3.0 %collective-permute-start.19 = (f32[8,128]{1,0:T(8,128)S(1)}, f32[8,128]{1,0:T(8,128)S(1)}, u32[]{:S(2)}, u32[]{:S(2)}) collective-permute-start(f32[8,128]{1,0:T(8,128)S(1)} %max.10), channel_id=1, source_target_pairs={{0,8},{2,10},{4,12},{6,14},{8,0},{10,2},{12,4},{14,6},{1,9},{3,11}... | collective-permute-start | bytes 12296 | tf_op jit(solution)/shard_map/ppermute | solution.py:412
  (67 shorter events, 13.3 us)
Async XLA Ops:
  5.4 18.9 %collective-permute-start.2 = (f32[256,640]{1,0:T(8,128)}, f32[256,640]{1,0:T(8,128)}, u32[]{:S(2)}, u32[]{:S(2)}) collective-permute-start(f32[256,640]{1,0:T(8,128)} %get-tuple-element.47), channel_id=1, source_target_pairs={{0,2},{2,0},{4,6},{6,4},{8,10},{10,8},{12,14},{14,12},{1,3},{3,1},... | collective-permute-start | bytes 1966088 | tf_op jit(solution)/shard_map/ppermute | solution.py:349
  8.4 29.8 %collective-permute-start = (f32[384,640]{1,0:T(8,128)}, f32[384,640]{1,0:T(8,128)S(1)}, u32[]{:S(2)}, u32[]{:S(2)}) collective-permute-start(f32[384,640]{1,0:T(8,128)} %get-tuple-element.43), channel_id=1, source_target_pairs={{0,4},{2,6},{4,0},{6,2},{8,12},{10,14},{12,8},{14,10},{1,5},{3,7},... | collective-permute-start | bytes 2949128 | tf_op jit(solution)/shard_map/ppermute | solution.py:352
  13.8 24.4 %collective-permute-start.1 = (f32[256,640]{1,0:T(8,128)}, f32[256,640]{1,0:T(8,128)S(1)}, u32[]{:S(2)}, u32[]{:S(2)}) collective-permute-start(f32[256,640]{1,0:T(8,128)} %get-tuple-element.46), channel_id=1, source_target_pairs={{0,2},{2,0},{4,6},{6,4},{8,10},{10,8},{12,14},{14,12},{1,3},{3,1},... | collective-permute-start | bytes 1966088 | tf_op jit(solution)/shard_map/ppermute | solution.py:349
  24.2 15.0 %copy-start.4 = (f32[256,640]{1,0:T(8,128)}, f32[256,640]{1,0:T(8,128)S(1)}, u32[]{:S(2)}) copy-start(f32[256,640]{1,0:T(8,128)S(1)} %get-tuple-element.59) | copy-start | bytes 1966084
  24.2 15.0 %copy-start.6 = (f32[256,640]{1,0:T(8,128)}, f32[256,640]{1,0:T(8,128)S(1)}, u32[]{:S(2)}) copy-start(f32[256,640]{1,0:T(8,128)S(1)} %get-tuple-element.63) | copy-start | bytes 1966084
  24.2 15.0 %copy-start.8 = (f32[256,640]{1,0:T(8,128)}, f32[256,640]{1,0:T(8,128)S(1)}, u32[]{:S(2)}) copy-start(f32[256,640]{1,0:T(8,128)S(1)} %get-tuple-element.42) | copy-start | bytes 1966084
  24.3 15.0 %copy-start.15 = (f32[256,640]{1,0:T(8,128)}, f32[256,640]{1,0:T(8,128)S(1)}, u32[]{:S(2)}) copy-start(f32[256,640]{1,0:T(8,128)S(1)} %get-tuple-element.62) | copy-start | bytes 1966084
  24.3 19.8 %copy-start.2 = (bf16[8,96,512]{2,1,0:T(8,128)(2,1)S(1)}, bf16[8,96,512]{2,1,0:T(8,128)(2,1)}, u32[]{:S(2)}) copy-start(bf16[8,96,512]{2,1,0:T(8,128)(2,1)} %refs_4_.3) | copy-start | bytes 2359300
  26.0 18.1 %copy-start = (bf16[8,96,512]{2,1,0:T(8,128)(2,1)S(1)}, bf16[8,96,512]{2,1,0:T(8,128)(2,1)}, u32[]{:S(2)}) copy-start(bf16[8,96,512]{2,1,0:T(8,128)(2,1)} %refs_3_.5) | copy-start | bytes 2359300
  26.0 18.1 %copy-start.1 = (bf16[8,8,4096]{2,1,0:T(8,128)(2,1)S(1)}, bf16[8,8,4096]{2,1,0:T(8,128)(2,1)}, u32[]{:S(2)}) copy-start(bf16[8,8,4096]{2,1,0:T(8,128)(2,1)} %refs_2_.5) | copy-start | bytes 1572868
  26.1 18.1 %copy-start.10 = (bf16[8,8,512]{2,1,0:T(8,128)(2,1)S(1)}, bf16[8,8,512]{2,1,0:T(8,128)(2,1)}, u32[]{:S(2)}) copy-start(bf16[8,8,512]{2,1,0:T(8,128)(2,1)} %refs_4_.5) | copy-start | bytes 196612
  26.1 18.1 %copy-start.13 = (bf16[8,8,512]{2,1,0:T(8,128)(2,1)S(1)}, bf16[8,8,512]{2,1,0:T(8,128)(2,1)}, u32[]{:S(2)}) copy-start(bf16[8,8,512]{2,1,0:T(8,128)(2,1)} %refs_5_.3) | copy-start | bytes 196612
  26.1 18.1 %copy-start.14 = (s32[8]{0:T(128)S(1)}, s32[8]{0:T(128)}, u32[]{:S(2)}) copy-start(s32[8]{0:T(128)} %refs_0_.5) | copy-start | bytes 100
  26.1 22.5 %collective-permute-start.6 = (f32[256,640]{1,0:T(8,128)S(1)}, f32[256,640]{1,0:T(8,128)S(1)}, u32[]{:S(2)}, u32[]{:S(2)}) collective-permute-start(f32[256,640]{1,0:T(8,128)S(1)} %add.42), channel_id=1, source_target_pairs={{0,4},{2,6},{12,8},{14,10},{1,5},{3,7},{13,9},{15,11},{16,20},{18,... | collective-permute-start | bytes 1966088 | tf_op jit(solution)/shard_map/ppermute | solution.py:355
  29.8 22.6 %collective-permute-start.5 = (f32[256,640]{1,0:T(8,128)}, f32[256,640]{1,0:T(8,128)}, u32[]{:S(2)}, u32[]{:S(2)}) collective-permute-start(f32[256,640]{1,0:T(8,128)} %get-tuple-element.52), channel_id=1, source_target_pairs={{0,2},{2,0},{4,6},{6,4},{8,10},{10,8},{12,14},{14,12},{1,3},{3,1},... | collective-permute-start | bytes 1966088 | tf_op jit(solution)/shard_map/ppermute | solution.py:349
  39.2 21.4 %collective-permute-start.4 = (f32[256,640]{1,0:T(8,128)}, f32[256,640]{1,0:T(8,128)}, u32[]{:S(2)}, u32[]{:S(2)}) collective-permute-start(f32[256,640]{1,0:T(8,128)} %add.41), channel_id=1, source_target_pairs={{0,4},{2,6},{12,8},{14,10},{1,5},{3,7},{13,9},{15,11},{16,20},{18,... | collective-permute-start | bytes 1966088 | tf_op jit(solution)/shard_map/ppermute | solution.py:355
  47.0 19.4 %collective-permute-start.3 = (f32[256,640]{1,0:T(8,128)}, f32[256,640]{1,0:T(8,128)}, u32[]{:S(2)}, u32[]{:S(2)}) collective-permute-start(f32[256,640]{1,0:T(8,128)} %get-tuple-element.49), channel_id=1, source_target_pairs={{0,2},{2,0},{4,6},{6,4},{8,10},{10,8},{12,14},{14,12},{1,3},{3,1},... | collective-permute-start | bytes 1966088 | tf_op jit(solution)/shard_map/ppermute | solution.py:349
  49.5 19.0 %collective-permute-start.8 = (f32[256,640]{1,0:T(8,128)}, f32[256,640]{1,0:T(8,128)}, u32[]{:S(2)}, u32[]{:S(2)}) collective-permute-start(f32[256,640]{1,0:T(8,128)} %add.44), channel_id=1, source_target_pairs={{4,8},{6,10},{8,4},{10,6},{5,9},{7,11},{9,5},{11,7},{20,24},{22,26... | collective-permute-start | bytes 1966088 | tf_op jit(solution)/shard_map/ppermute | solution.py:361
  54.4 14.1 %copy-start.5 = (f32[256,640]{1,0:T(8,128)S(1)}, f32[256,640]{1,0:T(8,128)}, u32[]{:S(2)}) copy-start(f32[256,640]{1,0:T(8,128)} %copy-done.4) | copy-start | bytes 1966084
  54.4 26.0 %collective-permute-start.10 = (f32[256,640]{1,0:T(8,128)S(1)}, f32[256,640]{1,0:T(8,128)S(1)}, u32[]{:S(2)}, u32[]{:S(2)}) collective-permute-start(f32[256,640]{1,0:T(8,128)S(1)} %copy-done.16), channel_id=1, source_target_pairs={{0,2},{2,0},{4,6},{6,4},{8,10},{10,8},{12,14},{14,12},{1,3},{3,1},... | collective-permute-start | bytes 1966088 | tf_op jit(solution)/shard_map/ppermute | solution.py:349
  55.7 18.8 %collective-permute-start.11 = (f32[256,640]{1,0:T(8,128)S(1)}, f32[256,640]{1,0:T(8,128)S(1)}, u32[]{:S(2)}, u32[]{:S(2)}) collective-permute-start(f32[256,640]{1,0:T(8,128)S(1)} %add.46), channel_id=1, source_target_pairs={{0,4},{2,6},{12,8},{14,10},{1,5},{3,7},{13,9},{15,11},{16,20},{18,... | collective-permute-start | bytes 1966088 | tf_op jit(solution)/shard_map/ppermute | solution.py:355
  62.0 19.1 %collective-permute-start.13 = (f32[256,640]{1,0:T(8,128)S(1)}, f32[256,640]{1,0:T(8,128)S(1)}, u32[]{:S(2)}, u32[]{:S(2)}) collective-permute-start(f32[256,640]{1,0:T(8,128)S(1)} %add.49), channel_id=1, source_target_pairs={{4,8},{6,10},{8,4},{10,6},{5,9},{7,11},{9,5},{11,7},{20,24},{22,26... | collective-permute-start | bytes 1966088 | tf_op jit(solution)/shard_map/ppermute | solution.py:361
  66.5 41.8 %collective-permute-start.7 = (f32[512,640]{1,0:T(8,128)S(1)}, f32[512,640]{1,0:T(8,128)S(1)}, u32[]{:S(2)}, u32[]{:S(2)}) collective-permute-start(f32[512,640]{1,0:T(8,128)S(1)} %pad_maximum_fusion), channel_id=1, source_target_pairs={{0,2},{2,0},{4,6},{6,4},{8,10},{10,8},{12,14},{14,12},{1,3},{3,1},... | collective-permute-start | bytes 3932168 | tf_op jit(solution)/shard_map/ppermute | solution.py:349
  70.0 18.6 %collective-permute-start.9 = (f32[256,640]{1,0:T(8,128)S(1)}, f32[256,640]{1,0:T(8,128)S(1)}, u32[]{:S(2)}, u32[]{:S(2)}) collective-permute-start(f32[256,640]{1,0:T(8,128)S(1)} %get-tuple-element.75), channel_id=1, source_target_pairs={{0,4},{2,6},{4,0},{6,2},{8,12},{10,14},{12,8},{14,10},{1,5},{3,7},... | collective-permute-start | bytes 1966088 | tf_op jit(solution)/shard_map/ppermute | solution.py:352
  80.4 27.8 %collective-permute-start.15 = (f32[256,640]{1,0:T(8,128)S(1)}, f32[256,640]{1,0:T(8,128)S(1)}, u32[]{:S(2)}, u32[]{:S(2)}) collective-permute-start(f32[256,640]{1,0:T(8,128)S(1)} %add.51), channel_id=1, source_target_pairs={{4,8},{6,10},{8,4},{10,6},{5,9},{7,11},{9,5},{11,7},{20,24},{22,26... | collective-permute-start | bytes 1966088 | tf_op jit(solution)/shard_map/ppermute | solution.py:361
  81.2 28.4 %collective-permute-start.14 = (f32[256,640]{1,0:T(8,128)S(1)}, f32[256,640]{1,0:T(8,128)S(1)}, u32[]{:S(2)}, u32[]{:S(2)}) collective-permute-start(f32[256,640]{1,0:T(8,128)S(1)} %add_add_fusion), channel_id=1, source_target_pairs={{0,4},{2,6},{4,0},{6,2},{8,12},{10,14},{12,8},{14,10},{1,5},{3,7},... | collective-permute-start | bytes 1966088 | tf_op jit(solution)/shard_map/ppermute | solution.py:352
  88.6 19.6 %copy-start.9 = (f32[256,640]{1,0:T(8,128)S(1)}, f32[256,640]{1,0:T(8,128)}, u32[]{:S(2)}) copy-start(f32[256,640]{1,0:T(8,128)} %get-tuple-element.68.refs_0_) | copy-start | bytes 1966084
  88.7 20.9 %collective-permute-start.12 = (f32[256,640]{1,0:T(8,128)S(1)}, f32[256,640]{1,0:T(8,128)S(1)}, u32[]{:S(2)}, u32[]{:S(2)}) collective-permute-start(f32[256,640]{1,0:T(8,128)S(1)} %add.47), channel_id=1, source_target_pairs={{4,8},{6,10},{8,4},{10,6},{5,9},{7,11},{9,5},{11,7},{20,24},{22,26... | collective-permute-start | bytes 1966088 | tf_op jit(solution)/shard_map/ppermute | solution.py:361
  89.6 18.6 %collective-permute-start.16 = (f32[128,640]{1,0:T(8,128)S(1)}, f32[128,640]{1,0:T(8,128)S(1)}, u32[]{:S(2)}, u32[]{:S(2)}) collective-permute-start(f32[128,640]{1,0:T(8,128)S(1)} %slice.10), channel_id=1, source_target_pairs={{0,4},{2,6},{12,8},{14,10},{1,5},{3,7},{13,9},{15,11},{16,20},{18,... | collective-permute-start | bytes 983048 | tf_op jit(solution)/shard_map/ppermute | solution.py:355
  109.9 3.6 %collective-permute-start.17 = (f32[8,128]{1,0:T(8,128)S(1)}, f32[8,128]{1,0:T(8,128)S(1)}, u32[]{:S(2)}, u32[]{:S(2)}) collective-permute-start(f32[8,128]{1,0:T(8,128)S(1)} %get-tuple-element.74), channel_id=1, source_target_pairs={{0,2},{2,0},{4,6},{6,4},{8,10},{10,8},{12,14},{14,12},{1,3},{3,1},... | collective-permute-start | bytes 12296 | tf_op jit(solution)/shard_map/ppermute | solution.py:412
  113.5 4.9 %collective-permute-start.18 = (f32[8,128]{1,0:T(8,128)S(1)}, f32[8,128]{1,0:T(8,128)S(1)}, u32[]{:S(2)}, u32[]{:S(2)}) collective-permute-start(f32[8,128]{1,0:T(8,128)S(1)} %max.9), channel_id=1, source_target_pairs={{0,4},{2,6},{4,0},{6,2},{8,12},{10,14},{12,8},{14,10},{1,5},{3,7},... | collective-permute-start | bytes 12296 | tf_op jit(solution)/shard_map/ppermute | solution.py:412
  118.3 4.6 %collective-permute-start.19 = (f32[8,128]{1,0:T(8,128)S(1)}, f32[8,128]{1,0:T(8,128)S(1)}, u32[]{:S(2)}, u32[]{:S(2)}) collective-permute-start(f32[8,128]{1,0:T(8,128)S(1)} %max.10), channel_id=1, source_target_pairs={{0,8},{2,10},{4,12},{6,14},{8,0},{10,2},{12,4},{14,6},{1,9},{3,11}... | collective-permute-start | bytes 12296 | tf_op jit(solution)/shard_map/ppermute | solution.py:412
  (5 other events, 11.4 us)

commit v5 on v4

--- a/solution.py
+++ b/solution.py
@@ -277,66 +277,57 @@
     )(features, *halves)
 
 
-def add_kernel(half, cut, *refs):
-    count = len(refs) - 3
-    total, peaks = refs[-2:]
-    size = total.shape[0]
-    last = refs[count - 1][...]
-    if not half:
-        piece = jnp.concatenate([refs[3][size:], refs[4][...]], axis=0)
-        rank = lax.axis_index("dp")
-        last = jnp.where((rank < 2) | (rank >= 6), last, piece)
-    total[...] = refs[0][...] + refs[1][half * size : (half + 1) * size] + refs[2][...] + last
-    buckets = size // BUCKET
+def add_kernel(*refs):
+    own_a, own_b, cross, mid_a, mid_b, first, late, last_a, last_b, total, peaks = refs
+    size = own_a.shape[0]
+    rank = lax.axis_index("dp")
+    edge = (rank < 2) | (rank >= 6)
+    piece = jnp.concatenate([first[size:], late[...]], axis=0)
+    arrived = jnp.where(edge, last_a[...], piece)
+    total[:size] = own_a[...] + cross[:size] + mid_a[...] + arrived
+    total[size:] = own_b[...] + cross[size:] + mid_b[...] + last_b[...]
     lane = lax.broadcasted_iota(jnp.int32, peaks.shape, 1)
-    peak = refs[count][...]
-    for b in range(buckets):
+    peak = jnp.zeros(peaks.shape, jnp.float32)
+    for b in range(2 * size // BUCKET):
         top = jnp.abs(total[b * BUCKET : (b + 1) * BUCKET])
         top = jnp.max(jnp.max(top, axis=0, keepdims=True), axis=1, keepdims=True)
-        peak = jnp.where(lane == half * buckets + b, top, peak)
+        peak = jnp.where(lane == b, top, peak)
     peaks[...] = peak
 
 
-def add_parts(half, cut, parts, peaks):
+def add_parts(parts):
     vmem = pl.BlockSpec(memory_space=pltpu.VMEM)
+    size, width = parts[0].shape
     return pl.pallas_call(
-        functools.partial(add_kernel, half, cut),
-        in_specs=[vmem] * (len(parts) + 1),
+        add_kernel,
+        in_specs=[vmem] * len(parts),
         out_specs=[vmem] * 2,
         out_shape=[
-            jax.ShapeDtypeStruct(parts[0].shape, jnp.float32),
-            jax.ShapeDtypeStruct(peaks.shape, jnp.float32),
+            jax.ShapeDtypeStruct((2 * size, width), jnp.float32),
+            jax.ShapeDtypeStruct((8, HD), jnp.float32),
         ],
         compiler_params=PARAMS,
         cost_estimate=SMALL,
         name="add_parts",
-    )(*parts, peaks)
-
-
-def place_kernel(total, *refs):
-    refs[-1][...] = total[...].T
-
-
-def place(half, total, grad, columns):
-    size, width = total.shape
-    in_specs = [pl.BlockSpec(memory_space=pltpu.VMEM)]
-    args = [total]
-    aliases = {}
-    if grad is not None:
-        in_specs.append(pl.BlockSpec(memory_space=pl.ANY))
-        args.append(grad)
-        aliases = {1: 0}
+    )(*parts)
+
+
+def place_kernel(total, grad):
+    grad[...] = total[...].T
+
+
+def place(total):
+    columns, width = total.shape
+    vmem = pl.BlockSpec(memory_space=pltpu.VMEM)
     return pl.pallas_call(
         place_kernel,
-        grid=(1,),
-        in_specs=in_specs,
-        out_specs=pl.BlockSpec((width, size), lambda i: (0, half)),
+        in_specs=[vmem],
+        out_specs=vmem,
         out_shape=jax.ShapeDtypeStruct((width, columns), jnp.float32),
-        input_output_aliases=aliases,
         compiler_params=PARAMS,
         cost_estimate=SMALL,
         name="place",
-    )(*args)
+    )(total)
 
 
 def reduce_on_grid(features, halves, firsts, attended, dp):
@@ -399,18 +390,13 @@
     e5 = after(pair(jnp.where(edge, own2b + y3, ownpa + m3)), y4)
     m5 = middle(own2a + y2 + e4)
     y5 = across(after(jnp.concatenate([crossoa + e0[:size], crossob], axis=0), y3))
-    late = outward(ownpa[cut:])
+    late = outward(after(ownpa[cut:], m5))
     e6 = pair(ownpb + y4 + m4)
     m6 = middle(own2b + y3 + e5)
-    peaks = jnp.zeros((8, HD), jnp.float32)
-    total, peaks = add_parts(a, cut, [ownoa, y5, m5, e0, late, e5], peaks)
-    grad, peaks = together(place(a, total, None, columns), peaks)
-    total, peaks = add_parts(b, cut, [ownob, y5, m6, e6], peaks)
-    grad = place(b, total, grad, columns)
-    for hop in (1, 2, 4):
-        peaks = jnp.maximum(
-            peaks, lax.ppermute(peaks, "dp", [(r, r ^ hop) for r in range(dp)])
-        )
+    total, peaks = add_parts([ownoa, ownob, y5, m5, m6, e0, late, e5, e6])
+    peaks = jnp.maximum(peaks, across(peaks))
+    peaks, grad = together(jnp.maximum(peaks, pair(peaks)), place(total))
+    peaks = jnp.maximum(peaks, lax.ppermute(peaks, "dp", [(r, r ^ 4) for r in range(dp)]))
     return attended, grad, peaks[0, : columns // BUCKET]
 
 

time: 124 us -> 122 us (0.984)
  starting transfers between devices: 48.8 us -> 46.1 us
  waiting for transfers between devices: 39.3 us -> 41.3 us
    ppermute x3 -> x4, waiting for transfers between devices: 2.41 us -> 11.4 us  [pair(): return lax.ppermute(x, 'dp', [(r, r ^ 2) for r in range(dp)])]
    ppermute x4, waiting for transfers between devices: 15.7 us -> 10.6 us  [outward(): return lax.ppermute(x, 'dp', [(r, r ^ 2) for r in (0, 1, 6, 7)])]
    ppermute x3 -> x1, starting transfers between devices: 7.47 us -> 3.04 us  [reduce_on_grid(): lax.ppermute(peaks, 'dp', [(r, r ^ 4) for r in range(dp)])]
    ppermute x3 -> x1, waiting for transfers between devices: 4.53 us -> 1.58 us  [reduce_on_grid(): lax.ppermute(peaks, 'dp', [(r, r ^ 4) for r in range(dp)])]
    ppermute x6 -> x7, starting transfers between devices: 10.1 us -> 11.6 us  [across(): return lax.ppermute(x, 'dp', [(r, r ^ 1) for r in range(dp)])]
    ppermute x6 -> x7, waiting for transfers between devices: 16.6 us -> 17.8 us  [across(): return lax.ppermute(x, 'dp', [(r, r ^ 1) for r in range(dp)])]
    pallas_call x4 -> x2, Pallas kernels: 2.69 us -> 1.82 us  [the longest x1 1.46 us: place(): pl.pallas_call(place_kernel, in_specs=[vmem], out_specs=vmem, out_shape=j...]
    ppermute x3 -> x4, starting transfers between devices: 8.17 us -> 8.41 us  [pair(): return lax.ppermute(x, 'dp', [(r, r ^ 2) for r in range(dp)])]
  transfers between devices with their start and end apart: 20 -> 20, of which waited for: 12 -> 13; matrix products, arithmetic and copies ran while one was open for 7% -> 8% of each run, Pallas kernels for 14% -> 14%
where the time goes in v5:
time: 122 us; the launch traced here: 121 us
  starting transfers between devices  46.1 us (38%)
  waiting for transfers between devices  41.3 us (34%)
  Pallas kernels  22.1 us (18%)
  other arithmetic  9.36 us (8%)
  local copies, waits for them, and re-layouts  1.63 us (1%)
    ppermute x4, starting transfers between devices, outward(): return lax.ppermute(x, 'dp', [(r, r ^ 2) for r in (0, 1, 6, 7)])  19.3 us
    ppermute x7, waiting for transfers between devices, across(): return lax.ppermute(x, 'dp', [(r, r ^ 1) for r in range(dp)])  17.8 us
    ppermute x7, starting transfers between devices, across(): return lax.ppermute(x, 'dp', [(r, r ^ 1) for r in range(dp)])  11.6 us
    ppermute x4, waiting for transfers between devices, pair(): return lax.ppermute(x, 'dp', [(r, r ^ 2) for r in range(dp)])  11.4 us
    ppermute x4, waiting for transfers between devices, outward(): return lax.ppermute(x, 'dp', [(r, r ^ 2) for r in (0, 1, 6, 7)])  10.6 us
    pallas_call x1, Pallas kernels, chunks(): pl.pallas_call(functools.partial(chunk_kernel, jobs), in_specs=[HBM, vmem...  8.84 us
    pallas_call x2, Pallas kernels, begin(): pl.pallas_call(functools.partial(begin_kernel, half, jobs), in_specs=[HBM...  8.58 us
    ppermute x4, starting transfers between devices, pair(): return lax.ppermute(x, 'dp', [(r, r ^ 2) for r in range(dp)])  8.41 us
  transfers between devices with their start and end apart: 20, of which 13 were waited for; matrix products, arithmetic and copies ran while one was open for 8% of the time, Pallas kernels for 14%

profile of v5, /device:TPU:0, one launch (start us, length us, event | category | flops | bytes accessed | tf_op | source)
XLA Modules:
  0.0 121.4 jit_solution(8905297463338447354)
XLA Ops:
  0.6 4.8 %value_cot.2 = (bf16[256,832]{1,0:T(8,128)(2,1)}, f32[384,640]{1,0:T(8,128)}, f32[256,640]{1,0:T(8,128)}) custom-call(s32[8]{0:T(128)} %refs_0_.5, f32[8]{0:T(128)} %refs_1_.5, bf16[8,8,4096]{2,1,0:T(8,128)(2,1)} %refs_2_.5, bf16[8,96,512]{2,1,0:T(8,128)(2,1)} %refs_3_.5, bf16[8,8,512]{2,1,0:T(8,128)(2,1)} %refs_4_.5, bf16[8,8,4096]{2,1,0:T(8,128)(2,1)} %refs_5_.5, ...), custom_call_target="tpu_custom_call" | custom-call | flops 1000 | bytes 1000 | tf_op jit(solution)/shard_map/value_cot/pallas_call | solution.py:201
  5.4 3.0 %collective-permute-start.2 = (f32[256,640]{1,0:T(8,128)}, f32[256,640]{1,0:T(8,128)}, u32[]{:S(2)}, u32[]{:S(2)}) collective-permute-start(f32[256,640]{1,0:T(8,128)} %get-tuple-element.47), channel_id=1, source_target_pairs={{0,2},{2,0},{4,6},{6,4},{8,10},{10,8},{12,14},{14,12},{1,3},{3,1},... | collective-permute-start | bytes 1966088 | tf_op jit(solution)/shard_map/ppermute | solution.py:340
  8.4 1.6 %collective-permute-start = (f32[384,640]{1,0:T(8,128)}, f32[384,640]{1,0:T(8,128)S(1)}, u32[]{:S(2)}, u32[]{:S(2)}) collective-permute-start(f32[384,640]{1,0:T(8,128)} %get-tuple-element.43), channel_id=1, source_target_pairs={{0,4},{2,6},{4,0},{6,2},{8,12},{10,14},{12,8},{14,10},{1,5},{3,7},... | collective-permute-start | bytes 2949128 | tf_op jit(solution)/shard_map/ppermute | solution.py:343
  10.0 3.8 %value_cot.3 = (bf16[256,832]{1,0:T(8,128)(2,1)}, f32[256,640]{1,0:T(8,128)}) custom-call(s32[8]{0:T(128)} %refs_0_.5, f32[8]{0:T(128)} %refs_1_.5, bf16[8,8,4096]{2,1,0:T(8,128)(2,1)} %refs_2_.5, bf16[8,96,512]{2,1,0:T(8,128)(2,1)} %refs_3_.5, bf16[8,8,512]{2,1,0:T(8,128)(2,1)} %refs_4_.5, bf16[8,8,4096]{2,1,0:T(8,128)(2,1)} %refs_5_.5, ...), custom_call_target="tpu_custom_call" | custom-call | flops 1000 | bytes 1000 | tf_op jit(solution)/shard_map/value_cot/pallas_call | solution.py:201
  15.4 8.8 %chunk.1 = (f32[256,640]{1,0:T(8,128)S(1)}, f32[256,640]{1,0:T(8,128)S(1)}, f32[256,640]{1,0:T(8,128)}, f32[256,640]{1,0:T(8,128)}, f32[256,640]{1,0:T(8,128)S(1...) custom-call(bf16[832,5120]{1,0:T(8,128)(2,1)} %bitcast.5, ...), custom_call_target="tpu_custom_call" | custom-call | flops 1000 | bytes 1000 | tf_op jit(solution)/shard_map/chunk/pallas_call | solution.py:265
  24.4 1.9 %add.42 = f32[256,640]{1,0:T(8,128)S(1)} add(f32[256,640]{1,0:T(8,128)S(1)} %get-tuple-element.53, f32[256,640]{1,0:T(8,128)} %collective-permute-done.2) | non-fusion elementwise | flops 163840 | bytes 1966080 | tf_op jit(solution)/shard_map/add | solution.py:382
  26.3 3.2 %collective-permute-start.6 = (f32[256,640]{1,0:T(8,128)S(1)}, f32[256,640]{1,0:T(8,128)S(1)}, u32[]{:S(2)}, u32[]{:S(2)}) collective-permute-start(f32[256,640]{1,0:T(8,128)S(1)} %add.42), channel_id=1, source_target_pairs={{0,4},{2,6},{12,8},{14,10},{1,5},{3,7},{13,9},{15,11},{16,20},{18,... | collective-permute-start | bytes 1966088 | tf_op jit(solution)/shard_map/ppermute | solution.py:346
  29.5 1.6 %collective-permute-start.5 = (f32[256,640]{1,0:T(8,128)}, f32[256,640]{1,0:T(8,128)}, u32[]{:S(2)}, u32[]{:S(2)}) collective-permute-start(f32[256,640]{1,0:T(8,128)} %get-tuple-element.52), channel_id=1, source_target_pairs={{0,2},{2,0},{4,6},{6,4},{8,10},{10,8},{12,14},{14,12},{1,3},{3,1},... | collective-permute-start | bytes 1966088 | tf_op jit(solution)/shard_map/ppermute | solution.py:340
  31.2 2.8 %attend.1 = bf16[8,8,4096]{2,1,0:T(8,128)(2,1)} custom-call(s32[8]{0:T(128)S(1)} %copy-done.14, bf16[8,8,4096]{2,1,0:T(8,128)(2,1)S(1)} %copy-done.1, bf16[8,96,512]{2,1,0:T(8,128)(2,1)S(1)} %copy-done, bf16[8,8,512]{2,1,0:T(8,128)(2,1)S(1)} %copy-done.10, bf16[8,96,512]{2,1,0:T(8,128)(2,1)S(1)} %copy-done.2, bf16[8,8,512]{2,1,0:T(8,128)(2,1)S(1)} %copy-done.13), custom_call_target="tpu_custom_call" | custom-call | flops 1000 | bytes 1000 | tf_op jit(solution)/shard_map/attend/pallas_call | solution.py:230
  34.0 4.2 %collective-permute-done.1 = f32[256,640]{1,0:T(8,128)S(1)} collective-permute-done((f32[256,640]{1,0:T(8,128)}, f32[256,640]{1,0:T(8,128)S(1)}, u32[]{:S(2)}, u32[]{:S(2)}) %collective-permute-start.1) | collective-permute-done | bytes 655392 | tf_op jit(solution)/shard_map/ppermute | solution.py:340
  39.2 4.9 %collective-permute-start.4 = (f32[256,640]{1,0:T(8,128)}, f32[256,640]{1,0:T(8,128)}, u32[]{:S(2)}, u32[]{:S(2)}) collective-permute-start(f32[256,640]{1,0:T(8,128)} %add.41), channel_id=1, source_target_pairs={{0,4},{2,6},{12,8},{14,10},{1,5},{3,7},{13,9},{15,11},{16,20},{18,... | collective-permute-start | bytes 1966088 | tf_op jit(solution)/shard_map/ppermute | solution.py:346
  44.1 1.5 %collective-permute-start.3 = (f32[256,640]{1,0:T(8,128)}, f32[256,640]{1,0:T(8,128)}, u32[]{:S(2)}, u32[]{:S(2)}) collective-permute-start(f32[256,640]{1,0:T(8,128)} %get-tuple-element.49), channel_id=1, source_target_pairs={{0,2},{2,0},{4,6},{6,4},{8,10},{10,8},{12,14},{14,12},{1,3},{3,1},... | collective-permute-start | bytes 1966088 | tf_op jit(solution)/shard_map/ppermute | solution.py:340
  47.4 1.5 %collective-permute-start.10 = (f32[256,640]{1,0:T(8,128)}, f32[256,640]{1,0:T(8,128)}, u32[]{:S(2)}, u32[]{:S(2)}) collective-permute-start(f32[256,640]{1,0:T(8,128)} %add.46), channel_id=1, source_target_pairs={{4,8},{6,10},{8,4},{10,6},{5,9},{7,11},{9,5},{11,7},{20,24},{22,26... | collective-permute-start | bytes 1966088 | tf_op jit(solution)/shard_map/ppermute | solution.py:352
  50.1 2.3 %collective-permute-done.5 = f32[256,640]{1,0:T(8,128)} collective-permute-done((f32[256,640]{1,0:T(8,128)}, f32[256,640]{1,0:T(8,128)}, u32[]{:S(2)}, u32[]{:S(2)}) %collective-permute-start.5) | collective-permute-done | bytes 655392 | tf_op jit(solution)/shard_map/ppermute | solution.py:340
  53.6 2.1 %collective-permute-start.12 = (f32[256,640]{1,0:T(8,128)S(1)}, f32[256,640]{1,0:T(8,128)S(1)}, u32[]{:S(2)}, u32[]{:S(2)}) collective-permute-start(f32[256,640]{1,0:T(8,128)S(1)} %copy-done.16), channel_id=1, source_target_pairs={{0,2},{2,0},{4,6},{6,4},{8,10},{10,8},{12,14},{14,12},{1,3},{3,1},... | collective-permute-start | bytes 1966088 | tf_op jit(solution)/shard_map/ppermute | solution.py:340
  55.7 3.5 %collective-permute-start.8 = (f32[256,640]{1,0:T(8,128)S(1)}, f32[256,640]{1,0:T(8,128)S(1)}, u32[]{:S(2)}, u32[]{:S(2)}) collective-permute-start(f32[256,640]{1,0:T(8,128)S(1)} %add.43), channel_id=1, source_target_pairs={{0,4},{2,6},{12,8},{14,10},{1,5},{3,7},{13,9},{15,11},{16,20},{18,... | collective-permute-start | bytes 1966088 | tf_op jit(solution)/shard_map/ppermute | solution.py:346
  62.7 3.8 %collective-permute-done.3 = f32[256,640]{1,0:T(8,128)} collective-permute-done((f32[256,640]{1,0:T(8,128)}, f32[256,640]{1,0:T(8,128)}, u32[]{:S(2)}, u32[]{:S(2)}) %collective-permute-start.3) | collective-permute-done | bytes 655392 | tf_op jit(solution)/shard_map/ppermute | solution.py:340
  66.5 1.5 %add_select_fusion = (f32[256,640]{1,0:T(8,128)S(1)}, f32[256,640]{1,0:T(8,128)S(1)}) fusion(f32[256,640]{1,0:T(8,128)S(1)} %get-tuple-element.62, f32[256,640]{1,0:T(8,128)} %collective-permute-done.10, pred[]{:T(512)S(6)} %or.3, f32[256,640]{1,0:T(8,128)S(1)} %copy-done.6, f32[256,640]{1,0:T(8,128)} %collective-permute-done.3), kind=kLoop, calls=%fused_computation.3 | loop fusion | flops 491520 | bytes 3932161 | tf_op jit(solution)/shard_map/jit(_where)/select_n | solution.py:390
  68.0 2.2 %collective-permute-start.11 = (f32[256,640]{1,0:T(8,128)S(1)}, f32[256,640]{1,0:T(8,128)S(1)}, u32[]{:S(2)}, u32[]{:S(2)}) collective-permute-start(f32[256,640]{1,0:T(8,128)S(1)} %get-tuple-element.73), channel_id=1, source_target_pairs={{0,4},{2,6},{4,0},{6,2},{8,12},{10,14},{12,8},{14,10},{1,5},{3,7},... | collective-permute-start | bytes 1966088 | tf_op jit(solution)/shard_map/ppermute | solution.py:343
  70.2 1.6 %collective-permute-start.7 = (f32[512,640]{1,0:T(8,128)S(1)}, f32[512,640]{1,0:T(8,128)S(1)}, u32[]{:S(2)}, u32[]{:S(2)}) collective-permute-start(f32[512,640]{1,0:T(8,128)S(1)} %pad_maximum_fusion), channel_id=1, source_target_pairs={{0,2},{2,0},{4,6},{6,4},{8,10},{10,8},{12,14},{14,12},{1,3},{3,1},... | collective-permute-start | bytes 3932168 | tf_op jit(solution)/shard_map/ppermute | solution.py:340
  71.8 2.7 %collective-permute-done.8 = f32[256,640]{1,0:T(8,128)S(1)} collective-permute-done((f32[256,640]{1,0:T(8,128)S(1)}, f32[256,640]{1,0:T(8,128)S(1)}, u32[]{:S(2)}, u32[]{:S(2)}) %collective-permute-start.8) | collective-permute-done | bytes 655392 | tf_op jit(solution)/shard_map/ppermute | solution.py:346
  75.4 5.0 %collective-permute-done.12 = f32[256,640]{1,0:T(8,128)S(1)} collective-permute-done((f32[256,640]{1,0:T(8,128)S(1)}, f32[256,640]{1,0:T(8,128)S(1)}, u32[]{:S(2)}, u32[]{:S(2)}) %collective-permute-start.12) | collective-permute-done | bytes 655392 | tf_op jit(solution)/shard_map/ppermute | solution.py:340
  80.5 2.2 %collective-permute-start.16 = (f32[256,640]{1,0:T(8,128)S(1)}, f32[256,640]{1,0:T(8,128)S(1)}, u32[]{:S(2)}, u32[]{:S(2)}) collective-permute-start(f32[256,640]{1,0:T(8,128)S(1)} %add_add_fusion), channel_id=1, source_target_pairs={{0,4},{2,6},{4,0},{6,2},{8,12},{10,14},{12,8},{14,10},{1,5},{3,7},... | collective-permute-start | bytes 1966088 | tf_op jit(solution)/shard_map/ppermute | solution.py:343
  82.7 5.9 %collective-permute-done.11.refs_7_ = f32[256,640]{1,0:T(8,128)S(1)} collective-permute-done((f32[256,640]{1,0:T(8,128)S(1)}, f32[256,640]{1,0:T(8,128)S(1)}, u32[]{:S(2)}, u32[]{:S(2)}) %collective-permute-start.11) | collective-permute-done | bytes 655392 | tf_op jit(solution)/shard_map/ppermute | solution.py:343
  89.6 7.7 %collective-permute-start.14 = (f32[128,640]{1,0:T(8,128)S(1)}, f32[128,640]{1,0:T(8,128)S(1)}, u32[]{:S(2)}, u32[]{:S(2)}) collective-permute-start(f32[128,640]{1,0:T(8,128)S(1)} %slice.10), channel_id=1, source_target_pairs={{0,4},{2,6},{12,8},{14,10},{1,5},{3,7},{13,9},{15,11},{16,20},{18,... | collective-permute-start | bytes 983048 | tf_op jit(solution)/shard_map/ppermute | solution.py:346
  97.3 5.4 %collective-permute-done.16.refs_8_ = f32[256,640]{1,0:T(8,128)S(1)} collective-permute-done((f32[256,640]{1,0:T(8,128)S(1)}, f32[256,640]{1,0:T(8,128)S(1)}, u32[]{:S(2)}, u32[]{:S(2)}) %collective-permute-start.16) | collective-permute-done | bytes 655392 | tf_op jit(solution)/shard_map/ppermute | solution.py:343
  102.7 5.6 %collective-permute-done.14.refs_6_ = f32[128,640]{1,0:T(8,128)S(1)} collective-permute-done((f32[128,640]{1,0:T(8,128)S(1)}, f32[128,640]{1,0:T(8,128)S(1)}, u32[]{:S(2)}, u32[]{:S(2)}) %collective-permute-start.14) | collective-permute-done | bytes 327712 | tf_op jit(solution)/shard_map/ppermute | solution.py:346
  109.8 2.4 %collective-permute-done.17 = f32[8,128]{1,0:T(8,128)S(1)} collective-permute-done((f32[8,128]{1,0:T(8,128)S(1)}, f32[8,128]{1,0:T(8,128)S(1)}, u32[]{:S(2)}, u32[]{:S(2)}) %collective-permute-start.17) | collective-permute-done | bytes 4128 | tf_op jit(solution)/shard_map/ppermute | solution.py:340
  112.2 2.5 %collective-permute-start.18 = (f32[8,128]{1,0:T(8,128)S(1)}, f32[8,128]{1,0:T(8,128)S(1)}, u32[]{:S(2)}, u32[]{:S(2)}) collective-permute-start(f32[8,128]{1,0:T(8,128)S(1)} %max.9), channel_id=1, source_target_pairs={{0,4},{2,6},{4,0},{6,2},{8,12},{10,14},{12,8},{14,10},{1,5},{3,7},... | collective-permute-start | bytes 12296 | tf_op jit(solution)/shard_map/ppermute | solution.py:343
  114.7 1.5 %place.1 = f32[640,512]{1,0:T(8,128)} custom-call(f32[512,640]{1,0:T(8,128)S(1)} %get-tuple-element.70.total), custom_call_target="tpu_custom_call" | custom-call | flops 1000 | bytes 1000 | tf_op jit(solution)/shard_map/place/pallas_call | solution.py:322
  116.3 3.0 %collective-permute-start.19 = (f32[8,128]{1,0:T(8,128)S(1)}, f32[8,128]{1,0:T(8,128)S(1)}, u32[]{:S(2)}, u32[]{:S(2)}) collective-permute-start(f32[8,128]{1,0:T(8,128)S(1)} %max.10), channel_id=1, source_target_pairs={{0,8},{2,10},{4,12},{6,14},{8,0},{10,2},{12,4},{14,6},{1,9},{3,11}... | collective-permute-start | bytes 12296 | tf_op jit(solution)/shard_map/ppermute | solution.py:399
  119.3 1.6 %collective-permute-done.19 = f32[8,128]{1,0:T(8,128)S(1)} collective-permute-done((f32[8,128]{1,0:T(8,128)S(1)}, f32[8,128]{1,0:T(8,128)S(1)}, u32[]{:S(2)}, u32[]{:S(2)}) %collective-permute-start.19) | collective-permute-done | bytes 4128 | tf_op jit(solution)/shard_map/ppermute | solution.py:399
  (64 shorter events, 14.3 us)
Async XLA Ops:
  5.4 19.0 %collective-permute-start.2 = (f32[256,640]{1,0:T(8,128)}, f32[256,640]{1,0:T(8,128)}, u32[]{:S(2)}, u32[]{:S(2)}) collective-permute-start(f32[256,640]{1,0:T(8,128)} %get-tuple-element.47), channel_id=1, source_target_pairs={{0,2},{2,0},{4,6},{6,4},{8,10},{10,8},{12,14},{14,12},{1,3},{3,1},... | collective-permute-start | bytes 1966088 | tf_op jit(solution)/shard_map/ppermute | solution.py:340
  8.4 29.8 %collective-permute-start = (f32[384,640]{1,0:T(8,128)}, f32[384,640]{1,0:T(8,128)S(1)}, u32[]{:S(2)}, u32[]{:S(2)}) collective-permute-start(f32[384,640]{1,0:T(8,128)} %get-tuple-element.43), channel_id=1, source_target_pairs={{0,4},{2,6},{4,0},{6,2},{8,12},{10,14},{12,8},{14,10},{1,5},{3,7},... | collective-permute-start | bytes 2949128 | tf_op jit(solution)/shard_map/ppermute | solution.py:343
  13.8 24.4 %collective-permute-start.1 = (f32[256,640]{1,0:T(8,128)}, f32[256,640]{1,0:T(8,128)S(1)}, u32[]{:S(2)}, u32[]{:S(2)}) collective-permute-start(f32[256,640]{1,0:T(8,128)} %get-tuple-element.46), channel_id=1, source_target_pairs={{0,2},{2,0},{4,6},{6,4},{8,10},{10,8},{12,14},{14,12},{1,3},{3,1},... | collective-permute-start | bytes 1966088 | tf_op jit(solution)/shard_map/ppermute | solution.py:340
  15.4 15.7 %copy-start.2 = (bf16[8,96,512]{2,1,0:T(8,128)(2,1)S(1)}, bf16[8,96,512]{2,1,0:T(8,128)(2,1)}, u32[]{:S(2)}) copy-start(bf16[8,96,512]{2,1,0:T(8,128)(2,1)} %refs_4_.3) | copy-start | bytes 2359300
  24.3 9.7 %copy-start.5 = (f32[256,640]{1,0:T(8,128)}, f32[256,640]{1,0:T(8,128)S(1)}, u32[]{:S(2)}) copy-start(f32[256,640]{1,0:T(8,128)S(1)} %get-tuple-element.61) | copy-start | bytes 1966084
  24.3 9.7 %copy-start.7 = (f32[256,640]{1,0:T(8,128)}, f32[256,640]{1,0:T(8,128)S(1)}, u32[]{:S(2)}) copy-start(f32[256,640]{1,0:T(8,128)S(1)} %get-tuple-element.59) | copy-start | bytes 1966084
  24.3 9.7 %copy-start.9 = (f32[256,640]{1,0:T(8,128)}, f32[256,640]{1,0:T(8,128)S(1)}, u32[]{:S(2)}) copy-start(f32[256,640]{1,0:T(8,128)S(1)} %get-tuple-element.42) | copy-start | bytes 1966084
  24.3 9.7 %copy-start.15 = (f32[256,640]{1,0:T(8,128)}, f32[256,640]{1,0:T(8,128)S(1)}, u32[]{:S(2)}) copy-start(f32[256,640]{1,0:T(8,128)S(1)} %get-tuple-element.64) | copy-start | bytes 1966084
  24.3 6.8 %copy-start = (bf16[8,96,512]{2,1,0:T(8,128)(2,1)S(1)}, bf16[8,96,512]{2,1,0:T(8,128)(2,1)}, u32[]{:S(2)}) copy-start(bf16[8,96,512]{2,1,0:T(8,128)(2,1)} %refs_3_.5) | copy-start | bytes 2359300
  24.3 6.8 %copy-start.1 = (bf16[8,8,4096]{2,1,0:T(8,128)(2,1)S(1)}, bf16[8,8,4096]{2,1,0:T(8,128)(2,1)}, u32[]{:S(2)}) copy-start(bf16[8,8,4096]{2,1,0:T(8,128)(2,1)} %refs_2_.5) | copy-start | bytes 1572868
  24.3 6.8 %copy-start.10 = (bf16[8,8,512]{2,1,0:T(8,128)(2,1)S(1)}, bf16[8,8,512]{2,1,0:T(8,128)(2,1)}, u32[]{:S(2)}) copy-start(bf16[8,8,512]{2,1,0:T(8,128)(2,1)} %refs_4_.5) | copy-start | bytes 196612
  24.4 6.8 %copy-start.13 = (bf16[8,8,512]{2,1,0:T(8,128)(2,1)S(1)}, bf16[8,8,512]{2,1,0:T(8,128)(2,1)}, u32[]{:S(2)}) copy-start(bf16[8,8,512]{2,1,0:T(8,128)(2,1)} %refs_5_.3) | copy-start | bytes 196612
  26.3 20.2 %collective-permute-start.6 = (f32[256,640]{1,0:T(8,128)S(1)}, f32[256,640]{1,0:T(8,128)S(1)}, u32[]{:S(2)}, u32[]{:S(2)}) collective-permute-start(f32[256,640]{1,0:T(8,128)S(1)} %add.42), channel_id=1, source_target_pairs={{0,4},{2,6},{12,8},{14,10},{1,5},{3,7},{13,9},{15,11},{16,20},{18,... | collective-permute-start | bytes 1966088 | tf_op jit(solution)/shard_map/ppermute | solution.py:346
  29.5 22.9 %collective-permute-start.5 = (f32[256,640]{1,0:T(8,128)}, f32[256,640]{1,0:T(8,128)}, u32[]{:S(2)}, u32[]{:S(2)}) collective-permute-start(f32[256,640]{1,0:T(8,128)} %get-tuple-element.52), channel_id=1, source_target_pairs={{0,2},{2,0},{4,6},{6,4},{8,10},{10,8},{12,14},{14,12},{1,3},{3,1},... | collective-permute-start | bytes 1966088 | tf_op jit(solution)/shard_map/ppermute | solution.py:340
  39.2 21.4 %collective-permute-start.4 = (f32[256,640]{1,0:T(8,128)}, f32[256,640]{1,0:T(8,128)}, u32[]{:S(2)}, u32[]{:S(2)}) collective-permute-start(f32[256,640]{1,0:T(8,128)} %add.41), channel_id=1, source_target_pairs={{0,4},{2,6},{12,8},{14,10},{1,5},{3,7},{13,9},{15,11},{16,20},{18,... | collective-permute-start | bytes 1966088 | tf_op jit(solution)/shard_map/ppermute | solution.py:346
  44.1 22.4 %collective-permute-start.3 = (f32[256,640]{1,0:T(8,128)}, f32[256,640]{1,0:T(8,128)}, u32[]{:S(2)}, u32[]{:S(2)}) collective-permute-start(f32[256,640]{1,0:T(8,128)} %get-tuple-element.49), channel_id=1, source_target_pairs={{0,2},{2,0},{4,6},{6,4},{8,10},{10,8},{12,14},{14,12},{1,3},{3,1},... | collective-permute-start | bytes 1966088 | tf_op jit(solution)/shard_map/ppermute | solution.py:340
  47.4 19.1 %collective-permute-start.10 = (f32[256,640]{1,0:T(8,128)}, f32[256,640]{1,0:T(8,128)}, u32[]{:S(2)}, u32[]{:S(2)}) collective-permute-start(f32[256,640]{1,0:T(8,128)} %add.46), channel_id=1, source_target_pairs={{4,8},{6,10},{8,4},{10,6},{5,9},{7,11},{9,5},{11,7},{20,24},{22,26... | collective-permute-start | bytes 1966088 | tf_op jit(solution)/shard_map/ppermute | solution.py:352
  53.6 12.9 %copy-start.6 = (f32[256,640]{1,0:T(8,128)S(1)}, f32[256,640]{1,0:T(8,128)}, u32[]{:S(2)}) copy-start(f32[256,640]{1,0:T(8,128)} %copy-done.5) | copy-start | bytes 1966084
  53.6 26.8 %collective-permute-start.12 = (f32[256,640]{1,0:T(8,128)S(1)}, f32[256,640]{1,0:T(8,128)S(1)}, u32[]{:S(2)}, u32[]{:S(2)}) collective-permute-start(f32[256,640]{1,0:T(8,128)S(1)} %copy-done.16), channel_id=1, source_target_pairs={{0,2},{2,0},{4,6},{6,4},{8,10},{10,8},{12,14},{14,12},{1,3},{3,1},... | collective-permute-start | bytes 1966088 | tf_op jit(solution)/shard_map/ppermute | solution.py:340
  55.7 18.8 %collective-permute-start.8 = (f32[256,640]{1,0:T(8,128)S(1)}, f32[256,640]{1,0:T(8,128)S(1)}, u32[]{:S(2)}, u32[]{:S(2)}) collective-permute-start(f32[256,640]{1,0:T(8,128)S(1)} %add.43), channel_id=1, source_target_pairs={{0,4},{2,6},{12,8},{14,10},{1,5},{3,7},{13,9},{15,11},{16,20},{18,... | collective-permute-start | bytes 1966088 | tf_op jit(solution)/shard_map/ppermute | solution.py:346
  62.0 18.4 %collective-permute-start.15 = (f32[256,640]{1,0:T(8,128)S(1)}, f32[256,640]{1,0:T(8,128)S(1)}, u32[]{:S(2)}, u32[]{:S(2)}) collective-permute-start(f32[256,640]{1,0:T(8,128)S(1)} %add.50), channel_id=1, source_target_pairs={{4,8},{6,10},{8,4},{10,6},{5,9},{7,11},{9,5},{11,7},{20,24},{22,26... | collective-permute-start | bytes 1966088 | tf_op jit(solution)/shard_map/ppermute | solution.py:352
  68.0 20.6 %collective-permute-start.11 = (f32[256,640]{1,0:T(8,128)S(1)}, f32[256,640]{1,0:T(8,128)S(1)}, u32[]{:S(2)}, u32[]{:S(2)}) collective-permute-start(f32[256,640]{1,0:T(8,128)S(1)} %get-tuple-element.73), channel_id=1, source_target_pairs={{0,4},{2,6},{4,0},{6,2},{8,12},{10,14},{12,8},{14,10},{1,5},{3,7},... | collective-permute-start | bytes 1966088 | tf_op jit(solution)/shard_map/ppermute | solution.py:343
  70.2 38.0 %collective-permute-start.7 = (f32[512,640]{1,0:T(8,128)S(1)}, f32[512,640]{1,0:T(8,128)S(1)}, u32[]{:S(2)}, u32[]{:S(2)}) collective-permute-start(f32[512,640]{1,0:T(8,128)S(1)} %pad_maximum_fusion), channel_id=1, source_target_pairs={{0,2},{2,0},{4,6},{6,4},{8,10},{10,8},{12,14},{14,12},{1,3},{3,1},... | collective-permute-start | bytes 3932168 | tf_op jit(solution)/shard_map/ppermute | solution.py:340
  74.7 14.9 %collective-permute-start.9 = (f32[256,640]{1,0:T(8,128)S(1)}, f32[256,640]{1,0:T(8,128)S(1)}, u32[]{:S(2)}, u32[]{:S(2)}) collective-permute-start(f32[256,640]{1,0:T(8,128)S(1)} %add.44), channel_id=1, source_target_pairs={{4,8},{6,10},{8,4},{10,6},{5,9},{7,11},{9,5},{11,7},{20,24},{22,26... | collective-permute-start | bytes 1966088 | tf_op jit(solution)/shard_map/ppermute | solution.py:352
  80.5 22.1 %collective-permute-start.16 = (f32[256,640]{1,0:T(8,128)S(1)}, f32[256,640]{1,0:T(8,128)S(1)}, u32[]{:S(2)}, u32[]{:S(2)}) collective-permute-start(f32[256,640]{1,0:T(8,128)S(1)} %add_add_fusion), channel_id=1, source_target_pairs={{0,4},{2,6},{4,0},{6,2},{8,12},{10,14},{12,8},{14,10},{1,5},{3,7},... | collective-permute-start | bytes 1966088 | tf_op jit(solution)/shard_map/ppermute | solution.py:343
  88.6 19.6 %copy-start.3 = (f32[256,640]{1,0:T(8,128)S(1)}, f32[256,640]{1,0:T(8,128)}, u32[]{:S(2)}) copy-start(f32[256,640]{1,0:T(8,128)} %get-tuple-element.40.refs_0_) | copy-start | bytes 1966084
  88.6 19.6 %copy-start.4 = (f32[256,640]{1,0:T(8,128)S(1)}, f32[256,640]{1,0:T(8,128)}, u32[]{:S(2)}) copy-start(f32[256,640]{1,0:T(8,128)} %get-tuple-element.41.refs_1_) | copy-start | bytes 1966084
  88.7 19.5 %collective-permute-start.13 = (f32[256,640]{1,0:T(8,128)S(1)}, f32[256,640]{1,0:T(8,128)S(1)}, u32[]{:S(2)}, u32[]{:S(2)}) collective-permute-start(f32[256,640]{1,0:T(8,128)S(1)} %add.48), channel_id=1, source_target_pairs={{4,8},{6,10},{8,4},{10,6},{5,9},{7,11},{9,5},{11,7},{20,24},{22,26... | collective-permute-start | bytes 1966088 | tf_op jit(solution)/shard_map/ppermute | solution.py:352
  89.6 18.6 %collective-permute-start.14 = (f32[128,640]{1,0:T(8,128)S(1)}, f32[128,640]{1,0:T(8,128)S(1)}, u32[]{:S(2)}, u32[]{:S(2)}) collective-permute-start(f32[128,640]{1,0:T(8,128)S(1)} %slice.10), channel_id=1, source_target_pairs={{0,4},{2,6},{12,8},{14,10},{1,5},{3,7},{13,9},{15,11},{16,20},{18,... | collective-permute-start | bytes 983048 | tf_op jit(solution)/shard_map/ppermute | solution.py:346
  108.6 3.6 %collective-permute-start.17 = (f32[8,128]{1,0:T(8,128)S(1)}, f32[8,128]{1,0:T(8,128)S(1)}, u32[]{:S(2)}, u32[]{:S(2)}) collective-permute-start(f32[8,128]{1,0:T(8,128)S(1)} %get-tuple-element.69), channel_id=1, source_target_pairs={{0,2},{2,0},{4,6},{6,4},{8,10},{10,8},{12,14},{14,12},{1,3},{3,1},... | collective-permute-start | bytes 12296 | tf_op jit(solution)/shard_map/ppermute | solution.py:340
  112.2 4.1 %collective-permute-start.18 = (f32[8,128]{1,0:T(8,128)S(1)}, f32[8,128]{1,0:T(8,128)S(1)}, u32[]{:S(2)}, u32[]{:S(2)}) collective-permute-start(f32[8,128]{1,0:T(8,128)S(1)} %max.9), channel_id=1, source_target_pairs={{0,4},{2,6},{4,0},{6,2},{8,12},{10,14},{12,8},{14,10},{1,5},{3,7},... | collective-permute-start | bytes 12296 | tf_op jit(solution)/shard_map/ppermute | solution.py:343
  116.3 4.6 %collective-permute-start.19 = (f32[8,128]{1,0:T(8,128)S(1)}, f32[8,128]{1,0:T(8,128)S(1)}, u32[]{:S(2)}, u32[]{:S(2)}) collective-permute-start(f32[8,128]{1,0:T(8,128)S(1)} %max.10), channel_id=1, source_target_pairs={{0,8},{2,10},{4,12},{6,14},{8,0},{10,2},{12,4},{14,6},{1,9},{3,11}... | collective-permute-start | bytes 12296 | tf_op jit(solution)/shard_map/ppermute | solution.py:399
  (5 other events, 20.8 us)

commit v6 on v5

--- a/solution.py
+++ b/solution.py
@@ -357,6 +357,9 @@
     def after(x, *others):
         return together(x, *others)[0]
 
+    def planes(x, hop):
+        return lax.ppermute(x, "dp", [(r, r ^ hop) for r in range(dp)])
+
     def make(*jobs):
         return chunks(jobs, features, halves, width)
 
@@ -394,9 +397,9 @@
     e6 = pair(ownpb + y4 + m4)
     m6 = middle(own2b + y3 + e5)
     total, peaks = add_parts([ownoa, ownob, y5, m5, m6, e0, late, e5, e6])
-    peaks = jnp.maximum(peaks, across(peaks))
-    peaks, grad = together(jnp.maximum(peaks, pair(peaks)), place(total))
-    peaks = jnp.maximum(peaks, lax.ppermute(peaks, "dp", [(r, r ^ 4) for r in range(dp)]))
+    peaks, grad = together(jnp.maximum(peaks, across(peaks)), place(total))
+    near, far, middle_peaks = [planes(peaks, hop) for hop in (2, 4, 6)]
+    peaks = jnp.maximum(jnp.maximum(peaks, near), jnp.maximum(far, middle_peaks))
     return attended, grad, peaks[0, : columns // BUCKET]
 
 

time: 122 us -> 121 us (level)
    ppermute x4 -> x3, starting transfers between devices: 8.41 us -> 5.92 us  [pair(): return lax.ppermute(x, 'dp', [(r, r ^ 2) for r in range(dp)])]
    ppermute x1 -> x3, waiting for transfers between devices: 1.58 us -> 3.37 us  [planes(): return lax.ppermute(x, 'dp', [(r, r ^ hop) for r in range(dp)])]
    ppermute x7, waiting for transfers between devices: 17.8 us -> 16.3 us  [across(): return lax.ppermute(x, 'dp', [(r, r ^ 1) for r in range(dp)])]
    ppermute x1 -> x3, starting transfers between devices: 3.04 us -> 4.39 us  [planes(): return lax.ppermute(x, 'dp', [(r, r ^ hop) for r in range(dp)])]
    ppermute x4 -> x3, waiting for transfers between devices: 11.4 us -> 11.3 us  [pair(): return lax.ppermute(x, 'dp', [(r, r ^ 2) for r in range(dp)])]
  transfers between devices with their start and end apart: 20 -> 21, of which waited for: 13 -> 13; matrix products, arithmetic and copies ran while one was open for 8% -> 8% of each run, Pallas kernels for 14% -> 14%
where the time goes in v6:
time: 121 us; the launch traced here: 120 us
  starting transfers between devices  45 us (37%)
  waiting for transfers between devices  41.5 us (34%)
  Pallas kernels  22.1 us (18%)
  other arithmetic  9.37 us (8%)
  local copies, waits for them, and re-layouts  1.63 us (1%)
    ppermute x4, starting transfers between devices, outward(): return lax.ppermute(x, 'dp', [(r, r ^ 2) for r in (0, 1, 6, 7)])  19.3 us
    ppermute x7, waiting for transfers between devices, across(): return lax.ppermute(x, 'dp', [(r, r ^ 1) for r in range(dp)])  16.3 us
    ppermute x7, starting transfers between devices, across(): return lax.ppermute(x, 'dp', [(r, r ^ 1) for r in range(dp)])  11.6 us
    ppermute x3, waiting for transfers between devices, pair(): return lax.ppermute(x, 'dp', [(r, r ^ 2) for r in range(dp)])  11.3 us
    ppermute x4, waiting for transfers between devices, outward(): return lax.ppermute(x, 'dp', [(r, r ^ 2) for r in (0, 1, 6, 7)])  10.6 us
    pallas_call x1, Pallas kernels, chunks(): pl.pallas_call(functools.partial(chunk_kernel, jobs), in_specs=[HBM, vmem...  8.85 us
    pallas_call x2, Pallas kernels, begin(): pl.pallas_call(functools.partial(begin_kernel, half, jobs), in_specs=[HBM...  8.59 us
    ppermute x3, starting transfers between devices, pair(): return lax.ppermute(x, 'dp', [(r, r ^ 2) for r in range(dp)])  5.92 us
  transfers between devices with their start and end apart: 21, of which 13 were waited for; matrix products, arithmetic and copies ran while one was open for 8% of the time, Pallas kernels for 14%

profile of v6, /device:TPU:0, one launch (start us, length us, event | category | flops | bytes accessed | tf_op | source)
XLA Modules:
  0.0 120.5 jit_solution(6167042287162312693)
XLA Ops:
  0.6 4.8 %value_cot.2 = (bf16[256,832]{1,0:T(8,128)(2,1)}, f32[384,640]{1,0:T(8,128)}, f32[256,640]{1,0:T(8,128)}) custom-call(s32[8]{0:T(128)} %refs_0_.5, f32[8]{0:T(128)} %refs_1_.5, bf16[8,8,4096]{2,1,0:T(8,128)(2,1)} %refs_2_.5, bf16[8,96,512]{2,1,0:T(8,128)(2,1)} %refs_3_.5, bf16[8,8,512]{2,1,0:T(8,128)(2,1)} %refs_4_.5, bf16[8,8,4096]{2,1,0:T(8,128)(2,1)} %refs_5_.5, ...), custom_call_target="tpu_custom_call" | custom-call | flops 1000 | bytes 1000 | tf_op jit(solution)/shard_map/value_cot/pallas_call | solution.py:201
  5.4 3.0 %collective-permute-start.2 = (f32[256,640]{1,0:T(8,128)}, f32[256,640]{1,0:T(8,128)}, u32[]{:S(2)}, u32[]{:S(2)}) collective-permute-start(f32[256,640]{1,0:T(8,128)} %get-tuple-element.47), channel_id=1, source_target_pairs={{0,2},{2,0},{4,6},{6,4},{8,10},{10,8},{12,14},{14,12},{1,3},{3,1},... | collective-permute-start | bytes 1966088 | tf_op jit(solution)/shard_map/ppermute | solution.py:340
  8.4 1.6 %collective-permute-start = (f32[384,640]{1,0:T(8,128)}, f32[384,640]{1,0:T(8,128)S(1)}, u32[]{:S(2)}, u32[]{:S(2)}) collective-permute-start(f32[384,640]{1,0:T(8,128)} %get-tuple-element.43), channel_id=1, source_target_pairs={{0,4},{2,6},{4,0},{6,2},{8,12},{10,14},{12,8},{14,10},{1,5},{3,7},... | collective-permute-start | bytes 2949128 | tf_op jit(solution)/shard_map/ppermute | solution.py:343
  10.0 3.8 %value_cot.3 = (bf16[256,832]{1,0:T(8,128)(2,1)}, f32[256,640]{1,0:T(8,128)}) custom-call(s32[8]{0:T(128)} %refs_0_.5, f32[8]{0:T(128)} %refs_1_.5, bf16[8,8,4096]{2,1,0:T(8,128)(2,1)} %refs_2_.5, bf16[8,96,512]{2,1,0:T(8,128)(2,1)} %refs_3_.5, bf16[8,8,512]{2,1,0:T(8,128)(2,1)} %refs_4_.5, bf16[8,8,4096]{2,1,0:T(8,128)(2,1)} %refs_5_.5, ...), custom_call_target="tpu_custom_call" | custom-call | flops 1000 | bytes 1000 | tf_op jit(solution)/shard_map/value_cot/pallas_call | solution.py:201
  15.4 8.8 %chunk.1 = (f32[256,640]{1,0:T(8,128)S(1)}, f32[256,640]{1,0:T(8,128)S(1)}, f32[256,640]{1,0:T(8,128)}, f32[256,640]{1,0:T(8,128)}, f32[256,640]{1,0:T(8,128)S(1...) custom-call(bf16[832,5120]{1,0:T(8,128)(2,1)} %bitcast.5, ...), custom_call_target="tpu_custom_call" | custom-call | flops 1000 | bytes 1000 | tf_op jit(solution)/shard_map/chunk/pallas_call | solution.py:265
  24.4 1.9 %add.42 = f32[256,640]{1,0:T(8,128)S(1)} add(f32[256,640]{1,0:T(8,128)S(1)} %get-tuple-element.53, f32[256,640]{1,0:T(8,128)} %collective-permute-done.2) | non-fusion elementwise | flops 163840 | bytes 1966080 | tf_op jit(solution)/shard_map/add | solution.py:385
  26.3 3.2 %collective-permute-start.6 = (f32[256,640]{1,0:T(8,128)S(1)}, f32[256,640]{1,0:T(8,128)S(1)}, u32[]{:S(2)}, u32[]{:S(2)}) collective-permute-start(f32[256,640]{1,0:T(8,128)S(1)} %add.42), channel_id=1, source_target_pairs={{0,4},{2,6},{12,8},{14,10},{1,5},{3,7},{13,9},{15,11},{16,20},{18,... | collective-permute-start | bytes 1966088 | tf_op jit(solution)/shard_map/ppermute | solution.py:346
  29.5 1.6 %collective-permute-start.5 = (f32[256,640]{1,0:T(8,128)}, f32[256,640]{1,0:T(8,128)}, u32[]{:S(2)}, u32[]{:S(2)}) collective-permute-start(f32[256,640]{1,0:T(8,128)} %get-tuple-element.52), channel_id=1, source_target_pairs={{0,2},{2,0},{4,6},{6,4},{8,10},{10,8},{12,14},{14,12},{1,3},{3,1},... | collective-permute-start | bytes 1966088 | tf_op jit(solution)/shard_map/ppermute | solution.py:340
  31.2 2.8 %attend.1 = bf16[8,8,4096]{2,1,0:T(8,128)(2,1)} custom-call(s32[8]{0:T(128)S(1)} %copy-done.14, bf16[8,8,4096]{2,1,0:T(8,128)(2,1)S(1)} %copy-done.1, bf16[8,96,512]{2,1,0:T(8,128)(2,1)S(1)} %copy-done, bf16[8,8,512]{2,1,0:T(8,128)(2,1)S(1)} %copy-done.10, bf16[8,96,512]{2,1,0:T(8,128)(2,1)S(1)} %copy-done.2, bf16[8,8,512]{2,1,0:T(8,128)(2,1)S(1)} %copy-done.13), custom_call_target="tpu_custom_call" | custom-call | flops 1000 | bytes 1000 | tf_op jit(solution)/shard_map/attend/pallas_call | solution.py:230
  34.0 4.2 %collective-permute-done.1 = f32[256,640]{1,0:T(8,128)S(1)} collective-permute-done((f32[256,640]{1,0:T(8,128)}, f32[256,640]{1,0:T(8,128)S(1)}, u32[]{:S(2)}, u32[]{:S(2)}) %collective-permute-start.1) | collective-permute-done | bytes 655392 | tf_op jit(solution)/shard_map/ppermute | solution.py:340
  39.2 4.9 %collective-permute-start.4 = (f32[256,640]{1,0:T(8,128)}, f32[256,640]{1,0:T(8,128)}, u32[]{:S(2)}, u32[]{:S(2)}) collective-permute-start(f32[256,640]{1,0:T(8,128)} %add.41), channel_id=1, source_target_pairs={{0,4},{2,6},{12,8},{14,10},{1,5},{3,7},{13,9},{15,11},{16,20},{18,... | collective-permute-start | bytes 1966088 | tf_op jit(solution)/shard_map/ppermute | solution.py:346
  44.1 1.5 %collective-permute-start.3 = (f32[256,640]{1,0:T(8,128)}, f32[256,640]{1,0:T(8,128)}, u32[]{:S(2)}, u32[]{:S(2)}) collective-permute-start(f32[256,640]{1,0:T(8,128)} %get-tuple-element.49), channel_id=1, source_target_pairs={{0,2},{2,0},{4,6},{6,4},{8,10},{10,8},{12,14},{14,12},{1,3},{3,1},... | collective-permute-start | bytes 1966088 | tf_op jit(solution)/shard_map/ppermute | solution.py:340
  47.4 1.5 %collective-permute-start.10 = (f32[256,640]{1,0:T(8,128)}, f32[256,640]{1,0:T(8,128)}, u32[]{:S(2)}, u32[]{:S(2)}) collective-permute-start(f32[256,640]{1,0:T(8,128)} %add.46), channel_id=1, source_target_pairs={{4,8},{6,10},{8,4},{10,6},{5,9},{7,11},{9,5},{11,7},{20,24},{22,26... | collective-permute-start | bytes 1966088 | tf_op jit(solution)/shard_map/ppermute | solution.py:352
  50.1 2.3 %collective-permute-done.5 = f32[256,640]{1,0:T(8,128)} collective-permute-done((f32[256,640]{1,0:T(8,128)}, f32[256,640]{1,0:T(8,128)}, u32[]{:S(2)}, u32[]{:S(2)}) %collective-permute-start.5) | collective-permute-done | bytes 655392 | tf_op jit(solution)/shard_map/ppermute | solution.py:340
  53.6 2.1 %collective-permute-start.12 = (f32[256,640]{1,0:T(8,128)S(1)}, f32[256,640]{1,0:T(8,128)S(1)}, u32[]{:S(2)}, u32[]{:S(2)}) collective-permute-start(f32[256,640]{1,0:T(8,128)S(1)} %copy-done.16), channel_id=1, source_target_pairs={{0,2},{2,0},{4,6},{6,4},{8,10},{10,8},{12,14},{14,12},{1,3},{3,1},... | collective-permute-start | bytes 1966088 | tf_op jit(solution)/shard_map/ppermute | solution.py:340
  55.7 3.5 %collective-permute-start.8 = (f32[256,640]{1,0:T(8,128)S(1)}, f32[256,640]{1,0:T(8,128)S(1)}, u32[]{:S(2)}, u32[]{:S(2)}) collective-permute-start(f32[256,640]{1,0:T(8,128)S(1)} %add.43), channel_id=1, source_target_pairs={{0,4},{2,6},{12,8},{14,10},{1,5},{3,7},{13,9},{15,11},{16,20},{18,... | collective-permute-start | bytes 1966088 | tf_op jit(solution)/shard_map/ppermute | solution.py:346
  59.2 1.4 %collective-permute-done.4 = f32[256,640]{1,0:T(8,128)} collective-permute-done((f32[256,640]{1,0:T(8,128)}, f32[256,640]{1,0:T(8,128)}, u32[]{:S(2)}, u32[]{:S(2)}) %collective-permute-start.4) | collective-permute-done | bytes 655392 | tf_op jit(solution)/shard_map/ppermute | solution.py:346
  60.6 1.4 %add.50 = f32[256,640]{1,0:T(8,128)S(1)} add(f32[256,640]{1,0:T(8,128)} %add.41, f32[256,640]{1,0:T(8,128)} %collective-permute-done.4) | non-fusion elementwise | flops 163840 | bytes 1966080 | tf_op jit(solution)/shard_map/add | solution.py:391
  62.7 3.8 %collective-permute-done.3 = f32[256,640]{1,0:T(8,128)} collective-permute-done((f32[256,640]{1,0:T(8,128)}, f32[256,640]{1,0:T(8,128)}, u32[]{:S(2)}, u32[]{:S(2)}) %collective-permute-start.3) | collective-permute-done | bytes 655392 | tf_op jit(solution)/shard_map/ppermute | solution.py:340
  66.5 1.5 %add_select_fusion = (f32[256,640]{1,0:T(8,128)S(1)}, f32[256,640]{1,0:T(8,128)S(1)}) fusion(f32[256,640]{1,0:T(8,128)S(1)} %get-tuple-element.62, f32[256,640]{1,0:T(8,128)} %collective-permute-done.10, pred[]{:T(512)S(6)} %or.3, f32[256,640]{1,0:T(8,128)S(1)} %copy-done.6, f32[256,640]{1,0:T(8,128)} %collective-permute-done.3), kind=kLoop, calls=%fused_computation.3 | loop fusion | flops 491520 | bytes 3932161 | tf_op jit(solution)/shard_map/jit(_where)/select_n | solution.py:393
  68.0 2.2 %collective-permute-start.11 = (f32[256,640]{1,0:T(8,128)S(1)}, f32[256,640]{1,0:T(8,128)S(1)}, u32[]{:S(2)}, u32[]{:S(2)}) collective-permute-start(f32[256,640]{1,0:T(8,128)S(1)} %get-tuple-element.73), channel_id=1, source_target_pairs={{0,4},{2,6},{4,0},{6,2},{8,12},{10,14},{12,8},{14,10},{1,5},{3,7},... | collective-permute-start | bytes 1966088 | tf_op jit(solution)/shard_map/ppermute | solution.py:343
  70.2 1.6 %collective-permute-start.7 = (f32[512,640]{1,0:T(8,128)S(1)}, f32[512,640]{1,0:T(8,128)S(1)}, u32[]{:S(2)}, u32[]{:S(2)}) collective-permute-start(f32[512,640]{1,0:T(8,128)S(1)} %pad_maximum_fusion), channel_id=1, source_target_pairs={{0,2},{2,0},{4,6},{6,4},{8,10},{10,8},{12,14},{14,12},{1,3},{3,1},... | collective-permute-start | bytes 3932168 | tf_op jit(solution)/shard_map/ppermute | solution.py:340
  71.8 2.7 %collective-permute-done.8 = f32[256,640]{1,0:T(8,128)S(1)} collective-permute-done((f32[256,640]{1,0:T(8,128)S(1)}, f32[256,640]{1,0:T(8,128)S(1)}, u32[]{:S(2)}, u32[]{:S(2)}) %collective-permute-start.8) | collective-permute-done | bytes 655392 | tf_op jit(solution)/shard_map/ppermute | solution.py:346
  75.4 5.0 %collective-permute-done.12 = f32[256,640]{1,0:T(8,128)S(1)} collective-permute-done((f32[256,640]{1,0:T(8,128)S(1)}, f32[256,640]{1,0:T(8,128)S(1)}, u32[]{:S(2)}, u32[]{:S(2)}) %collective-permute-start.12) | collective-permute-done | bytes 655392 | tf_op jit(solution)/shard_map/ppermute | solution.py:340
  80.5 2.2 %collective-permute-start.16 = (f32[256,640]{1,0:T(8,128)S(1)}, f32[256,640]{1,0:T(8,128)S(1)}, u32[]{:S(2)}, u32[]{:S(2)}) collective-permute-start(f32[256,640]{1,0:T(8,128)S(1)} %add_add_fusion), channel_id=1, source_target_pairs={{0,4},{2,6},{4,0},{6,2},{8,12},{10,14},{12,8},{14,10},{1,5},{3,7},... | collective-permute-start | bytes 1966088 | tf_op jit(solution)/shard_map/ppermute | solution.py:343
  82.7 5.9 %collective-permute-done.11.refs_7_ = f32[256,640]{1,0:T(8,128)S(1)} collective-permute-done((f32[256,640]{1,0:T(8,128)S(1)}, f32[256,640]{1,0:T(8,128)S(1)}, u32[]{:S(2)}, u32[]{:S(2)}) %collective-permute-start.11) | collective-permute-done | bytes 655392 | tf_op jit(solution)/shard_map/ppermute | solution.py:343
  89.6 7.7 %collective-permute-start.14 = (f32[128,640]{1,0:T(8,128)S(1)}, f32[128,640]{1,0:T(8,128)S(1)}, u32[]{:S(2)}, u32[]{:S(2)}) collective-permute-start(f32[128,640]{1,0:T(8,128)S(1)} %slice.10), channel_id=1, source_target_pairs={{0,4},{2,6},{12,8},{14,10},{1,5},{3,7},{13,9},{15,11},{16,20},{18,... | collective-permute-start | bytes 983048 | tf_op jit(solution)/shard_map/ppermute | solution.py:346
  97.3 5.4 %collective-permute-done.16.refs_8_ = f32[256,640]{1,0:T(8,128)S(1)} collective-permute-done((f32[256,640]{1,0:T(8,128)S(1)}, f32[256,640]{1,0:T(8,128)S(1)}, u32[]{:S(2)}, u32[]{:S(2)}) %collective-permute-start.16) | collective-permute-done | bytes 655392 | tf_op jit(solution)/shard_map/ppermute | solution.py:343
  102.6 5.6 %collective-permute-done.14.refs_6_ = f32[128,640]{1,0:T(8,128)S(1)} collective-permute-done((f32[128,640]{1,0:T(8,128)S(1)}, f32[128,640]{1,0:T(8,128)S(1)}, u32[]{:S(2)}, u32[]{:S(2)}) %collective-permute-start.14) | collective-permute-done | bytes 327712 | tf_op jit(solution)/shard_map/ppermute | solution.py:346
  109.8 1.5 %place.1 = f32[640,512]{1,0:T(8,128)} custom-call(f32[512,640]{1,0:T(8,128)S(1)} %get-tuple-element.70.total), custom_call_target="tpu_custom_call" | custom-call | flops 1000 | bytes 1000 | tf_op jit(solution)/shard_map/place/pallas_call | solution.py:322
  112.2 3.3 %collective-permute-start.20 = (f32[8,128]{1,0:T(8,128)S(1)}, f32[8,128]{1,0:T(8,128)S(1)}, u32[]{:S(2)}, u32[]{:S(2)}) collective-permute-start(f32[8,128]{1,0:T(8,128)S(1)} %max.12), channel_id=1, source_target_pairs={{0,12},{2,14},{4,8},{6,10},{8,4},{10,6},{12,0},{14,2},{1,13},{3,15... | collective-permute-start | bytes 12296 | tf_op jit(solution)/shard_map/ppermute | solution.py:361
  117.6 2.4 %collective-permute-done.19 = f32[8,128]{1,0:T(8,128)S(1)} collective-permute-done((f32[8,128]{1,0:T(8,128)S(1)}, f32[8,128]{1,0:T(8,128)S(1)}, u32[]{:S(2)}, u32[]{:S(2)}) %collective-permute-start.19) | collective-permute-done | bytes 4128 | tf_op jit(solution)/shard_map/ppermute | solution.py:361
  (65 shorter events, 14.6 us)
Async XLA Ops:
  5.4 19.0 %collective-permute-start.2 = (f32[256,640]{1,0:T(8,128)}, f32[256,640]{1,0:T(8,128)}, u32[]{:S(2)}, u32[]{:S(2)}) collective-permute-start(f32[256,640]{1,0:T(8,128)} %get-tuple-element.47), channel_id=1, source_target_pairs={{0,2},{2,0},{4,6},{6,4},{8,10},{10,8},{12,14},{14,12},{1,3},{3,1},... | collective-permute-start | bytes 1966088 | tf_op jit(solution)/shard_map/ppermute | solution.py:340
  8.4 29.8 %collective-permute-start = (f32[384,640]{1,0:T(8,128)}, f32[384,640]{1,0:T(8,128)S(1)}, u32[]{:S(2)}, u32[]{:S(2)}) collective-permute-start(f32[384,640]{1,0:T(8,128)} %get-tuple-element.43), channel_id=1, source_target_pairs={{0,4},{2,6},{4,0},{6,2},{8,12},{10,14},{12,8},{14,10},{1,5},{3,7},... | collective-permute-start | bytes 2949128 | tf_op jit(solution)/shard_map/ppermute | solution.py:343
  13.8 24.4 %collective-permute-start.1 = (f32[256,640]{1,0:T(8,128)}, f32[256,640]{1,0:T(8,128)S(1)}, u32[]{:S(2)}, u32[]{:S(2)}) collective-permute-start(f32[256,640]{1,0:T(8,128)} %get-tuple-element.46), channel_id=1, source_target_pairs={{0,2},{2,0},{4,6},{6,4},{8,10},{10,8},{12,14},{14,12},{1,3},{3,1},... | collective-permute-start | bytes 1966088 | tf_op jit(solution)/shard_map/ppermute | solution.py:340
  15.4 15.7 %copy-start.2 = (bf16[8,96,512]{2,1,0:T(8,128)(2,1)S(1)}, bf16[8,96,512]{2,1,0:T(8,128)(2,1)}, u32[]{:S(2)}) copy-start(bf16[8,96,512]{2,1,0:T(8,128)(2,1)} %refs_4_.3) | copy-start | bytes 2359300
  24.3 9.7 %copy-start.5 = (f32[256,640]{1,0:T(8,128)}, f32[256,640]{1,0:T(8,128)S(1)}, u32[]{:S(2)}) copy-start(f32[256,640]{1,0:T(8,128)S(1)} %get-tuple-element.61) | copy-start | bytes 1966084
  24.3 9.7 %copy-start.7 = (f32[256,640]{1,0:T(8,128)}, f32[256,640]{1,0:T(8,128)S(1)}, u32[]{:S(2)}) copy-start(f32[256,640]{1,0:T(8,128)S(1)} %get-tuple-element.59) | copy-start | bytes 1966084
  24.3 9.7 %copy-start.9 = (f32[256,640]{1,0:T(8,128)}, f32[256,640]{1,0:T(8,128)S(1)}, u32[]{:S(2)}) copy-start(f32[256,640]{1,0:T(8,128)S(1)} %get-tuple-element.42) | copy-start | bytes 1966084
  24.3 9.7 %copy-start.15 = (f32[256,640]{1,0:T(8,128)}, f32[256,640]{1,0:T(8,128)S(1)}, u32[]{:S(2)}) copy-start(f32[256,640]{1,0:T(8,128)S(1)} %get-tuple-element.64) | copy-start | bytes 1966084
  24.3 6.8 %copy-start = (bf16[8,96,512]{2,1,0:T(8,128)(2,1)S(1)}, bf16[8,96,512]{2,1,0:T(8,128)(2,1)}, u32[]{:S(2)}) copy-start(bf16[8,96,512]{2,1,0:T(8,128)(2,1)} %refs_3_.5) | copy-start | bytes 2359300
  24.4 6.8 %copy-start.1 = (bf16[8,8,4096]{2,1,0:T(8,128)(2,1)S(1)}, bf16[8,8,4096]{2,1,0:T(8,128)(2,1)}, u32[]{:S(2)}) copy-start(bf16[8,8,4096]{2,1,0:T(8,128)(2,1)} %refs_2_.5) | copy-start | bytes 1572868
  24.4 6.8 %copy-start.10 = (bf16[8,8,512]{2,1,0:T(8,128)(2,1)S(1)}, bf16[8,8,512]{2,1,0:T(8,128)(2,1)}, u32[]{:S(2)}) copy-start(bf16[8,8,512]{2,1,0:T(8,128)(2,1)} %refs_4_.5) | copy-start | bytes 196612
  26.3 20.1 %collective-permute-start.6 = (f32[256,640]{1,0:T(8,128)S(1)}, f32[256,640]{1,0:T(8,128)S(1)}, u32[]{:S(2)}, u32[]{:S(2)}) collective-permute-start(f32[256,640]{1,0:T(8,128)S(1)} %add.42), channel_id=1, source_target_pairs={{0,4},{2,6},{12,8},{14,10},{1,5},{3,7},{13,9},{15,11},{16,20},{18,... | collective-permute-start | bytes 1966088 | tf_op jit(solution)/shard_map/ppermute | solution.py:346
  29.5 22.9 %collective-permute-start.5 = (f32[256,640]{1,0:T(8,128)}, f32[256,640]{1,0:T(8,128)}, u32[]{:S(2)}, u32[]{:S(2)}) collective-permute-start(f32[256,640]{1,0:T(8,128)} %get-tuple-element.52), channel_id=1, source_target_pairs={{0,2},{2,0},{4,6},{6,4},{8,10},{10,8},{12,14},{14,12},{1,3},{3,1},... | collective-permute-start | bytes 1966088 | tf_op jit(solution)/shard_map/ppermute | solution.py:340
  39.2 21.4 %collective-permute-start.4 = (f32[256,640]{1,0:T(8,128)}, f32[256,640]{1,0:T(8,128)}, u32[]{:S(2)}, u32[]{:S(2)}) collective-permute-start(f32[256,640]{1,0:T(8,128)} %add.41), channel_id=1, source_target_pairs={{0,4},{2,6},{12,8},{14,10},{1,5},{3,7},{13,9},{15,11},{16,20},{18,... | collective-permute-start | bytes 1966088 | tf_op jit(solution)/shard_map/ppermute | solution.py:346
  44.1 22.4 %collective-permute-start.3 = (f32[256,640]{1,0:T(8,128)}, f32[256,640]{1,0:T(8,128)}, u32[]{:S(2)}, u32[]{:S(2)}) collective-permute-start(f32[256,640]{1,0:T(8,128)} %get-tuple-element.49), channel_id=1, source_target_pairs={{0,2},{2,0},{4,6},{6,4},{8,10},{10,8},{12,14},{14,12},{1,3},{3,1},... | collective-permute-start | bytes 1966088 | tf_op jit(solution)/shard_map/ppermute | solution.py:340
  47.4 19.1 %collective-permute-start.10 = (f32[256,640]{1,0:T(8,128)}, f32[256,640]{1,0:T(8,128)}, u32[]{:S(2)}, u32[]{:S(2)}) collective-permute-start(f32[256,640]{1,0:T(8,128)} %add.46), channel_id=1, source_target_pairs={{4,8},{6,10},{8,4},{10,6},{5,9},{7,11},{9,5},{11,7},{20,24},{22,26... | collective-permute-start | bytes 1966088 | tf_op jit(solution)/shard_map/ppermute | solution.py:352
  53.6 12.9 %copy-start.6 = (f32[256,640]{1,0:T(8,128)S(1)}, f32[256,640]{1,0:T(8,128)}, u32[]{:S(2)}) copy-start(f32[256,640]{1,0:T(8,128)} %copy-done.5) | copy-start | bytes 1966084
  53.6 26.8 %collective-permute-start.12 = (f32[256,640]{1,0:T(8,128)S(1)}, f32[256,640]{1,0:T(8,128)S(1)}, u32[]{:S(2)}, u32[]{:S(2)}) collective-permute-start(f32[256,640]{1,0:T(8,128)S(1)} %copy-done.16), channel_id=1, source_target_pairs={{0,2},{2,0},{4,6},{6,4},{8,10},{10,8},{12,14},{14,12},{1,3},{3,1},... | collective-permute-start | bytes 1966088 | tf_op jit(solution)/shard_map/ppermute | solution.py:340
  55.7 18.8 %collective-permute-start.8 = (f32[256,640]{1,0:T(8,128)S(1)}, f32[256,640]{1,0:T(8,128)S(1)}, u32[]{:S(2)}, u32[]{:S(2)}) collective-permute-start(f32[256,640]{1,0:T(8,128)S(1)} %add.43), channel_id=1, source_target_pairs={{0,4},{2,6},{12,8},{14,10},{1,5},{3,7},{13,9},{15,11},{16,20},{18,... | collective-permute-start | bytes 1966088 | tf_op jit(solution)/shard_map/ppermute | solution.py:346
  62.0 18.4 %collective-permute-start.15 = (f32[256,640]{1,0:T(8,128)S(1)}, f32[256,640]{1,0:T(8,128)S(1)}, u32[]{:S(2)}, u32[]{:S(2)}) collective-permute-start(f32[256,640]{1,0:T(8,128)S(1)} %add.50), channel_id=1, source_target_pairs={{4,8},{6,10},{8,4},{10,6},{5,9},{7,11},{9,5},{11,7},{20,24},{22,26... | collective-permute-start | bytes 1966088 | tf_op jit(solution)/shard_map/ppermute | solution.py:352
  68.0 20.6 %collective-permute-start.11 = (f32[256,640]{1,0:T(8,128)S(1)}, f32[256,640]{1,0:T(8,128)S(1)}, u32[]{:S(2)}, u32[]{:S(2)}) collective-permute-start(f32[256,640]{1,0:T(8,128)S(1)} %get-tuple-element.73), channel_id=1, source_target_pairs={{0,4},{2,6},{4,0},{6,2},{8,12},{10,14},{12,8},{14,10},{1,5},{3,7},... | collective-permute-start | bytes 1966088 | tf_op jit(solution)/shard_map/ppermute | solution.py:343
  70.2 38.0 %collective-permute-start.7 = (f32[512,640]{1,0:T(8,128)S(1)}, f32[512,640]{1,0:T(8,128)S(1)}, u32[]{:S(2)}, u32[]{:S(2)}) collective-permute-start(f32[512,640]{1,0:T(8,128)S(1)} %pad_maximum_fusion), channel_id=1, source_target_pairs={{0,2},{2,0},{4,6},{6,4},{8,10},{10,8},{12,14},{14,12},{1,3},{3,1},... | collective-permute-start | bytes 3932168 | tf_op jit(solution)/shard_map/ppermute | solution.py:340
  74.7 14.9 %collective-permute-start.9 = (f32[256,640]{1,0:T(8,128)S(1)}, f32[256,640]{1,0:T(8,128)S(1)}, u32[]{:S(2)}, u32[]{:S(2)}) collective-permute-start(f32[256,640]{1,0:T(8,128)S(1)} %add.44), channel_id=1, source_target_pairs={{4,8},{6,10},{8,4},{10,6},{5,9},{7,11},{9,5},{11,7},{20,24},{22,26... | collective-permute-start | bytes 1966088 | tf_op jit(solution)/shard_map/ppermute | solution.py:352
  80.5 22.1 %collective-permute-start.16 = (f32[256,640]{1,0:T(8,128)S(1)}, f32[256,640]{1,0:T(8,128)S(1)}, u32[]{:S(2)}, u32[]{:S(2)}) collective-permute-start(f32[256,640]{1,0:T(8,128)S(1)} %add_add_fusion), channel_id=1, source_target_pairs={{0,4},{2,6},{4,0},{6,2},{8,12},{10,14},{12,8},{14,10},{1,5},{3,7},... | collective-permute-start | bytes 1966088 | tf_op jit(solution)/shard_map/ppermute | solution.py:343
  88.6 19.6 %copy-start.3 = (f32[256,640]{1,0:T(8,128)S(1)}, f32[256,640]{1,0:T(8,128)}, u32[]{:S(2)}) copy-start(f32[256,640]{1,0:T(8,128)} %get-tuple-element.40.refs_0_) | copy-start | bytes 1966084
  88.6 19.6 %copy-start.4 = (f32[256,640]{1,0:T(8,128)S(1)}, f32[256,640]{1,0:T(8,128)}, u32[]{:S(2)}) copy-start(f32[256,640]{1,0:T(8,128)} %get-tuple-element.41.refs_1_) | copy-start | bytes 1966084
  88.7 19.5 %collective-permute-start.13 = (f32[256,640]{1,0:T(8,128)S(1)}, f32[256,640]{1,0:T(8,128)S(1)}, u32[]{:S(2)}, u32[]{:S(2)}) collective-permute-start(f32[256,640]{1,0:T(8,128)S(1)} %add.48), channel_id=1, source_target_pairs={{4,8},{6,10},{8,4},{10,6},{5,9},{7,11},{9,5},{11,7},{20,24},{22,26... | collective-permute-start | bytes 1966088 | tf_op jit(solution)/shard_map/ppermute | solution.py:352
  89.6 18.6 %collective-permute-start.14 = (f32[128,640]{1,0:T(8,128)S(1)}, f32[128,640]{1,0:T(8,128)S(1)}, u32[]{:S(2)}, u32[]{:S(2)}) collective-permute-start(f32[128,640]{1,0:T(8,128)S(1)} %slice.10), channel_id=1, source_target_pairs={{0,4},{2,6},{12,8},{14,10},{1,5},{3,7},{13,9},{15,11},{16,20},{18,... | collective-permute-start | bytes 983048 | tf_op jit(solution)/shard_map/ppermute | solution.py:346
  108.6 3.6 %collective-permute-start.17 = (f32[8,128]{1,0:T(8,128)S(1)}, f32[8,128]{1,0:T(8,128)S(1)}, u32[]{:S(2)}, u32[]{:S(2)}) collective-permute-start(f32[8,128]{1,0:T(8,128)S(1)} %get-tuple-element.69), channel_id=1, source_target_pairs={{0,2},{2,0},{4,6},{6,4},{8,10},{10,8},{12,14},{14,12},{1,3},{3,1},... | collective-permute-start | bytes 12296 | tf_op jit(solution)/shard_map/ppermute | solution.py:340
  112.2 5.4 %collective-permute-start.20 = (f32[8,128]{1,0:T(8,128)S(1)}, f32[8,128]{1,0:T(8,128)S(1)}, u32[]{:S(2)}, u32[]{:S(2)}) collective-permute-start(f32[8,128]{1,0:T(8,128)S(1)} %max.12), channel_id=1, source_target_pairs={{0,12},{2,14},{4,8},{6,10},{8,4},{10,6},{12,0},{14,2},{1,13},{3,15... | collective-permute-start | bytes 12296 | tf_op jit(solution)/shard_map/ppermute | solution.py:361
  115.5 4.5 %collective-permute-start.19 = (f32[8,128]{1,0:T(8,128)S(1)}, f32[8,128]{1,0:T(8,128)S(1)}, u32[]{:S(2)}, u32[]{:S(2)}) collective-permute-start(f32[8,128]{1,0:T(8,128)S(1)} %max.12), channel_id=1, source_target_pairs={{0,8},{2,10},{4,12},{6,14},{8,0},{10,2},{12,4},{14,6},{1,9},{3,11}... | collective-permute-start | bytes 12296 | tf_op jit(solution)/shard_map/ppermute | solution.py:361
  116.1 3.8 %collective-permute-start.18 = (f32[8,128]{1,0:T(8,128)S(1)}, f32[8,128]{1,0:T(8,128)S(1)}, u32[]{:S(2)}, u32[]{:S(2)}) collective-permute-start(f32[8,128]{1,0:T(8,128)S(1)} %max.12), channel_id=1, source_target_pairs={{0,4},{2,6},{4,0},{6,2},{8,12},{10,14},{12,8},{14,10},{1,5},{3,7},... | collective-permute-start | bytes 12296 | tf_op jit(solution)/shard_map/ppermute | solution.py:361
  (6 other events, 27.5 us)

commit v7 on v6

--- a/solution.py
+++ b/solution.py
@@ -166,11 +166,26 @@
     features, refs = refs[0], refs[1:]
     cot_half, refs = refs[0], refs[1:]
     outs, refs = refs[: len(jobs)], refs[len(jobs) :]
-    bufs, (rows, blocks, sems, block_sems) = refs[:6], refs[6:]
+    bufs, (rows, blocks, both, sems, block_sems) = refs[:6], refs[6:]
     sources = list(ins[:2]) + [lanes_of(ref, half) for ref in ins[2:]]
     copies = copy_all(sources, bufs, sems)
     kinds = [kind for job in jobs for kind, _ in job]
-    block_copies = start_features(features, kinds, blocks, block_sems)
+    width = blocks.shape[2]
+    joined = kinds[:2] == [(PAIR, CROSS), (PAIR, SAME)]
+    if joined:
+        rank = lax.axis_index("dp")
+        row = rank - (rank // 2) * 2
+        first = pl.multiple_of((block_of((PAIR, SAME)) - row) * width, HD)
+        copy = pltpu.make_async_copy(
+            features.at[:, pl.ds(first, 2 * width)], both, block_sems.at[0]
+        )
+        copy.start()
+        block_copies = [copy, None]
+        block_copies += start_features(
+            features, kinds[2:], blocks.at[pl.ds(2, len(kinds) - 2)], block_sems.at[pl.ds(2, len(kinds) - 2)]
+        )
+    else:
+        block_copies = start_features(features, kinds, blocks, block_sems)
     for copy in copies:
         copy.wait()
     lengths, rewards, q, ck, nk, cot = bufs
@@ -181,9 +196,15 @@
     for out, job in zip(outs, jobs):
         first = 0
         for _, size in job:
-            block_copies[place].wait()
+            if block_copies[place] is not None:
+                block_copies[place].wait()
+            if joined and place < 2:
+                place_row = 1 - row if place == 0 else row
+                block = both[:, pl.ds(pl.multiple_of(place_row * width, HD), width)]
+            else:
+                block = blocks[place]
             out[first : first + size] = jnp.dot(
-                cots[:size], blocks[place], preferred_element_type=jnp.float32
+                cots[:size], block, preferred_element_type=jnp.float32
             )
             first += size
             place += 1
@@ -208,6 +229,7 @@
         + [
             pltpu.VMEM((depth, columns), jnp.float32),
             pltpu.VMEM((count, depth, width), jnp.bfloat16),
+            pltpu.VMEM((depth, 2 * width), jnp.bfloat16),
             pltpu.SemaphoreType.DMA((6,)),
             pltpu.SemaphoreType.DMA((count,)),
         ],
@@ -304,7 +326,7 @@
         out_specs=[vmem] * 2,
         out_shape=[
             jax.ShapeDtypeStruct((2 * size, width), jnp.float32),
-            jax.ShapeDtypeStruct((8, HD), jnp.float32),
+            jax.ShapeDtypeStruct((1, HD), jnp.float32),
         ],
         compiler_params=PARAMS,
         cost_estimate=SMALL,
@@ -397,7 +419,8 @@
     e6 = pair(ownpb + y4 + m4)
     m6 = middle(own2b + y3 + e5)
     total, peaks = add_parts([ownoa, ownob, y5, m5, m6, e0, late, e5, e6])
-    peaks, grad = together(jnp.maximum(peaks, across(peaks)), place(total))
+    grad = place(total)
+    peaks = jnp.maximum(peaks, across(peaks))
     near, far, middle_peaks = [planes(peaks, hop) for hop in (2, 4, 6)]
     peaks = jnp.maximum(jnp.maximum(peaks, near), jnp.maximum(far, middle_peaks))
     return attended, grad, peaks[0, : columns // BUCKET]

time: 121 us -> 121 us (level)
    ppermute x3, waiting for transfers between devices: 3.37 us -> 1.85 us  [planes(): return lax.ppermute(x, 'dp', [(r, r ^ hop) for r in range(dp)])]
    ppermute x7, waiting for transfers between devices: 16.3 us -> 17.6 us  [across(): return lax.ppermute(x, 'dp', [(r, r ^ 1) for r in range(dp)])]
  transfers between devices with their start and end apart: 21 -> 21, of which waited for: 13 -> 12; matrix products, arithmetic and copies ran while one was open for 8% -> 8% of each run, Pallas kernels for 14% -> 14%
where the time goes in v7:
time: 121 us; the launch traced here: 120 us
  starting transfers between devices  45 us (37%)
  waiting for transfers between devices  41.3 us (34%)
  Pallas kernels  21.9 us (18%)
  other arithmetic  9.37 us (8%)
  local copies, waits for them, and re-layouts  1.63 us (1%)
    ppermute x4, starting transfers between devices, outward(): return lax.ppermute(x, 'dp', [(r, r ^ 2) for r in (0, 1, 6, 7)])  19.3 us
    ppermute x7, waiting for transfers between devices, across(): return lax.ppermute(x, 'dp', [(r, r ^ 1) for r in range(dp)])  17.6 us
    ppermute x7, starting transfers between devices, across(): return lax.ppermute(x, 'dp', [(r, r ^ 1) for r in range(dp)])  11.6 us
    ppermute x3, waiting for transfers between devices, pair(): return lax.ppermute(x, 'dp', [(r, r ^ 2) for r in range(dp)])  11.3 us
    ppermute x4, waiting for transfers between devices, outward(): return lax.ppermute(x, 'dp', [(r, r ^ 2) for r in (0, 1, 6, 7)])  10.6 us
    pallas_call x1, Pallas kernels, chunks(): pl.pallas_call(functools.partial(chunk_kernel, jobs), in_specs=[HBM, vmem...  8.85 us
    pallas_call x2, Pallas kernels, begin(): pl.pallas_call(functools.partial(begin_kernel, half, jobs), in_specs=[HBM...  8.41 us
    ppermute x3, starting transfers between devices, pair(): return lax.ppermute(x, 'dp', [(r, r ^ 2) for r in range(dp)])  5.93 us
  transfers between devices with their start and end apart: 21, of which 12 were waited for; matrix products, arithmetic and copies ran while one was open for 8% of the time, Pallas kernels for 14%

profile of v7, /device:TPU:0, one launch (start us, length us, event | category | flops | bytes accessed | tf_op | source)
XLA Modules:
  0.0 120.2 jit_solution(8048955705101325163)
XLA Ops:
  0.6 4.6 %value_cot.2 = (bf16[256,832]{1,0:T(8,128)(2,1)}, f32[384,640]{1,0:T(8,128)}, f32[256,640]{1,0:T(8,128)}) custom-call(s32[8]{0:T(128)} %refs_0_.5, f32[8]{0:T(128)} %refs_1_.5, bf16[8,8,4096]{2,1,0:T(8,128)(2,1)} %refs_2_.5, bf16[8,96,512]{2,1,0:T(8,128)(2,1)} %refs_3_.5, bf16[8,8,512]{2,1,0:T(8,128)(2,1)} %refs_4_.5, bf16[8,8,4096]{2,1,0:T(8,128)(2,1)} %refs_5_.5, ...), custom_call_target="tpu_custom_call" | custom-call | flops 1000 | bytes 1000 | tf_op jit(solution)/shard_map/value_cot/pallas_call | solution.py:222
  5.2 3.0 %collective-permute-start.2 = (f32[256,640]{1,0:T(8,128)}, f32[256,640]{1,0:T(8,128)}, u32[]{:S(2)}, u32[]{:S(2)}) collective-permute-start(f32[256,640]{1,0:T(8,128)} %get-tuple-element.45), channel_id=1, source_target_pairs={{0,2},{2,0},{4,6},{6,4},{8,10},{10,8},{12,14},{14,12},{1,3},{3,1},... | collective-permute-start | bytes 1966088 | tf_op jit(solution)/shard_map/ppermute | solution.py:362
  8.3 1.6 %collective-permute-start = (f32[384,640]{1,0:T(8,128)}, f32[384,640]{1,0:T(8,128)S(1)}, u32[]{:S(2)}, u32[]{:S(2)}) collective-permute-start(f32[384,640]{1,0:T(8,128)} %get-tuple-element.41), channel_id=1, source_target_pairs={{0,4},{2,6},{4,0},{6,2},{8,12},{10,14},{12,8},{14,10},{1,5},{3,7},... | collective-permute-start | bytes 2949128 | tf_op jit(solution)/shard_map/ppermute | solution.py:365
  9.8 3.8 %value_cot.3 = (bf16[256,832]{1,0:T(8,128)(2,1)}, f32[256,640]{1,0:T(8,128)}) custom-call(s32[8]{0:T(128)} %refs_0_.5, f32[8]{0:T(128)} %refs_1_.5, bf16[8,8,4096]{2,1,0:T(8,128)(2,1)} %refs_2_.5, bf16[8,96,512]{2,1,0:T(8,128)(2,1)} %refs_3_.5, bf16[8,8,512]{2,1,0:T(8,128)(2,1)} %refs_4_.5, bf16[8,8,4096]{2,1,0:T(8,128)(2,1)} %refs_5_.5, ...), custom_call_target="tpu_custom_call" | custom-call | flops 1000 | bytes 1000 | tf_op jit(solution)/shard_map/value_cot/pallas_call | solution.py:222
  15.2 8.8 %chunk.1 = (f32[256,640]{1,0:T(8,128)S(1)}, f32[256,640]{1,0:T(8,128)S(1)}, f32[256,640]{1,0:T(8,128)}, f32[256,640]{1,0:T(8,128)}, f32[256,640]{1,0:T(8,128)S(1...) custom-call(bf16[832,5120]{1,0:T(8,128)(2,1)} %bitcast.5, ...), custom_call_target="tpu_custom_call" | custom-call | flops 1000 | bytes 1000 | tf_op jit(solution)/shard_map/chunk/pallas_call | solution.py:287
  24.2 1.9 %add.42 = f32[256,640]{1,0:T(8,128)S(1)} add(f32[256,640]{1,0:T(8,128)S(1)} %get-tuple-element.51, f32[256,640]{1,0:T(8,128)} %collective-permute-done.2) | non-fusion elementwise | flops 163840 | bytes 1966080 | tf_op jit(solution)/shard_map/add | solution.py:407
  26.1 3.2 %collective-permute-start.6 = (f32[256,640]{1,0:T(8,128)S(1)}, f32[256,640]{1,0:T(8,128)S(1)}, u32[]{:S(2)}, u32[]{:S(2)}) collective-permute-start(f32[256,640]{1,0:T(8,128)S(1)} %add.42), channel_id=1, source_target_pairs={{0,4},{2,6},{12,8},{14,10},{1,5},{3,7},{13,9},{15,11},{16,20},{18,... | collective-permute-start | bytes 1966088 | tf_op jit(solution)/shard_map/ppermute | solution.py:368
  29.4 1.6 %collective-permute-start.5 = (f32[256,640]{1,0:T(8,128)}, f32[256,640]{1,0:T(8,128)}, u32[]{:S(2)}, u32[]{:S(2)}) collective-permute-start(f32[256,640]{1,0:T(8,128)} %get-tuple-element.50), channel_id=1, source_target_pairs={{0,2},{2,0},{4,6},{6,4},{8,10},{10,8},{12,14},{14,12},{1,3},{3,1},... | collective-permute-start | bytes 1966088 | tf_op jit(solution)/shard_map/ppermute | solution.py:362
  31.0 2.8 %attend.1 = bf16[8,8,4096]{2,1,0:T(8,128)(2,1)} custom-call(s32[8]{0:T(128)S(1)} %copy-done.14, bf16[8,8,4096]{2,1,0:T(8,128)(2,1)S(1)} %copy-done.1, bf16[8,96,512]{2,1,0:T(8,128)(2,1)S(1)} %copy-done, bf16[8,8,512]{2,1,0:T(8,128)(2,1)S(1)} %copy-done.10, bf16[8,96,512]{2,1,0:T(8,128)(2,1)S(1)} %copy-done.2, bf16[8,8,512]{2,1,0:T(8,128)(2,1)S(1)} %copy-done.13), custom_call_target="tpu_custom_call" | custom-call | flops 1000 | bytes 1000 | tf_op jit(solution)/shard_map/attend/pallas_call | solution.py:252
  33.9 4.2 %collective-permute-done.1 = f32[256,640]{1,0:T(8,128)S(1)} collective-permute-done((f32[256,640]{1,0:T(8,128)}, f32[256,640]{1,0:T(8,128)S(1)}, u32[]{:S(2)}, u32[]{:S(2)}) %collective-permute-start.1) | collective-permute-done | bytes 655392 | tf_op jit(solution)/shard_map/ppermute | solution.py:362
  39.0 4.9 %collective-permute-start.4 = (f32[256,640]{1,0:T(8,128)}, f32[256,640]{1,0:T(8,128)}, u32[]{:S(2)}, u32[]{:S(2)}) collective-permute-start(f32[256,640]{1,0:T(8,128)} %add.41), channel_id=1, source_target_pairs={{0,4},{2,6},{12,8},{14,10},{1,5},{3,7},{13,9},{15,11},{16,20},{18,... | collective-permute-start | bytes 1966088 | tf_op jit(solution)/shard_map/ppermute | solution.py:368
  43.9 1.5 %collective-permute-start.3 = (f32[256,640]{1,0:T(8,128)}, f32[256,640]{1,0:T(8,128)}, u32[]{:S(2)}, u32[]{:S(2)}) collective-permute-start(f32[256,640]{1,0:T(8,128)} %get-tuple-element.47), channel_id=1, source_target_pairs={{0,2},{2,0},{4,6},{6,4},{8,10},{10,8},{12,14},{14,12},{1,3},{3,1},... | collective-permute-start | bytes 1966088 | tf_op jit(solution)/shard_map/ppermute | solution.py:362
  47.2 1.5 %collective-permute-start.10 = (f32[256,640]{1,0:T(8,128)}, f32[256,640]{1,0:T(8,128)}, u32[]{:S(2)}, u32[]{:S(2)}) collective-permute-start(f32[256,640]{1,0:T(8,128)} %add.46), channel_id=1, source_target_pairs={{4,8},{6,10},{8,4},{10,6},{5,9},{7,11},{9,5},{11,7},{20,24},{22,26... | collective-permute-start | bytes 1966088 | tf_op jit(solution)/shard_map/ppermute | solution.py:374
  50.0 2.3 %collective-permute-done.5 = f32[256,640]{1,0:T(8,128)} collective-permute-done((f32[256,640]{1,0:T(8,128)}, f32[256,640]{1,0:T(8,128)}, u32[]{:S(2)}, u32[]{:S(2)}) %collective-permute-start.5) | collective-permute-done | bytes 655392 | tf_op jit(solution)/shard_map/ppermute | solution.py:362
  53.4 2.1 %collective-permute-start.12 = (f32[256,640]{1,0:T(8,128)S(1)}, f32[256,640]{1,0:T(8,128)S(1)}, u32[]{:S(2)}, u32[]{:S(2)}) collective-permute-start(f32[256,640]{1,0:T(8,128)S(1)} %copy-done.16), channel_id=1, source_target_pairs={{0,2},{2,0},{4,6},{6,4},{8,10},{10,8},{12,14},{14,12},{1,3},{3,1},... | collective-permute-start | bytes 1966088 | tf_op jit(solution)/shard_map/ppermute | solution.py:362
  55.5 3.5 %collective-permute-start.8 = (f32[256,640]{1,0:T(8,128)S(1)}, f32[256,640]{1,0:T(8,128)S(1)}, u32[]{:S(2)}, u32[]{:S(2)}) collective-permute-start(f32[256,640]{1,0:T(8,128)S(1)} %add.43), channel_id=1, source_target_pairs={{0,4},{2,6},{12,8},{14,10},{1,5},{3,7},{13,9},{15,11},{16,20},{18,... | collective-permute-start | bytes 1966088 | tf_op jit(solution)/shard_map/ppermute | solution.py:368
  59.0 1.4 %collective-permute-done.4 = f32[256,640]{1,0:T(8,128)} collective-permute-done((f32[256,640]{1,0:T(8,128)}, f32[256,640]{1,0:T(8,128)}, u32[]{:S(2)}, u32[]{:S(2)}) %collective-permute-start.4) | collective-permute-done | bytes 655392 | tf_op jit(solution)/shard_map/ppermute | solution.py:368
  62.5 3.8 %collective-permute-done.3 = f32[256,640]{1,0:T(8,128)} collective-permute-done((f32[256,640]{1,0:T(8,128)}, f32[256,640]{1,0:T(8,128)}, u32[]{:S(2)}, u32[]{:S(2)}) %collective-permute-start.3) | collective-permute-done | bytes 655392 | tf_op jit(solution)/shard_map/ppermute | solution.py:362
  66.3 1.5 %add_select_fusion = (f32[256,640]{1,0:T(8,128)S(1)}, f32[256,640]{1,0:T(8,128)S(1)}) fusion(f32[256,640]{1,0:T(8,128)S(1)} %get-tuple-element.60, f32[256,640]{1,0:T(8,128)} %collective-permute-done.10, pred[]{:T(512)S(6)} %or.3, f32[256,640]{1,0:T(8,128)S(1)} %copy-done.6, f32[256,640]{1,0:T(8,128)} %collective-permute-done.3), kind=kLoop, calls=%fused_computation.3 | loop fusion | flops 491520 | bytes 3932161 | tf_op jit(solution)/shard_map/jit(_where)/select_n | solution.py:415
  67.8 2.2 %collective-permute-start.11 = (f32[256,640]{1,0:T(8,128)S(1)}, f32[256,640]{1,0:T(8,128)S(1)}, u32[]{:S(2)}, u32[]{:S(2)}) collective-permute-start(f32[256,640]{1,0:T(8,128)S(1)} %get-tuple-element.69), channel_id=1, source_target_pairs={{0,4},{2,6},{4,0},{6,2},{8,12},{10,14},{12,8},{14,10},{1,5},{3,7},... | collective-permute-start | bytes 1966088 | tf_op jit(solution)/shard_map/ppermute | solution.py:365
  70.0 1.6 %collective-permute-start.7 = (f32[512,640]{1,0:T(8,128)S(1)}, f32[512,640]{1,0:T(8,128)S(1)}, u32[]{:S(2)}, u32[]{:S(2)}) collective-permute-start(f32[512,640]{1,0:T(8,128)S(1)} %pad_maximum_fusion), channel_id=1, source_target_pairs={{0,2},{2,0},{4,6},{6,4},{8,10},{10,8},{12,14},{14,12},{1,3},{3,1},... | collective-permute-start | bytes 3932168 | tf_op jit(solution)/shard_map/ppermute | solution.py:362
  71.6 2.7 %collective-permute-done.8 = f32[256,640]{1,0:T(8,128)S(1)} collective-permute-done((f32[256,640]{1,0:T(8,128)S(1)}, f32[256,640]{1,0:T(8,128)S(1)}, u32[]{:S(2)}, u32[]{:S(2)}) %collective-permute-start.8) | collective-permute-done | bytes 655392 | tf_op jit(solution)/shard_map/ppermute | solution.py:368
  75.2 5.0 %collective-permute-done.12 = f32[256,640]{1,0:T(8,128)S(1)} collective-permute-done((f32[256,640]{1,0:T(8,128)S(1)}, f32[256,640]{1,0:T(8,128)S(1)}, u32[]{:S(2)}, u32[]{:S(2)}) %collective-permute-start.12) | collective-permute-done | bytes 655392 | tf_op jit(solution)/shard_map/ppermute | solution.py:362
  80.3 2.2 %collective-permute-start.16 = (f32[256,640]{1,0:T(8,128)S(1)}, f32[256,640]{1,0:T(8,128)S(1)}, u32[]{:S(2)}, u32[]{:S(2)}) collective-permute-start(f32[256,640]{1,0:T(8,128)S(1)} %add_add_fusion), channel_id=1, source_target_pairs={{0,4},{2,6},{4,0},{6,2},{8,12},{10,14},{12,8},{14,10},{1,5},{3,7},... | collective-permute-start | bytes 1966088 | tf_op jit(solution)/shard_map/ppermute | solution.py:365
  82.5 5.9 %collective-permute-done.11.refs_7_ = f32[256,640]{1,0:T(8,128)S(1)} collective-permute-done((f32[256,640]{1,0:T(8,128)S(1)}, f32[256,640]{1,0:T(8,128)S(1)}, u32[]{:S(2)}, u32[]{:S(2)}) %collective-permute-start.11) | collective-permute-done | bytes 655392 | tf_op jit(solution)/shard_map/ppermute | solution.py:365
  89.4 7.7 %collective-permute-start.14 = (f32[128,640]{1,0:T(8,128)S(1)}, f32[128,640]{1,0:T(8,128)S(1)}, u32[]{:S(2)}, u32[]{:S(2)}) collective-permute-start(f32[128,640]{1,0:T(8,128)S(1)} %slice.10), channel_id=1, source_target_pairs={{0,4},{2,6},{12,8},{14,10},{1,5},{3,7},{13,9},{15,11},{16,20},{18,... | collective-permute-start | bytes 983048 | tf_op jit(solution)/shard_map/ppermute | solution.py:368
  97.1 5.4 %collective-permute-done.16.refs_8_ = f32[256,640]{1,0:T(8,128)S(1)} collective-permute-done((f32[256,640]{1,0:T(8,128)S(1)}, f32[256,640]{1,0:T(8,128)S(1)}, u32[]{:S(2)}, u32[]{:S(2)}) %collective-permute-start.16) | collective-permute-done | bytes 655392 | tf_op jit(solution)/shard_map/ppermute | solution.py:365
  102.5 5.6 %collective-permute-done.14.refs_6_ = f32[128,640]{1,0:T(8,128)S(1)} collective-permute-done((f32[128,640]{1,0:T(8,128)S(1)}, f32[128,640]{1,0:T(8,128)S(1)}, u32[]{:S(2)}, u32[]{:S(2)}) %collective-permute-start.14) | collective-permute-done | bytes 327712 | tf_op jit(solution)/shard_map/ppermute | solution.py:368
  109.6 2.4 %collective-permute-done.17 = f32[1,128]{1,0:T(1,128)S(1)} collective-permute-done((f32[1,128]{1,0:T(1,128)S(1)}, f32[1,128]{1,0:T(1,128)S(1)}, u32[]{:S(2)}, u32[]{:S(2)}) %collective-permute-start.17) | collective-permute-done | bytes 544 | tf_op jit(solution)/shard_map/ppermute | solution.py:362
  111.9 3.3 %collective-permute-start.20 = (f32[1,128]{1,0:T(1,128)S(1)}, f32[1,128]{1,0:T(1,128)S(1)}, u32[]{:S(2)}, u32[]{:S(2)}) collective-permute-start(f32[1,128]{1,0:T(1,128)S(1)} %max.12), channel_id=1, source_target_pairs={{0,12},{2,14},{4,8},{6,10},{8,4},{10,6},{12,0},{14,2},{1,13},{3,15... | collective-permute-start | bytes 1544 | tf_op jit(solution)/shard_map/ppermute | solution.py:383
  116.3 1.5 %place.1 = f32[640,512]{1,0:T(8,128)} custom-call(f32[512,640]{1,0:T(8,128)S(1)} %get-tuple-element.67.total), custom_call_target="tpu_custom_call" | custom-call | flops 1000 | bytes 1000 | tf_op jit(solution)/shard_map/place/pallas_call | solution.py:344
  117.8 1.8 %collective-permute-done.19 = f32[1,128]{1,0:T(1,128)S(1)} collective-permute-done((f32[1,128]{1,0:T(1,128)S(1)}, f32[1,128]{1,0:T(1,128)S(1)}, u32[]{:S(2)}, u32[]{:S(2)}) %collective-permute-start.19) | collective-permute-done | bytes 544 | tf_op jit(solution)/shard_map/ppermute | solution.py:383
  (65 shorter events, 13.9 us)
Async XLA Ops:
  5.2 19.0 %collective-permute-start.2 = (f32[256,640]{1,0:T(8,128)}, f32[256,640]{1,0:T(8,128)}, u32[]{:S(2)}, u32[]{:S(2)}) collective-permute-start(f32[256,640]{1,0:T(8,128)} %get-tuple-element.45), channel_id=1, source_target_pairs={{0,2},{2,0},{4,6},{6,4},{8,10},{10,8},{12,14},{14,12},{1,3},{3,1},... | collective-permute-start | bytes 1966088 | tf_op jit(solution)/shard_map/ppermute | solution.py:362
  8.3 29.8 %collective-permute-start = (f32[384,640]{1,0:T(8,128)}, f32[384,640]{1,0:T(8,128)S(1)}, u32[]{:S(2)}, u32[]{:S(2)}) collective-permute-start(f32[384,640]{1,0:T(8,128)} %get-tuple-element.41), channel_id=1, source_target_pairs={{0,4},{2,6},{4,0},{6,2},{8,12},{10,14},{12,8},{14,10},{1,5},{3,7},... | collective-permute-start | bytes 2949128 | tf_op jit(solution)/shard_map/ppermute | solution.py:365
  13.7 24.4 %collective-permute-start.1 = (f32[256,640]{1,0:T(8,128)}, f32[256,640]{1,0:T(8,128)S(1)}, u32[]{:S(2)}, u32[]{:S(2)}) collective-permute-start(f32[256,640]{1,0:T(8,128)} %get-tuple-element.44), channel_id=1, source_target_pairs={{0,2},{2,0},{4,6},{6,4},{8,10},{10,8},{12,14},{14,12},{1,3},{3,1},... | collective-permute-start | bytes 1966088 | tf_op jit(solution)/shard_map/ppermute | solution.py:362
  15.2 15.7 %copy-start.2 = (bf16[8,96,512]{2,1,0:T(8,128)(2,1)S(1)}, bf16[8,96,512]{2,1,0:T(8,128)(2,1)}, u32[]{:S(2)}) copy-start(bf16[8,96,512]{2,1,0:T(8,128)(2,1)} %refs_4_.3) | copy-start | bytes 2359300
  24.1 9.7 %copy-start.5 = (f32[256,640]{1,0:T(8,128)}, f32[256,640]{1,0:T(8,128)S(1)}, u32[]{:S(2)}) copy-start(f32[256,640]{1,0:T(8,128)S(1)} %get-tuple-element.59) | copy-start | bytes 1966084
  24.1 9.7 %copy-start.7 = (f32[256,640]{1,0:T(8,128)}, f32[256,640]{1,0:T(8,128)S(1)}, u32[]{:S(2)}) copy-start(f32[256,640]{1,0:T(8,128)S(1)} %get-tuple-element.57) | copy-start | bytes 1966084
  24.1 9.7 %copy-start.9 = (f32[256,640]{1,0:T(8,128)}, f32[256,640]{1,0:T(8,128)S(1)}, u32[]{:S(2)}) copy-start(f32[256,640]{1,0:T(8,128)S(1)} %get-tuple-element.40) | copy-start | bytes 1966084
  24.1 9.7 %copy-start.15 = (f32[256,640]{1,0:T(8,128)}, f32[256,640]{1,0:T(8,128)S(1)}, u32[]{:S(2)}) copy-start(f32[256,640]{1,0:T(8,128)S(1)} %get-tuple-element.62) | copy-start | bytes 1966084
  24.1 6.8 %copy-start = (bf16[8,96,512]{2,1,0:T(8,128)(2,1)S(1)}, bf16[8,96,512]{2,1,0:T(8,128)(2,1)}, u32[]{:S(2)}) copy-start(bf16[8,96,512]{2,1,0:T(8,128)(2,1)} %refs_3_.5) | copy-start | bytes 2359300
  24.2 6.8 %copy-start.1 = (bf16[8,8,4096]{2,1,0:T(8,128)(2,1)S(1)}, bf16[8,8,4096]{2,1,0:T(8,128)(2,1)}, u32[]{:S(2)}) copy-start(bf16[8,8,4096]{2,1,0:T(8,128)(2,1)} %refs_2_.5) | copy-start | bytes 1572868
  24.2 6.8 %copy-start.10 = (bf16[8,8,512]{2,1,0:T(8,128)(2,1)S(1)}, bf16[8,8,512]{2,1,0:T(8,128)(2,1)}, u32[]{:S(2)}) copy-start(bf16[8,8,512]{2,1,0:T(8,128)(2,1)} %refs_4_.5) | copy-start | bytes 196612
  26.1 20.1 %collective-permute-start.6 = (f32[256,640]{1,0:T(8,128)S(1)}, f32[256,640]{1,0:T(8,128)S(1)}, u32[]{:S(2)}, u32[]{:S(2)}) collective-permute-start(f32[256,640]{1,0:T(8,128)S(1)} %add.42), channel_id=1, source_target_pairs={{0,4},{2,6},{12,8},{14,10},{1,5},{3,7},{13,9},{15,11},{16,20},{18,... | collective-permute-start | bytes 1966088 | tf_op jit(solution)/shard_map/ppermute | solution.py:368
  29.4 22.9 %collective-permute-start.5 = (f32[256,640]{1,0:T(8,128)}, f32[256,640]{1,0:T(8,128)}, u32[]{:S(2)}, u32[]{:S(2)}) collective-permute-start(f32[256,640]{1,0:T(8,128)} %get-tuple-element.50), channel_id=1, source_target_pairs={{0,2},{2,0},{4,6},{6,4},{8,10},{10,8},{12,14},{14,12},{1,3},{3,1},... | collective-permute-start | bytes 1966088 | tf_op jit(solution)/shard_map/ppermute | solution.py:362
  39.0 21.4 %collective-permute-start.4 = (f32[256,640]{1,0:T(8,128)}, f32[256,640]{1,0:T(8,128)}, u32[]{:S(2)}, u32[]{:S(2)}) collective-permute-start(f32[256,640]{1,0:T(8,128)} %add.41), channel_id=1, source_target_pairs={{0,4},{2,6},{12,8},{14,10},{1,5},{3,7},{13,9},{15,11},{16,20},{18,... | collective-permute-start | bytes 1966088 | tf_op jit(solution)/shard_map/ppermute | solution.py:368
  43.9 22.4 %collective-permute-start.3 = (f32[256,640]{1,0:T(8,128)}, f32[256,640]{1,0:T(8,128)}, u32[]{:S(2)}, u32[]{:S(2)}) collective-permute-start(f32[256,640]{1,0:T(8,128)} %get-tuple-element.47), channel_id=1, source_target_pairs={{0,2},{2,0},{4,6},{6,4},{8,10},{10,8},{12,14},{14,12},{1,3},{3,1},... | collective-permute-start | bytes 1966088 | tf_op jit(solution)/shard_map/ppermute | solution.py:362
  47.2 19.1 %collective-permute-start.10 = (f32[256,640]{1,0:T(8,128)}, f32[256,640]{1,0:T(8,128)}, u32[]{:S(2)}, u32[]{:S(2)}) collective-permute-start(f32[256,640]{1,0:T(8,128)} %add.46), channel_id=1, source_target_pairs={{4,8},{6,10},{8,4},{10,6},{5,9},{7,11},{9,5},{11,7},{20,24},{22,26... | collective-permute-start | bytes 1966088 | tf_op jit(solution)/shard_map/ppermute | solution.py:374
  53.4 12.9 %copy-start.6 = (f32[256,640]{1,0:T(8,128)S(1)}, f32[256,640]{1,0:T(8,128)}, u32[]{:S(2)}) copy-start(f32[256,640]{1,0:T(8,128)} %copy-done.5) | copy-start | bytes 1966084
  53.4 26.8 %collective-permute-start.12 = (f32[256,640]{1,0:T(8,128)S(1)}, f32[256,640]{1,0:T(8,128)S(1)}, u32[]{:S(2)}, u32[]{:S(2)}) collective-permute-start(f32[256,640]{1,0:T(8,128)S(1)} %copy-done.16), channel_id=1, source_target_pairs={{0,2},{2,0},{4,6},{6,4},{8,10},{10,8},{12,14},{14,12},{1,3},{3,1},... | collective-permute-start | bytes 1966088 | tf_op jit(solution)/shard_map/ppermute | solution.py:362
  55.5 18.9 %collective-permute-start.8 = (f32[256,640]{1,0:T(8,128)S(1)}, f32[256,640]{1,0:T(8,128)S(1)}, u32[]{:S(2)}, u32[]{:S(2)}) collective-permute-start(f32[256,640]{1,0:T(8,128)S(1)} %add.43), channel_id=1, source_target_pairs={{0,4},{2,6},{12,8},{14,10},{1,5},{3,7},{13,9},{15,11},{16,20},{18,... | collective-permute-start | bytes 1966088 | tf_op jit(solution)/shard_map/ppermute | solution.py:368
  61.8 18.4 %collective-permute-start.15 = (f32[256,640]{1,0:T(8,128)S(1)}, f32[256,640]{1,0:T(8,128)S(1)}, u32[]{:S(2)}, u32[]{:S(2)}) collective-permute-start(f32[256,640]{1,0:T(8,128)S(1)} %add.50), channel_id=1, source_target_pairs={{4,8},{6,10},{8,4},{10,6},{5,9},{7,11},{9,5},{11,7},{20,24},{22,26... | collective-permute-start | bytes 1966088 | tf_op jit(solution)/shard_map/ppermute | solution.py:374
  67.8 20.6 %collective-permute-start.11 = (f32[256,640]{1,0:T(8,128)S(1)}, f32[256,640]{1,0:T(8,128)S(1)}, u32[]{:S(2)}, u32[]{:S(2)}) collective-permute-start(f32[256,640]{1,0:T(8,128)S(1)} %get-tuple-element.69), channel_id=1, source_target_pairs={{0,4},{2,6},{4,0},{6,2},{8,12},{10,14},{12,8},{14,10},{1,5},{3,7},... | collective-permute-start | bytes 1966088 | tf_op jit(solution)/shard_map/ppermute | solution.py:365
  70.0 38.0 %collective-permute-start.7 = (f32[512,640]{1,0:T(8,128)S(1)}, f32[512,640]{1,0:T(8,128)S(1)}, u32[]{:S(2)}, u32[]{:S(2)}) collective-permute-start(f32[512,640]{1,0:T(8,128)S(1)} %pad_maximum_fusion), channel_id=1, source_target_pairs={{0,2},{2,0},{4,6},{6,4},{8,10},{10,8},{12,14},{14,12},{1,3},{3,1},... | collective-permute-start | bytes 3932168 | tf_op jit(solution)/shard_map/ppermute | solution.py:362
  74.5 14.9 %collective-permute-start.9 = (f32[256,640]{1,0:T(8,128)S(1)}, f32[256,640]{1,0:T(8,128)S(1)}, u32[]{:S(2)}, u32[]{:S(2)}) collective-permute-start(f32[256,640]{1,0:T(8,128)S(1)} %add.44), channel_id=1, source_target_pairs={{4,8},{6,10},{8,4},{10,6},{5,9},{7,11},{9,5},{11,7},{20,24},{22,26... | collective-permute-start | bytes 1966088 | tf_op jit(solution)/shard_map/ppermute | solution.py:374
  80.3 22.2 %collective-permute-start.16 = (f32[256,640]{1,0:T(8,128)S(1)}, f32[256,640]{1,0:T(8,128)S(1)}, u32[]{:S(2)}, u32[]{:S(2)}) collective-permute-start(f32[256,640]{1,0:T(8,128)S(1)} %add_add_fusion), channel_id=1, source_target_pairs={{0,4},{2,6},{4,0},{6,2},{8,12},{10,14},{12,8},{14,10},{1,5},{3,7},... | collective-permute-start | bytes 1966088 | tf_op jit(solution)/shard_map/ppermute | solution.py:365
  88.4 19.6 %copy-start.3 = (f32[256,640]{1,0:T(8,128)S(1)}, f32[256,640]{1,0:T(8,128)}, u32[]{:S(2)}) copy-start(f32[256,640]{1,0:T(8,128)} %get-tuple-element.38.refs_0_) | copy-start | bytes 1966084
  88.4 19.6 %copy-start.4 = (f32[256,640]{1,0:T(8,128)S(1)}, f32[256,640]{1,0:T(8,128)}, u32[]{:S(2)}) copy-start(f32[256,640]{1,0:T(8,128)} %get-tuple-element.39.refs_1_) | copy-start | bytes 1966084
  88.5 19.5 %collective-permute-start.13 = (f32[256,640]{1,0:T(8,128)S(1)}, f32[256,640]{1,0:T(8,128)S(1)}, u32[]{:S(2)}, u32[]{:S(2)}) collective-permute-start(f32[256,640]{1,0:T(8,128)S(1)} %add.48), channel_id=1, source_target_pairs={{4,8},{6,10},{8,4},{10,6},{5,9},{7,11},{9,5},{11,7},{20,24},{22,26... | collective-permute-start | bytes 1966088 | tf_op jit(solution)/shard_map/ppermute | solution.py:374
  89.4 18.6 %collective-permute-start.14 = (f32[128,640]{1,0:T(8,128)S(1)}, f32[128,640]{1,0:T(8,128)S(1)}, u32[]{:S(2)}, u32[]{:S(2)}) collective-permute-start(f32[128,640]{1,0:T(8,128)S(1)} %slice.10), channel_id=1, source_target_pairs={{0,4},{2,6},{12,8},{14,10},{1,5},{3,7},{13,9},{15,11},{16,20},{18,... | collective-permute-start | bytes 983048 | tf_op jit(solution)/shard_map/ppermute | solution.py:368
  108.4 3.5 %collective-permute-start.17 = (f32[1,128]{1,0:T(1,128)S(1)}, f32[1,128]{1,0:T(1,128)S(1)}, u32[]{:S(2)}, u32[]{:S(2)}) collective-permute-start(f32[1,128]{1,0:T(1,128)S(1)} %get-tuple-element.68), channel_id=1, source_target_pairs={{0,2},{2,0},{4,6},{6,4},{8,10},{10,8},{12,14},{14,12},{1,3},{3,1},... | collective-permute-start | bytes 1544 | tf_op jit(solution)/shard_map/ppermute | solution.py:362
  111.9 5.9 %collective-permute-start.20 = (f32[1,128]{1,0:T(1,128)S(1)}, f32[1,128]{1,0:T(1,128)S(1)}, u32[]{:S(2)}, u32[]{:S(2)}) collective-permute-start(f32[1,128]{1,0:T(1,128)S(1)} %max.12), channel_id=1, source_target_pairs={{0,12},{2,14},{4,8},{6,10},{8,4},{10,6},{12,0},{14,2},{1,13},{3,15... | collective-permute-start | bytes 1544 | tf_op jit(solution)/shard_map/ppermute | solution.py:383
  115.2 4.4 %collective-permute-start.19 = (f32[1,128]{1,0:T(1,128)S(1)}, f32[1,128]{1,0:T(1,128)S(1)}, u32[]{:S(2)}, u32[]{:S(2)}) collective-permute-start(f32[1,128]{1,0:T(1,128)S(1)} %max.12), channel_id=1, source_target_pairs={{0,8},{2,10},{4,12},{6,14},{8,0},{10,2},{12,4},{14,6},{1,9},{3,11}... | collective-permute-start | bytes 1544 | tf_op jit(solution)/shard_map/ppermute | solution.py:383
  115.9 3.8 %collective-permute-start.18 = (f32[1,128]{1,0:T(1,128)S(1)}, f32[1,128]{1,0:T(1,128)S(1)}, u32[]{:S(2)}, u32[]{:S(2)}) collective-permute-start(f32[1,128]{1,0:T(1,128)S(1)} %max.12), channel_id=1, source_target_pairs={{0,4},{2,6},{4,0},{6,2},{8,12},{10,14},{12,8},{14,10},{1,5},{3,7},... | collective-permute-start | bytes 1544 | tf_op jit(solution)/shard_map/ppermute | solution.py:383
  (6 other events, 27.5 us)
